TPU v7x, 256 devices: a whole 4x4x8 slice. The times are simulated.
256 devices in a mesh: ep: 64 (over z, y, core), tp: 4 (over x).
Axes of the slice: x: 4, y: 4, z: 8, core: 2. Of those that a mesh axis runs over, the one named last changes fastest.
Arguments:
- hidden_rows: bfloat16 [4096, 7168], P('ep', 'tp'), may hold values from -6 to 6
- expert_ids: int32 [4096, 8], P('ep'), may hold values from 0 to 63, all different within a row; in each aligned block of 64 rows (0 to 63, 64 to 127, ...) at most 12 rows name the same one
- affinity: float32 [4096, 8], P('ep'), may hold values from 0.05 to 1
- w_gate: bfloat16 [64, 7168, 1024], P('ep', None, 'tp'), may hold values from -0.0625 to 0.0625
- w_up: bfloat16 [64, 7168, 1024], P('ep', None, 'tp'), may hold values from -0.0625 to 0.0625
- w_down: bfloat16 [64, 1024, 7168], P('ep', 'tp'), may hold values from -0.1875 to 0.1875
Outputs:
- mixed_rows: bfloat16 [4096, 7168], P('ep', 'tp')
Inputs may be any that keep to these rules, and one draw needn't show every extreme that they name: `expert_ids`: each row names 8 different experts. In the rows of one device no expert is named more than 12 times, and in every draw some expert is named exactly 12 times there.
All inputs are finite; a program needn't handle non-finite values.
Results may differ from a plain program's by a relative error of at most 0.015.
Values may be sent and summed in bfloat16 or wider, within the bound.
No kernel may reach another device: no remote copies, remote signals or barrier semaphores. Data moves between devices by JAX's collectives and lax.ppermute only.
A program may use at most 128 MiB of HBM per device.

v0:
```python
import jax
import jax.numpy as jnp
from jax import lax
from jax.sharding import PartitionSpec as P

CAP = 12


route_scale = 2.5


def place_rows(source_rows, position, choose, experts, ep_count):
    repeated = jnp.repeat(source_rows, choose, axis=0)
    buffer = jnp.zeros((experts * CAP, source_rows.shape[1]), jnp.bfloat16)
    buffer = buffer.at[position].set(repeated)
    return buffer.reshape(ep_count, experts * CAP // ep_count, source_rows.shape[1])


def on_device(hidden_rows, expert_ids, affinity, w_gate, w_up, w_down):
    ep_count = lax.axis_size("ep")
    local_experts = w_gate.shape[0]
    experts = local_experts * ep_count
    row_count = expert_ids.shape[0]
    choose = expert_ids.shape[1]
    feature_part = hidden_rows.shape[1]
    flat_ids = expert_ids.reshape(-1)
    onehot = (flat_ids[:, None] == jnp.arange(experts, dtype=jnp.int32)[None, :]).astype(jnp.int32)
    earlier = jnp.cumsum(onehot, axis=0) - onehot
    slot_index = jnp.sum(earlier * onehot, axis=1)
    position = flat_ids * CAP + slot_index
    route_weight = route_scale * affinity / jnp.sum(affinity, axis=1, keepdims=True)
    full_rows = lax.all_gather(hidden_rows, "tp", axis=1, tiled=True)
    outgoing = place_rows(full_rows, position, choose, experts, ep_count)
    arrived = lax.all_to_all(outgoing, "ep", split_axis=0, concat_axis=0, tiled=True)
    feat_width = arrived.shape[2]
    inputs = arrived.reshape(ep_count, local_experts, CAP, feat_width)
    gate_proj = jnp.einsum("secd,edh->sech", inputs, w_gate, preferred_element_type=jnp.float32)
    up_proj = jnp.einsum("secd,edh->sech", inputs, w_up, preferred_element_type=jnp.float32)
    activated = (jax.nn.silu(gate_proj) * up_proj).astype(jnp.bfloat16)
    partial_out = jnp.einsum(
        "sech,ehd->secd", activated, w_down, preferred_element_type=jnp.float32
    )
    partial_down = partial_out.reshape(ep_count, local_experts * CAP, feat_width).astype(
        jnp.bfloat16
    )
    summed = lax.psum_scatter(partial_down, "tp", scatter_dimension=2, tiled=True).astype(
        jnp.float32
    )
    returned = lax.all_to_all(
        summed.astype(jnp.bfloat16), "ep", split_axis=0, concat_axis=0, tiled=True
    )
    picked = returned.reshape(experts * CAP, feature_part)[position].reshape(
        row_count, choose, feature_part
    )
    mixed_rows = jnp.sum(picked.astype(jnp.float32) * route_weight[:, :, None], axis=1)
    return mixed_rows.astype(jnp.bfloat16)


def solution(mesh):
    in_specs = (
        P("ep", "tp"),
        P("ep", None),
        P("ep", None),
        P("ep", None, "tp"),
        P("ep", None, "tp"),
        P("ep", "tp", None),
    )
    out_specs = P("ep", "tp")
    return jax.shard_map(
        on_device, mesh=mesh, in_specs=in_specs, out_specs=out_specs, check_vma=False
    )
```

profile of v0, /device:TPU:1, one launch (start us, length us, event | category | flops | bytes accessed | tf_op | source)
XLA Modules:
  0.0 641.2 jit_solution(15004281457791610725)
XLA Ops:
  6.5 0.8 copy.16
  7.3 0.1 eq.29
  7.4 0.1 eq.25
  7.5 0.7 broadcast_multiply_fusion
  8.2 1.2 reduce-window.6
  9.4 0.2 slice_reduce_fusion
  9.7 0.1 copy.15
  9.8 0.1 mul.42
  9.9 13.7 %all_gather.3 = bf16[64,7168]{1,0:T(8,128)(2,1)S(1)} all-gather(bf16[64,1792]{1,0:T(8,128)(2,1)} %param.6), channel_id=1, replica_groups=mesh['ep'=64,'tp'=4] {'tp'}, dimensions={1}, use_global_device_ids=true | all-gather | bytes 1146880 | tf_op jit(solution)/shard_map/all_gather | solution.py:32
  23.5 0.1 fusion.39
  23.7 16.5 %scatter_custom_fusion = bf16[768,7168]{1,0:T(8,128)(2,1)} fusion(s32[512]{0:T(512)S(1)} %bitcast.71, bf16[]{:T(256)} %constant.7.clone.1, bf16[64,7168]{1,0:T(8,128)(2,1)S(1)} %all_gather.3), kind=kCustom, calls=%fused_computation.7 | custom fusion | bytes 11927554 | tf_op jit(solution)/shard_map/scatter | solution.py:15
  40.2 15.3 %reshape.83 = bf16[64,12,7168]{2,1,0:T(8,128)(2,1)} reshape(bf16[768,7168]{1,0:T(8,128)(2,1)} %scatter_custom_fusion) | data formatting | bytes 22020096 | tf_op jit(solution)/shard_map/reshape | solution.py:16
  55.5 333.3 %all_to_all.10 = bf16[64,12,7168]{2,1,0:T(8,128)(2,1)S(1)} all-to-all(bf16[64,12,7168]{2,1,0:T(8,128)(2,1)} %reshape.83), channel_id=1, replica_groups=mesh['ep'=64,'tp'=4] {'ep'}, dimensions={0} | all-to-all | bytes 22020096 | tf_op jit(solution)/shard_map/all_to_all | solution.py:34
  388.9 11.9 %fusion.12 = f32[64,1,12,256]{3,0,2,1:T(8,128)S(1)} fusion(bf16[1,7168,256]{2,1,0:T(8,128)(2,1)S(1)} %copy-done.2, bf16[64,12,7168]{2,1,0:T(8,128)(2,1)S(1)} %all_to_all.10), kind=kOutput, calls=%fused_computation.16 | convolution fusion | flops 2818572288 | bytes 15466496 | tf_op jit(solution)/shard_map/secd,edh->sech/dot_general | solution.py:37
  400.8 14.3 %fusion.32 = bf16[64,12,256]{2,0,1:T(8,128)(2,1)S(1)} fusion(bf16[1,7168,256]{2,1,0:T(8,128)(2,1)} %param.10, bf16[64,12,7168]{2,1,0:T(8,128)(2,1)S(1)} %all_to_all.10, f32[64,1,12,256]{3,0,2,1:T(8,128)S(1)} %fusion.12), kind=kOutput, calls=%fused_computation.20 | convolution fusion | flops 2819751936 | bytes 15859712 | tf_op jit(solution)/shard_map/secd,edh->sech/dot_general | solution.py:38
  415.0 5.7 convolution_convert_fusion
  420.8 102.5 %reduce-scatter.2.cloned.1.call-done = bf16[64,12,1792]{2,0,1:T(8,128)(2,1)} async-done(((bf16[64,12,7168]{2,0,1:T(8,128)(2,1)}), bf16[64,12,1792]{2,0,1:T(8,128)(2,1)}) %reduce-scatter.2.cloned.1.call-update) | async-done | bytes 2752528 | tf_op jit(solution)/shard_map/reduce_scatter | solution.py:46
  523.3 5.1 copy.21
  528.4 10.9 %all-to-all-start.1 = ((bf16[64,12,1792]{2,1,0:T(8,128)(2,1)}), bf16[64,12,1792]{2,1,0:T(8,128)(2,1)}, u32[]{:S(2)}, u32[]{:S(2)}) async-start(bf16[64,12,1792]{2,1,0:T(8,128)(2,1)} %copy.21), calls=%async_computation.2 | async-start | bytes 7340032 | tf_op jit(solution)/shard_map/all_to_all | solution.py:49
  539.4 0.1 copy.22
  539.5 83.6 %all-to-all-done.1 = bf16[64,12,1792]{2,1,0:T(8,128)(2,1)} async-done(((bf16[64,12,1792]{2,1,0:T(8,128)(2,1)}), bf16[64,12,1792]{2,1,0:T(8,128)(2,1)}, u32[]{:S(2)}, u32[]{:S(2)}) %all-to-all-start.1) | async-done | bytes 2752544 | tf_op jit(solution)/shard_map/all_to_all | solution.py:49
  623.1 3.8 reshape.88
  626.9 3.2 gather_fusion
  630.1 3.8 fusion.7
  (15 shorter events, 0.1 us)
Async XLA Ops:
  6.5 516.8 %reduce-scatter.2.cloned.1.call-start = ((), (), s32[]{:S(2)}) async-start(), calls=%async_computation.3 | async-start | bytes 13762560 | tf_op jit(solution)/shard_map/reduce_scatter | solution.py:46
  55.5 333.3 %copy-start.2 = (bf16[1,7168,256]{2,1,0:T(8,128)(2,1)S(1)}, bf16[1,7168,256]{2,1,0:T(8,128)(2,1)}, u32[]{:S(2)}) copy-start(bf16[1,7168,256]{2,1,0:T(8,128)(2,1)} %param.9) | copy-start | bytes 11010052
  400.8 14.3 %copy-start = (bf16[1,256,7168]{2,1,0:T(8,128)(2,1)S(1)}, bf16[1,256,7168]{2,1,0:T(8,128)(2,1)}, u32[]{:S(2)}) copy-start(bf16[1,256,7168]{2,1,0:T(8,128)(2,1)} %param.11) | copy-start | bytes 11010052
  528.4 10.9 %copy-start.1 = (f32[64,8]{0,1:T(8,128)S(1)}, f32[64,8]{0,1:T(8,128)}, u32[]{:S(2)}) copy-start(f32[64,8]{0,1:T(8,128)} %param.8) | copy-start | bytes 6148
  528.4 94.7 %all-to-all-start.1 = ((bf16[64,12,1792]{2,1,0:T(8,128)(2,1)}), bf16[64,12,1792]{2,1,0:T(8,128)(2,1)}, u32[]{:S(2)}, u32[]{:S(2)}) async-start(bf16[64,12,1792]{2,1,0:T(8,128)(2,1)} %copy.21), calls=%async_computation.2 | async-start | bytes 7340032 | tf_op jit(solution)/shard_map/all_to_all | solution.py:49
Sparse Core Ops, SparseCore 0:
  420.9 102.3 reduce-scatter.1
where the time goes:
time: 645 us; the launch traced here: 641 us
  blocking collectives  347 us (54%)
  waiting for transfers between devices  186 us (29%)
  local copies, waits for them, and re-layouts  45.4 us (7%)
  matrix products  31.9 us (5%)
  between operations  13.9 us (2%)
  starting transfers between devices  10.9 us (2%)
    all_to_all x1, blocking collectives, on_device(): lax.all_to_all(outgoing, 'ep', split_axis=0, concat_axis=0, tiled=True)  333 us
    reduce_scatter x1, waiting for transfers between devices, on_device(): lax.psum_scatter(partial_down, 'tp', scatter_dimension=2, tiled=True)  103 us
    all_to_all x1, waiting for transfers between devices, on_device(): lax.all_to_all(summed.astype(jnp.bfloat16), 'ep', split_axis=0, concat_ax...  83.6 us
    scatter x1, local copies, waits for them, and re-layouts, place_rows(): buffer = buffer.at[position].set(repeated)  16.5 us
    reshape x1, local copies, waits for them, and re-layouts, place_rows(): buffer.reshape(ep_count, experts * CAP // ep_count, source_rows.shape[1])  15.3 us
    dot_general x1, matrix products, on_device(): jnp.einsum('secd,edh->sech', inputs, w_up, preferred_element_type=jnp.flo...  14.3 us
    all_gather x1, blocking collectives, on_device(): full_rows = lax.all_gather(hidden_rows, 'tp', axis=1, tiled=True)  13.7 us
  transfers between devices with their start and end apart: 2, of which 2 were waited for; matrix products, arithmetic and copies ran while one was open for 0% of the time, Pallas kernels for 0%

commit v1 on v0

v1 whole, which is shorter than its diff:
```python
import functools

import jax
import jax.numpy as jnp
from jax import lax
from jax.experimental import pallas as pl
from jax.experimental.pallas import tpu as pltpu
from jax.sharding import PartitionSpec as P

CAP = 12
CHUNKS = ((0, 8), (8, 4))
VMEM_LIMIT = 48 * 1024 * 1024


route_scale = 2.5


def hidden_kernel(x_ref, gate_ref, up_ref, out_ref, gate_sum, up_sum):
    step = pl.program_id(0)
    x = x_ref[0]
    gate_part = jnp.dot(x, gate_ref[0], preferred_element_type=jnp.float32)
    up_part = jnp.dot(x, up_ref[0], preferred_element_type=jnp.float32)

    @pl.when(step == 0)
    def _():
        gate_sum[...] = gate_part
        up_sum[...] = up_part

    @pl.when(step > 0)
    def _():
        gate_sum[...] += gate_part
        up_sum[...] += up_part

    @pl.when(step == pl.num_programs(0) - 1)
    def _():
        gate = gate_sum[...]
        out_ref[...] = (gate / (1.0 + jnp.exp(-gate)) * up_sum[...]).astype(out_ref.dtype)


def hidden_units(x, w_gate, w_up):
    parts, rows, width = x.shape
    hidden = w_gate.shape[1]
    w_gate = w_gate.reshape(parts, width, hidden)
    w_up = w_up.reshape(parts, width, hidden)
    return pl.pallas_call(
        hidden_kernel,
        grid=(parts,),
        in_specs=[
            pl.BlockSpec((1, rows, width), lambda i: (i, 0, 0)),
            pl.BlockSpec((1, width, hidden), lambda i: (i, 0, 0)),
            pl.BlockSpec((1, width, hidden), lambda i: (i, 0, 0)),
        ],
        out_specs=pl.BlockSpec((rows, hidden), lambda i: (0, 0)),
        out_shape=jax.ShapeDtypeStruct((rows, hidden), jnp.bfloat16),
        scratch_shapes=[pltpu.VMEM((rows, hidden), jnp.float32), pltpu.VMEM((rows, hidden), jnp.float32)],
        compiler_params=pltpu.CompilerParams(vmem_limit_bytes=VMEM_LIMIT),
        cost_estimate=pl.CostEstimate(
            flops=4 * rows * parts * width * hidden,
            bytes_accessed=2 * parts * width * (rows + 2 * hidden) + 2 * rows * hidden,
            transcendentals=rows * hidden,
        ),
        name="hidden_units",
    )(x, w_gate, w_up)


def down_kernel(a_ref, w_ref, out_ref):
    total = jnp.dot(a_ref[0], w_ref[0], preferred_element_type=jnp.float32)
    for part in range(1, a_ref.shape[0]):
        total += jnp.dot(a_ref[part], w_ref[part], preferred_element_type=jnp.float32)
    out_ref[...] = total.astype(out_ref.dtype)


def down(act, w_down):
    parts, rows, hidden = act.shape
    width = w_down.shape[2]
    tile = 256
    return pl.pallas_call(
        down_kernel,
        grid=(width // tile,),
        in_specs=[
            pl.BlockSpec((parts, rows, hidden), lambda i: (0, 0, 0)),
            pl.BlockSpec((parts, hidden, tile), lambda i: (0, 0, i)),
        ],
        out_specs=pl.BlockSpec((rows, tile), lambda i: (0, i)),
        out_shape=jax.ShapeDtypeStruct((rows, width), jnp.bfloat16),
        compiler_params=pltpu.CompilerParams(vmem_limit_bytes=VMEM_LIMIT),
        cost_estimate=pl.CostEstimate(
            flops=2 * rows * parts * hidden * width,
            bytes_accessed=2 * (parts * hidden * (rows + width) + rows * width),
            transcendentals=0,
        ),
        name="down",
    )(act, w_down)


def on_device(hidden_rows, expert_ids, affinity, w_gate, w_up, w_down):
    experts = lax.axis_size("ep")
    tp_count = lax.axis_size("tp")
    row_count, width = hidden_rows.shape
    w_gate, w_up, w_down = w_gate[0], w_up[0], w_down[0]

    down_rows = lax.all_to_all(
        w_down.reshape(w_down.shape[0], tp_count, width), "tp", split_axis=1, concat_axis=1, tiled=True
    )
    down_rows = down_rows.transpose(1, 0, 2)

    route_weight = route_scale * affinity / jnp.sum(affinity, axis=1, keepdims=True)
    named = expert_ids[:, :, None] == jnp.arange(experts, dtype=jnp.int32)
    chosen = jnp.any(named, axis=1)
    weight = jnp.sum(jnp.where(named, route_weight[:, :, None], 0.0), axis=1)
    earlier = jnp.tril(jnp.ones((row_count, row_count), jnp.bfloat16), -1)
    slot = jnp.dot(earlier, chosen.astype(jnp.bfloat16), preferred_element_type=jnp.float32).astype(jnp.int32)
    slot = jnp.where(chosen, slot, CAP)

    places, arrived = [], []
    for first, count in CHUNKS:
        here = slot[:, :, None] == first + jnp.arange(count, dtype=jnp.int32)
        places.append(here.reshape(row_count, experts * count))
        outgoing = jnp.dot(
            places[-1].astype(jnp.bfloat16).T, hidden_rows, preferred_element_type=jnp.float32
        ).astype(jnp.bfloat16)
        outgoing = outgoing.reshape(experts, count, width)
        arrived.append(lax.all_to_all(outgoing, "ep", split_axis=0, concat_axis=0, tiled=True))

    mixed = jnp.zeros((row_count, width), jnp.float32)
    for (first, count), place, rows in zip(CHUNKS, places, arrived):
        x = lax.all_gather(rows.reshape(experts * count, width), "tp")
        activated = hidden_units(x, w_gate, w_up)
        activated = lax.all_gather(activated, "tp")
        outputs = down(activated, down_rows).reshape(experts, count, width)
        returned = lax.all_to_all(outputs, "ep", split_axis=0, concat_axis=0, tiled=True)
        returned = returned.reshape(experts * count, width)
        mix = jnp.where(place, jnp.repeat(weight, count, axis=1), 0.0)
        high = mix.astype(jnp.bfloat16)
        low = (mix - high.astype(jnp.float32)).astype(jnp.bfloat16)
        mixed = mixed + jnp.dot(high, returned, preferred_element_type=jnp.float32)
        mixed = mixed + jnp.dot(low, returned, preferred_element_type=jnp.float32)
    return mixed.astype(jnp.bfloat16)


def solution(mesh):
    in_specs = (
        P("ep", "tp"),
        P("ep", None),
        P("ep", None),
        P("ep", None, "tp"),
        P("ep", None, "tp"),
        P("ep", "tp", None),
    )
    out_specs = P("ep", "tp")
    return jax.shard_map(
        on_device, mesh=mesh, in_specs=in_specs, out_specs=out_specs, check_vma=False
    )
```

time: 645 us -> 332 us (0.51)
  blocking collectives: 347 us -> 172 us
  waiting for transfers between devices: 186 us -> 68 us
  matrix products: 31.9 us -> 4.42 us
  Pallas kernels: 0 us -> 25.9 us
  local copies, waits for them, and re-layouts: 45.4 us -> 21 us
  starting transfers between devices: 10.9 us -> 25.8 us
    all_to_all x1 -> x2, blocking collectives: 333 us -> 88.9 us  [on_device(): lax.all_to_all(outgoing, 'ep', split_axis=0, concat_axis=0, tiled=True)]
    reduce_scatter x1 -> x0, waiting for transfers between devices: 103 us -> none  [on_device(): lax.psum_scatter(partial_down, 'tp', scatter_dimension=2, tiled=True)]
    all_gather x1, blocking collectives: 13.7 us -> 83 us  [on_device(): activated = lax.all_gather(activated, 'tp')]
    all_to_all x1 -> x3, waiting for transfers between devices: 83.6 us -> 42.2 us  [the longest x2 42.2 us: on_device(): lax.all_to_all(outputs, 'ep', split_axis=0, concat_axis=0, tiled=True)]
    dot_general x3 -> x7, matrix products: 31.9 us -> 4.42 us  [the longest x2 1.59 us: on_device(): mixed = mixed + jnp.dot(high, returned, preferred_element_type=jnp.float32)]
    pallas_call x0 -> x4, Pallas kernels: none -> 25.9 us  [the longest x2 13.3 us: hidden_units(): pl.pallas_call(hidden_kernel, grid=(parts,), in_specs=[pl.BlockSpec((1, r...]
    all_gather x0 -> x3, waiting for transfers between devices: none -> 25.7 us  [the longest x1 25.7 us: on_device(): activated = lax.all_gather(activated, 'tp')]
    reshape x2, local copies, waits for them, and re-layouts: 19.1 us -> 1.34 us  [the longest x1 1.13 us: on_device(): outputs = down(activated, down_rows).reshape(experts, count, width)]
  transfers between devices with their start and end apart: 2 -> 6, of which waited for: 2 -> 2; matrix products, arithmetic and copies ran while one was open for 0% -> 5% of each run, Pallas kernels for 0% -> 8%
where the time goes in v1:
time: 332 us; the launch traced here: 331 us
  blocking collectives  172 us (52%)
  waiting for transfers between devices  68 us (20%)
  Pallas kernels  25.9 us (8%)
  starting transfers between devices  25.8 us (8%)
  local copies, waits for them, and re-layouts  21 us (6%)
  between operations  13.3 us (4%)
  matrix products  4.42 us (1%)
    all_to_all x2, blocking collectives, on_device(): lax.all_to_all(outgoing, 'ep', split_axis=0, concat_axis=0, tiled=True)  88.9 us
    all_gather x1, blocking collectives, on_device(): activated = lax.all_gather(activated, 'tp')  83 us
    all_to_all x2, waiting for transfers between devices, on_device(): lax.all_to_all(outputs, 'ep', split_axis=0, concat_axis=0, tiled=True)  42.2 us
    all_gather x1, waiting for transfers between devices, on_device(): activated = lax.all_gather(activated, 'tp')  25.7 us
    all_to_all x2, starting transfers between devices, on_device(): lax.all_to_all(outputs, 'ep', split_axis=0, concat_axis=0, tiled=True)  20.9 us
    pallas_call x2, Pallas kernels, hidden_units(): pl.pallas_call(hidden_kernel, grid=(parts,), in_specs=[pl.BlockSpec((1, r...  13.3 us
    pallas_call x2, Pallas kernels, down(): pl.pallas_call(down_kernel, grid=(width // tile,), in_specs=[pl.BlockSpec...  12.5 us
    unnamed x14, local copies, waits for them, and re-layouts  12.1 us
  transfers between devices with their start and end apart: 6, of which 2 were waited for; matrix products, arithmetic and copies ran while one was open for 5% of the time, Pallas kernels for 8%

profile of v1, /device:TPU:1, one launch (start us, length us, event | category | flops | bytes accessed | tf_op | source)
XLA Modules:
  0.0 330.9 jit_solution(1391882191293171403)
XLA Ops:
  6.5 0.8 copy.37
  8.7 38.3 %all_to_all.25 = bf16[64,4,1792]{2,1,0:T(4,128)(2,1)S(1)} all-to-all(bf16[64,4,1792]{2,1,0:T(4,128)(2,1)S(1)} %reshape.56), channel_id=1, replica_groups=mesh['ep'=64,'tp'=4] {'ep'}, dimensions={0} | all-to-all | bytes 1835008 | tf_op jit(solution)/shard_map/all_to_all | solution.py:123
  46.9 1.1 all_gather_reshape.7
  48.2 0.7 fusion
  48.9 50.6 %all_to_all.26 = bf16[64,8,1792]{2,1,0:T(8,128)(2,1)} all-to-all(bf16[64,8,1792]{2,1,0:T(8,128)(2,1)S(1)} %fusion), channel_id=1, replica_groups=mesh['ep'=64,'tp'=4] {'ep'}, dimensions={0} | all-to-all | bytes 3670016 | tf_op jit(solution)/shard_map/all_to_all | solution.py:123
  99.6 6.0 %copy.41 = bf16[1,256,7168]{1,2,0:T(8,128)(2,1)} copy(bf16[1,256,7168]{2,1,0:T(8,128)(2,1)} %param.11) | data formatting | bytes 7340032 | tf_op args[5]
  105.6 6.0 %copy.42 = bf16[256,4,1792]{2,0,1:T(8,128)(2,1)} copy(bf16[256,4,1792]{0,2,1:T(8,128)(2,1)} %bitcast.39) | data formatting | bytes 7340032 | tf_op jit(solution)/shard_map/reshape;squeeze | solution.py:103
  111.5 4.9 %all-to-all-start.1 = ((bf16[256,4,1792]{2,0,1:T(8,128)(2,1)}), bf16[256,4,1792]{2,0,1:T(8,128)(2,1)}, u32[]{:S(2)}, u32[]{:S(2)}) async-start(bf16[256,4,1792]{2,0,1:T(8,128)(2,1)} %copy.42), calls=%async_computation.1 | async-start | bytes 7340032 | tf_op jit(solution)/shard_map/all_to_all | solution.py:102
  116.4 2.0 copy-done.2
  118.5 5.2 %hidden_units.3 = bf16[256,256]{1,0:T(8,128)(2,1)S(1)} custom-call(bf16[4,256,1792]{2,1,0:T(8,128)(2,1)S(1)} %copy-done.2, bf16[4,1792,256]{2,1,0:T(8,128)(2,1)} %bitcast.35, bf16[4,1792,256]{2,1,0:T(8,128)(2,1)} %bitcast.40), custom_call_target="tpu_custom_call" | custom-call | flops 1879048192 | bytes 11141120 | tf_op jit(solution)/shard_map/hidden_units/pallas_call | solution.py:45
  123.7 83.0 %all-gather.1 = bf16[1024,256]{1,0:T(8,128)(2,1)S(1)} all-gather(bf16[256,256]{1,0:T(8,128)(2,1)S(1)} %hidden_units.3), channel_id=3, replica_groups=mesh['ep'=64,'tp'=4] {'tp'}, dimensions={0}, use_global_device_ids=true | all-gather | bytes 655360 | tf_op jit(solution)/shard_map/all_gather | solution.py:129
  206.7 5.5 %down.3 = bf16[256,1792]{1,0:T(8,128)(2,1)S(1)} custom-call(bf16[4,256,256]{2,1,0:T(8,128)(2,1)S(1)} %bitcast.37, bf16[4,256,1792]{2,1,0:T(8,128)(2,1)} %bitcast.7.w_ref), custom_call_target="tpu_custom_call" | custom-call | flops 939524096 | bytes 5111808 | tf_op jit(solution)/shard_map/down/pallas_call | solution.py:77
  212.2 1.1 reshape.57
  213.3 9.1 %all-to-all-start.4 = ((bf16[64,4,1792]{2,1,0:T(4,128)(2,1)}), bf16[64,4,1792]{2,1,0:T(4,128)(2,1)S(1)}, u32[]{:S(2)}, u32[]{:S(2)}) async-start(bf16[64,4,1792]{2,1,0:T(4,128)(2,1)} %reshape.57), calls=%async_computation.4 | async-start | bytes 1835008 | tf_op jit(solution)/shard_map/all_to_all | solution.py:131
  222.5 2.0 copy-done.1
  224.6 8.1 %hidden_units.2 = bf16[512,256]{1,0:T(8,128)(2,1)} custom-call(bf16[4,512,1792]{2,1,0:T(8,128)(2,1)} %all-gather.6.cloned.1.call-done.x_ref, bf16[4,1792,256]{2,1,0:T(8,128)(2,1)S(1)} %bitcast.36, bf16[4,1792,256]{2,1,0:T(8,128)(2,1)} %bitcast.41), custom_call_target="tpu_custom_call" | custom-call | flops 3758096384 | bytes 14942208 | tf_op jit(solution)/shard_map/hidden_units/pallas_call | solution.py:45
  232.7 25.7 %all-gather.10.cloned.1.call-done = bf16[2048,256]{1,0:T(8,128)(2,1)} async-done(((bf16[512,256]{1,0:T(8,128)(2,1)}), bf16[2048,256]{1,0:T(8,128)(2,1)}) %all-gather.10.cloned.1.call-update) | async-done | bytes 1048592 | tf_op jit(solution)/shard_map/all_gather | solution.py:129
  258.4 1.2 copy-done.3
  259.6 7.1 %down.2 = bf16[512,1792]{1,0:T(8,128)(2,1)} custom-call(bf16[4,512,256]{2,1,0:T(8,128)(2,1)S(1)} %bitcast.38, bf16[4,256,1792]{2,1,0:T(8,128)(2,1)} %bitcast.7.w_ref), custom_call_target="tpu_custom_call" | custom-call | flops 1879048192 | bytes 6553600 | tf_op jit(solution)/shard_map/down/pallas_call | solution.py:77
  266.7 11.7 %all-to-all-start.2 = ((bf16[64,8,1792]{2,1,0:T(8,128)(2,1)}), bf16[64,8,1792]{2,1,0:T(8,128)(2,1)S(1)}, u32[]{:S(2)}, u32[]{:S(2)}) async-start(bf16[64,8,1792]{2,1,0:T(8,128)(2,1)} %bitcast.8), calls=%async_computation.2 | async-start | bytes 3670016 | tf_op jit(solution)/shard_map/all_to_all | solution.py:131
  279.4 1.1 convolution_bitcast_fusion.3
  280.5 42.2 %all-to-all-done.2 = bf16[64,8,1792]{2,1,0:T(8,128)(2,1)S(1)} async-done(((bf16[64,8,1792]{2,1,0:T(8,128)(2,1)}), bf16[64,8,1792]{2,1,0:T(8,128)(2,1)S(1)}, u32[]{:S(2)}, u32[]{:S(2)}) %all-to-all-start.2) | async-done | bytes 1835040 | tf_op jit(solution)/shard_map/all_to_all | solution.py:131
  322.7 0.5 convolution_bitcast_fusion.1
  323.2 1.2 fusion.4
  (39 shorter events, 2.5 us)
Async XLA Ops:
  6.5 1.4 copy-start
  6.5 109.9 %all-gather.8.cloned.1.call-start = ((), (), s32[]{:S(2)}) async-start(), calls=%async_computation.6 | async-start | bytes 4587520 | tf_op jit(solution)/shard_map/all_gather | solution.py:127
  48.1 174.4 %all-gather.6.cloned.1.call-start = ((), (), s32[]{:S(2)}) async-start(), calls=%async_computation.5 | async-start | bytes 9175040 | tf_op jit(solution)/shard_map/all_gather | solution.py:127
  111.5 95.2 %all-to-all-start.1 = ((bf16[256,4,1792]{2,0,1:T(8,128)(2,1)}), bf16[256,4,1792]{2,0,1:T(8,128)(2,1)}, u32[]{:S(2)}, u32[]{:S(2)}) async-start(bf16[256,4,1792]{2,0,1:T(8,128)(2,1)} %copy.42), calls=%async_computation.1 | async-start | bytes 7340032 | tf_op jit(solution)/shard_map/all_to_all | solution.py:102
  116.4 2.0 copy-start.2
  213.3 53.4 %all-to-all-start.4 = ((bf16[64,4,1792]{2,1,0:T(4,128)(2,1)}), bf16[64,4,1792]{2,1,0:T(4,128)(2,1)S(1)}, u32[]{:S(2)}, u32[]{:S(2)}) async-start(bf16[64,4,1792]{2,1,0:T(4,128)(2,1)} %reshape.57), calls=%async_computation.4 | async-start | bytes 1835008 | tf_op jit(solution)/shard_map/all_to_all | solution.py:131
  222.5 35.9 %all-gather.10.cloned.1.call-start = ((), (), s32[]{:S(2)}) async-start(), calls=%async_computation.7 | async-start | bytes 1310720 | tf_op jit(solution)/shard_map/all_gather | solution.py:129
  222.5 2.0 copy-start.1
  258.4 1.2 copy-start.3
  266.7 11.7 %copy-start.5 = (f32[64,8]{0,1:T(8,128)S(1)}, f32[64,8]{0,1:T(8,128)}, u32[]{:S(2)}) copy-start(f32[64,8]{0,1:T(8,128)} %param.8) | copy-start | bytes 6148
  266.7 56.0 %all-to-all-start.2 = ((bf16[64,8,1792]{2,1,0:T(8,128)(2,1)}), bf16[64,8,1792]{2,1,0:T(8,128)(2,1)S(1)}, u32[]{:S(2)}, u32[]{:S(2)}) async-start(bf16[64,8,1792]{2,1,0:T(8,128)(2,1)} %bitcast.8), calls=%async_computation.2 | async-start | bytes 3670016 | tf_op jit(solution)/shard_map/all_to_all | solution.py:131
  280.5 42.7 %copy-start.4 = (f32[64,1792]{1,0:T(8,128)S(1)}, f32[64,1792]{1,0:T(8,128)}, u32[]{:S(2)}) copy-start(f32[64,1792]{1,0:T(8,128)} %convolution_bitcast_fusion.3) | copy-start | bytes 1376260
Sparse Core Ops, SparseCore 0:
  48.2 43.5 all-gather.7
  99.7 117.8 all-gather.5
  232.8 25.5 all-gather.9

commit v2 on v1

v2 whole, which is shorter than its diff:
```python
import functools

import jax
import jax.numpy as jnp
from jax import lax
from jax.experimental import pallas as pl
from jax.experimental.pallas import tpu as pltpu
from jax.sharding import PartitionSpec as P

CAP = 12
CHUNKS = ((0, 4, False), (4, 4, True), (8, 4, False))
SENDS = (1, 3, 2)
STEPS = (0, 3, 1, 2)
TILES = 2
TOLD = (100, 100, 1)
WAIT_TOLD = 200_000_000_000
MIB = 1024 * 1024
CORNER = pl.BlockSpec((16, 128), lambda *index: (0, 0))
IN_HBM = pl.BlockSpec(memory_space=pltpu.HBM)
CORNER_SLOTS = pl.BlockSpec((8, 4, 128), lambda *index: (0, 0, 0))


route_scale = 2.5


def store_slots(out_ref, total):
    count = out_ref.shape[1]
    for expert in range(out_ref.shape[0]):
        out_ref[expert] = total[expert * count:(expert + 1) * count].astype(out_ref.dtype)


def silu_times(gate, up):
    return gate / (1.0 + jnp.exp(-gate)) * up


def hidden_kernel(gathered, parts, me_ref, *refs):
    arrays = 1 if gathered else parts
    xs, (gate_ref, up_ref) = refs[:arrays], refs[arrays:arrays + 2]
    out_ref, x_buffer, gate_buffer, up_buffer, gate_sum, up_sum, arrivals = refs[-7:]
    copies = []
    for number, step in enumerate(range(parts) if gathered else STEPS):
        part = step if gathered else lax.rem(me_ref[0] + step, parts)
        x_part = xs[0].at[step] if gathered else xs[number]
        pairs = (
            (x_part, x_buffer.at[number]),
            (gate_ref.at[part], gate_buffer.at[number]),
            (up_ref.at[part], up_buffer.at[number]),
        )
        copies.append(
            [pltpu.make_async_copy(a, b, arrivals.at[number, i]) for i, (a, b) in enumerate(pairs)]
        )
        for copy in copies[-1]:
            copy.start()
    for number in range(parts):
        for copy in copies[number]:
            copy.wait()
        x = x_buffer[number]
        gate_part = jnp.dot(x, gate_buffer[number], preferred_element_type=jnp.float32)
        up_part = jnp.dot(x, up_buffer[number], preferred_element_type=jnp.float32)
        if number == 0:
            gate_sum[...] = gate_part
            up_sum[...] = up_part
        elif number < parts - 1:
            gate_sum[...] += gate_part
            up_sum[...] += up_part
        else:
            out_ref[...] = silu_times(gate_sum[...] + gate_part, up_sum[...] + up_part).astype(out_ref.dtype)


def hidden_units(me, xs, w_gate, w_up, after, told):
    gathered = len(xs) == 1
    parts, width, hidden = w_gate.shape
    rows = xs[0].shape[-2]
    return pl.pallas_call(
        functools.partial(hidden_kernel, gathered, parts),
        grid_spec=pltpu.PrefetchScalarGridSpec(
            num_scalar_prefetch=1,
            grid=(1,),
            in_specs=[IN_HBM] * (len(xs) + 2) + [CORNER] * len(after),
            out_specs=pl.BlockSpec((rows, hidden), lambda i, me: (0, 0)),
            scratch_shapes=[
                pltpu.VMEM((parts, rows, width), jnp.bfloat16),
                pltpu.VMEM((parts, width, hidden), jnp.bfloat16),
                pltpu.VMEM((parts, width, hidden), jnp.bfloat16),
                pltpu.VMEM((rows, hidden), jnp.float32),
                pltpu.VMEM((rows, hidden), jnp.float32),
                pltpu.SemaphoreType.DMA((parts, 3)),
            ],
        ),
        out_shape=jax.ShapeDtypeStruct((rows, hidden), jnp.bfloat16),
        compiler_params=pltpu.CompilerParams(vmem_limit_bytes=60 * MIB),
        cost_estimate=pl.CostEstimate(
            flops=4 * rows * parts * width * hidden * told,
            bytes_accessed=2 * parts * width * (rows + 2 * hidden) + 2 * rows * hidden,
            transcendentals=rows * hidden,
        ),
        name="hidden_units",
    )(me, *xs, w_gate, w_up, *after)


def down_kernel(parts, me_ref, *refs):
    acts, own_ref, pieces = refs[:parts], refs[parts], refs[parts + 1:2 * parts]
    out_ref, weights, slots, arrivals, departures = refs[-5:]
    width = slots.shape[2]
    tile = width // TILES
    copies = []
    for number in range(TILES):
        sources = [own_ref.at[:, pl.ds(pl.multiple_of(me_ref[0] * width + number * tile, 128), tile)]]
        sources += [piece.at[:, pl.ds(number * tile, tile)] for piece in pieces]
        copies.append([
            pltpu.make_async_copy(source, weights.at[number, i], arrivals.at[number, i])
            for i, source in enumerate(sources)
        ])
        for copy in copies[-1]:
            copy.start()
    leaving = []
    for number in range(TILES):
        for copy in copies[number]:
            copy.wait()
        total = jnp.dot(acts[0][...], weights[number, 0], preferred_element_type=jnp.float32)
        for i in range(1, parts):
            total += jnp.dot(acts[i][...], weights[number, i], preferred_element_type=jnp.float32)
        store_slots(slots.at[:, :, pl.ds(number * tile, tile)], total)
        where = pl.ds(number * tile, tile)
        leaving.append(
            pltpu.make_async_copy(slots.at[:, :, where], out_ref.at[:, :, where], departures.at[number])
        )
        leaving[-1].start()
    for copy in leaving:
        copy.wait()


def down(me, acts, w_down, pieces, experts):
    rows, hidden = acts[0].shape
    width = pieces[0].shape[1]
    parts = len(acts)
    shape = (experts, rows // experts, width)
    return pl.pallas_call(
        functools.partial(down_kernel, parts),
        grid_spec=pltpu.PrefetchScalarGridSpec(
            num_scalar_prefetch=1,
            grid=(1,),
            in_specs=[pl.BlockSpec((rows, hidden), lambda i, me: (0, 0))] * parts + [IN_HBM] * parts,
            out_specs=IN_HBM,
            scratch_shapes=[
                pltpu.VMEM((TILES, parts, hidden, width // TILES), jnp.bfloat16),
                pltpu.VMEM(shape, jnp.bfloat16),
                pltpu.SemaphoreType.DMA((TILES, parts)),
                pltpu.SemaphoreType.DMA((TILES,)),
            ],
        ),
        out_shape=jax.ShapeDtypeStruct(shape, jnp.bfloat16),
        compiler_params=pltpu.CompilerParams(vmem_limit_bytes=60 * MIB),
        cost_estimate=pl.CostEstimate(
            flops=2 * rows * parts * hidden * width,
            bytes_accessed=2 * (parts * hidden * (rows + width) + rows * width),
            transcendentals=0,
        ),
        name="down",
    )(me, *acts, w_down, *pieces)


def place_kernel(spot_ref, rows_ref, *rest):
    out_ref, slots, departures = rest[-3:]
    tile = rows_ref.shape[1] // TILES
    leaving = []
    for number in range(TILES):
        where = pl.ds(number * tile, tile)
        total = lax.dot_general(
            spot_ref[...], rows_ref[:, where], (((0,), (0,)), ((), ())), preferred_element_type=jnp.float32
        )
        store_slots(slots.at[:, :, where], total)
        leaving.append(
            pltpu.make_async_copy(slots.at[:, :, where], out_ref.at[:, :, where], departures.at[number])
        )
        leaving[-1].start()
    for copy in leaving:
        copy.wait()


def wait_kernel(*refs):
    refs[-1][...] = jnp.zeros(refs[-1].shape, refs[-1].dtype)


def wait_for(arrays, told):
    return pl.pallas_call(
        wait_kernel,
        grid=(1,),
        in_specs=[CORNER if array.ndim == 2 else CORNER_SLOTS for array in arrays],
        out_specs=CORNER,
        out_shape=jax.ShapeDtypeStruct((16, 128), jnp.bfloat16),
        cost_estimate=pl.CostEstimate(flops=told, bytes_accessed=0, transcendentals=0),
        name="wait_for",
    )(*arrays)


def place_rows(spot, rows, experts, after, told):
    slots, width = spot.shape[1], rows.shape[1]
    shape = (experts, slots // experts, width)
    return pl.pallas_call(
        place_kernel,
        grid=(1,),
        in_specs=[
            pl.BlockSpec((rows.shape[0], slots), lambda i: (0, 0)),
            pl.BlockSpec((rows.shape[0], width), lambda i: (0, 0)),
        ]
        + [CORNER if array.ndim == 2 else CORNER_SLOTS for array in after],
        out_specs=IN_HBM,
        scratch_shapes=[pltpu.VMEM(shape, jnp.bfloat16), pltpu.SemaphoreType.DMA((TILES,))],
        out_shape=jax.ShapeDtypeStruct(shape, jnp.bfloat16),
        compiler_params=pltpu.CompilerParams(vmem_limit_bytes=60 * MIB),
        cost_estimate=pl.CostEstimate(
            flops=2 * slots * rows.shape[0] * width * told,
            bytes_accessed=2 * (slots + rows.shape[0]) * width,
            transcendentals=0,
        ),
        name="place_rows",
    )(spot, rows, *after)


def on_device(hidden_rows, expert_ids, affinity, w_gate, w_up, w_down):
    experts = lax.axis_size("ep")
    parts = lax.axis_size("tp")
    row_count, width = hidden_rows.shape
    place = lax.axis_index("tp")
    me = place.reshape(1).astype(jnp.int32)
    w_gate = w_gate[0].reshape(parts, width, w_gate.shape[2])
    w_up = w_up[0].reshape(parts, width, w_up.shape[2])
    w_down = w_down[0]

    def send(array, step):
        return lax.ppermute(array, "tp", [(i, (i + step) % parts) for i in range(parts)])

    def send_all(array):
        return [send(array, step) for step in SENDS]

    slices = [
        lax.dynamic_slice_in_dim(w_down, (place + step) % parts * width, width, axis=1) for step in SENDS
    ]
    pieces = [send(part, step) for part, step in zip(slices, SENDS)]

    route_weight = route_scale * affinity / jnp.sum(affinity, axis=1, keepdims=True)
    named = expert_ids[:, :, None] == jnp.arange(experts, dtype=jnp.int32)
    chosen = jnp.any(named, axis=1)
    weight = jnp.sum(jnp.where(named, route_weight[:, :, None], 0.0), axis=1)
    earlier = jnp.tril(jnp.ones((row_count, row_count), jnp.bfloat16), -1)
    slot = jnp.dot(earlier, chosen.astype(jnp.bfloat16), preferred_element_type=jnp.float32).astype(jnp.int32)
    slot = jnp.where(chosen, slot, CAP)

    places, gathered = [], []
    for number, (first, count, by_permutes) in enumerate(CHUNKS):
        here = slot[:, :, None] == first + jnp.arange(count, dtype=jnp.int32)
        places.append(here.reshape(row_count, experts * count))
        after = slices if number == 0 else [before] if number == 1 else [before, waited]
        outgoing = place_rows(places[-1].astype(jnp.bfloat16), hidden_rows, experts, after, 1)
        rows = lax.all_to_all(outgoing, "ep", split_axis=0, concat_axis=0, tiled=True)
        if number == 0:
            waited = wait_for([*pieces, rows], WAIT_TOLD)
        before = rows
        rows = rows.reshape(experts * count, width)
        gathered.append([rows] + send_all(rows) if by_permutes else lax.all_gather(rows, "tp"))

    mixed = jnp.zeros((row_count, width), jnp.float32)
    for number, ((first, count, by_permutes), spot, x, told) in enumerate(zip(CHUNKS, places, gathered, TOLD)):
        after = [activated] if number else []
        activated = hidden_units(me, x if by_permutes else [x], w_gate, w_up, after, told)
        outputs = down(me, [activated] + send_all(activated), w_down, pieces, experts)
        returned = lax.all_to_all(outputs, "ep", split_axis=0, concat_axis=0, tiled=True)
        returned = returned.reshape(experts * count, width)
        mix = jnp.where(spot, jnp.repeat(weight, count, axis=1), 0.0)
        high = mix.astype(jnp.bfloat16)
        low = (mix - high.astype(jnp.float32)).astype(jnp.bfloat16)
        mixed = mixed + jnp.dot(high, returned, preferred_element_type=jnp.float32)
        mixed = mixed + jnp.dot(low, returned, preferred_element_type=jnp.float32)
    return mixed.astype(jnp.bfloat16)


def solution(mesh):
    in_specs = (
        P("ep", "tp"),
        P("ep", None),
        P("ep", None),
        P("ep", None, "tp"),
        P("ep", None, "tp"),
        P("ep", "tp", None),
    )
    out_specs = P("ep", "tp")
    return jax.shard_map(
        on_device, mesh=mesh, in_specs=in_specs, out_specs=out_specs, check_vma=False
    )
```

time: 332 us -> 272 us (0.82)
  blocking collectives: 172 us -> 0 us
  starting transfers between devices: 25.8 us -> 77.9 us
  waiting for transfers between devices: 68 us -> 119 us
  Pallas kernels: 25.9 us -> 40.9 us
  local copies, waits for them, and re-layouts: 21 us -> 13.1 us
    all_to_all x2 -> x0, blocking collectives: 88.9 us -> none  [on_device(): lax.all_to_all(outgoing, 'ep', split_axis=0, concat_axis=0, tiled=True)]
    all_gather x1 -> x0, blocking collectives: 83 us -> none  [on_device(): activated = lax.all_gather(activated, 'tp')]
    ppermute x0 -> x15, waiting for transfers between devices: none -> 57 us  [send(): lax.ppermute(array, 'tp', [(i, (i + step) % parts) for i in range(parts)])]
    all_to_all x1 -> x3, waiting for transfers between devices: 0.01 us -> 33.9 us  [on_device(): lax.all_to_all(outgoing, 'ep', split_axis=0, concat_axis=0, tiled=True)]
    all_to_all x1 -> x3, starting transfers between devices: 4.86 us -> 27.3 us  [on_device(): lax.all_to_all(outgoing, 'ep', split_axis=0, concat_axis=0, tiled=True)]
    all_gather x3 -> x2, waiting for transfers between devices: 25.7 us -> 3.61 us  [on_device(): lax.all_gather(rows, 'tp')]
    ppermute x0 -> x15, starting transfers between devices: none -> 18.9 us  [send(): lax.ppermute(array, 'tp', [(i, (i + step) % parts) for i in range(parts)])]
    all_to_all x2 -> x3, waiting for transfers between devices: 42.2 us -> 24.1 us  [on_device(): lax.all_to_all(outputs, 'ep', split_axis=0, concat_axis=0, tiled=True)]
  transfers between devices with their start and end apart: 6 -> 23, of which waited for: 2 -> 13; matrix products, arithmetic and copies ran while one was open for 5% -> 4% of each run, Pallas kernels for 8% -> 14%
where the time goes in v2:
time: 272 us; the launch traced here: 271 us
  waiting for transfers between devices  119 us (44%)
  starting transfers between devices  77.9 us (29%)
  Pallas kernels  40.9 us (15%)
  between operations  13.9 us (5%)
  local copies, waits for them, and re-layouts  13.1 us (5%)
  matrix products  5.12 us (2%)
    ppermute x15, waiting for transfers between devices, send(): lax.ppermute(array, 'tp', [(i, (i + step) % parts) for i in range(parts)])  57 us
    all_to_all x3, waiting for transfers between devices, on_device(): lax.all_to_all(outgoing, 'ep', split_axis=0, concat_axis=0, tiled=True)  33.9 us
    all_to_all x3, starting transfers between devices, on_device(): lax.all_to_all(outputs, 'ep', split_axis=0, concat_axis=0, tiled=True)  31.6 us
    all_to_all x3, starting transfers between devices, on_device(): lax.all_to_all(outgoing, 'ep', split_axis=0, concat_axis=0, tiled=True)  27.3 us
    all_to_all x3, waiting for transfers between devices, on_device(): lax.all_to_all(outputs, 'ep', split_axis=0, concat_axis=0, tiled=True)  24.1 us
    ppermute x15, starting transfers between devices, send(): lax.ppermute(array, 'tp', [(i, (i + step) % parts) for i in range(parts)])  18.9 us
    pallas_call x3, Pallas kernels, hidden_units(): pl.pallas_call(functools.partial(hidden_kernel, gathered, parts), grid_sp...  18.2 us
    pallas_call x3, Pallas kernels, down(): pl.pallas_call(functools.partial(down_kernel, parts), grid_spec=pltpu.Pre...  14.6 us
  transfers between devices with their start and end apart: 23, of which 13 were waited for; matrix products, arithmetic and copies ran while one was open for 4% of the time, Pallas kernels for 14%

profile of v2, /device:TPU:1, one launch (start us, length us, event | category | flops | bytes accessed | tf_op | source)
XLA Modules:
  0.0 270.9 jit_solution(10441099138325813628)
XLA Ops:
  9.2 3.3 %dynamic-slice_bitcast_fusion = (bf16[256,1792]{1,0:T(8,128)(2,1)}, bf16[256,1792]{1,0:T(8,128)(2,1)}, bf16[256,1792]{1,0:T(8,128)(2,1)}) fusion(bf16[1,256,7168]{2,1,0:T(8,128)(2,1)} %param.11, s32[]{:T(128)S(6)} %select_n.61, s32[]{:T(128)S(6)} %select_n.59, s32[]{:T(128)S(6)} %select_n.57), kind=kLoop, calls=%fused_computation.14 | loop fusion | bytes 5505036 | tf_op jit(solution)/shard_map/dynamic_slice | solution.py:238
  14.8 13.2 %all-to-all-start = ((bf16[64,4,1792]{2,1,0:T(4,128)(2,1)}), bf16[64,4,1792]{2,1,0:T(4,128)(2,1)S(1)}, u32[]{:S(2)}, u32[]{:S(2)}) async-start(bf16[64,4,1792]{2,1,0:T(4,128)(2,1)} %place_rows.3), calls=%async_computation | async-start | bytes 1835008 | tf_op jit(solution)/shard_map/all_to_all | solution.py:256
  32.3 21.0 %all-to-all-done.rest_0_.refs_3_ = bf16[64,4,1792]{2,1,0:T(4,128)(2,1)S(1)} async-done(((bf16[64,4,1792]{2,1,0:T(4,128)(2,1)}), bf16[64,4,1792]{2,1,0:T(4,128)(2,1)S(1)}, u32[]{:S(2)}, u32[]{:S(2)}) %all-to-all-start) | async-done | bytes 917536 | tf_op jit(solution)/shard_map/all_to_all | solution.py:256
  56.8 6.6 %all-to-all-start.2 = ((bf16[64,4,1792]{2,1,0:T(4,128)(2,1)}), bf16[64,4,1792]{2,1,0:T(4,128)(2,1)}, u32[]{:S(2)}, u32[]{:S(2)}) async-start(bf16[64,4,1792]{2,1,0:T(4,128)(2,1)} %place_rows.4), calls=%async_computation.2 | async-start | bytes 1835008 | tf_op jit(solution)/shard_map/all_to_all | solution.py:256
  63.4 10.9 %collective-permute-done.5.refs_7_.refs_2_ = bf16[256,1792]{1,0:T(8,128)(2,1)} collective-permute-done((bf16[256,1792]{1,0:T(8,128)(2,1)}, bf16[256,1792]{1,0:T(8,128)(2,1)}, u32[]{:S(2)}, u32[]{:S(2)}) %collective-permute-start.5) | collective-permute-done | bytes 917536 | tf_op jit(solution)/shard_map/ppermute | solution.py:232
  75.7 13.0 %all-to-all-done.2.rest_0_ = bf16[64,4,1792]{2,1,0:T(4,128)(2,1)} async-done(((bf16[64,4,1792]{2,1,0:T(4,128)(2,1)}), bf16[64,4,1792]{2,1,0:T(4,128)(2,1)}, u32[]{:S(2)}, u32[]{:S(2)}) %all-to-all-start.2) | async-done | bytes 917536 | tf_op jit(solution)/shard_map/all_to_all | solution.py:256
  97.6 7.5 %all-to-all-start.4 = ((bf16[64,4,1792]{2,1,0:T(4,128)(2,1)}), bf16[64,4,1792]{2,1,0:T(4,128)(2,1)}, u32[]{:S(2)}, u32[]{:S(2)}) async-start(bf16[64,4,1792]{2,1,0:T(4,128)(2,1)} %place_rows.5), calls=%async_computation.4 | async-start | bytes 1835008 | tf_op jit(solution)/shard_map/all_to_all | solution.py:256
  105.1 3.6 %all-gather.3.cloned.1.call-done.refs_0_ = bf16[4,256,1792]{2,1,0:T(8,128)(2,1)} async-done(((bf16[1,256,1792]{2,1,0:T(8,128)(2,1)}), bf16[4,256,1792]{2,1,0:T(8,128)(2,1)}) %all-gather.3.cloned.1.call-update) | async-done | bytes 3670032 | tf_op jit(solution)/shard_map/all_gather | solution.py:261
  108.7 5.6 %hidden_units.3.refs_0_.refs_6_ = bf16[256,256]{1,0:T(8,128)(2,1)} custom-call(s32[1]{0:T(128)} %bitcast.me_ref, bf16[4,256,1792]{2,1,0:T(8,128)(2,1)} %all-gather.3.cloned.1.call-done.refs_0_, bf16[4,1792,256]{2,1,0:T(8,128)(2,1)} %bitcast.39, bf16[4,1792,256]{2,1,0:T(8,128)(2,1)} %bitcast.42), custom_call_target="tpu_custom_call" | custom-call | flops 187904819200 | bytes 11141120 | tf_op jit(solution)/shard_map/hidden_units/pallas_call | solution.py:74
  117.2 26.4 %collective-permute-done.refs_1_ = bf16[256,256]{1,0:T(8,128)(2,1)S(1)} collective-permute-done((bf16[256,256]{1,0:T(8,128)(2,1)}, bf16[256,256]{1,0:T(8,128)(2,1)S(1)}, u32[]{:S(2)}, u32[]{:S(2)}) %collective-permute-start) | collective-permute-done | bytes 131104 | tf_op jit(solution)/shard_map/ppermute | solution.py:232
  149.8 4.9 %down.3 = bf16[64,4,1792]{2,1,0:T(4,128)(2,1)} custom-call(s32[1]{0:T(128)} %bitcast.me_ref, bf16[256,256]{1,0:T(8,128)(2,1)} %hidden_units.3.refs_0_.refs_6_, bf16[256,256]{1,0:T(8,128)(2,1)} %copy-done.7, bf16[256,256]{1,0:T(8,128)(2,1)} %copy-done.8, bf16[256,256]{1,0:T(8,128)(2,1)} %copy-done.9, bf16[256,7168]{1,0:T(8,128)(2,1)} %bitcast.36, ...), custom_call_target="tpu_custom_call" | custom-call | flops 939524096 | bytes 5111808 | tf_op jit(solution)/shard_map/down/pallas_call | solution.py:138
  154.6 12.7 %all-to-all-start.1 = ((bf16[64,4,1792]{2,1,0:T(4,128)(2,1)}), bf16[64,4,1792]{2,1,0:T(4,128)(2,1)}, u32[]{:S(2)}, u32[]{:S(2)}) async-start(bf16[64,4,1792]{2,1,0:T(4,128)(2,1)} %down.3), calls=%async_computation.1 | async-start | bytes 1835008 | tf_op jit(solution)/shard_map/all_to_all | solution.py:268
  167.4 6.4 %hidden_units.4.refs_0_.refs_3_ = bf16[256,256]{1,0:T(8,128)(2,1)} custom-call(s32[1]{0:T(128)} %bitcast.me_ref, bf16[256,1792]{1,0:T(8,128)(2,1)} %reshape.73.refs_0_, bf16[256,1792]{1,0:T(8,128)(2,1)} %collective-permute-done.6.refs_1_, bf16[256,1792]{1,0:T(8,128)(2,1)} %collective-permute-done.7.refs_2_, ...), custom_call_target="tpu_custom_call" | custom-call | flops 187904819200 | bytes 11141120 | tf_op jit(solution)/shard_map/hidden_units/pallas_call | solution.py:74
  173.8 2.7 collective-permute-start.10
  176.5 7.5 %collective-permute-done.9.refs_1_ = bf16[256,256]{1,0:T(8,128)(2,1)S(1)} collective-permute-done((bf16[256,256]{1,0:T(8,128)(2,1)}, bf16[256,256]{1,0:T(8,128)(2,1)S(1)}, u32[]{:S(2)}, u32[]{:S(2)}) %collective-permute-start.9) | collective-permute-done | bytes 131104 | tf_op jit(solution)/shard_map/ppermute | solution.py:232
  184.0 3.5 %collective-permute-done.11.refs_3_ = bf16[256,256]{1,0:T(8,128)(2,1)S(1)} collective-permute-done((bf16[256,256]{1,0:T(8,128)(2,1)}, bf16[256,256]{1,0:T(8,128)(2,1)S(1)}, u32[]{:S(2)}, u32[]{:S(2)}) %collective-permute-start.11) | collective-permute-done | bytes 131104 | tf_op jit(solution)/shard_map/ppermute | solution.py:232
  188.2 4.9 %down.4 = bf16[64,4,1792]{2,1,0:T(4,128)(2,1)} custom-call(s32[1]{0:T(128)} %bitcast.me_ref, bf16[256,256]{1,0:T(8,128)(2,1)} %hidden_units.4.refs_0_.refs_3_, bf16[256,256]{1,0:T(8,128)(2,1)} %copy-done.12, bf16[256,256]{1,0:T(8,128)(2,1)} %copy-done.14, bf16[256,256]{1,0:T(8,128)(2,1)} %copy-done.15, bf16[256,7168]{1,0:T(8,128)(2,1)} %bitcast.37, ...), custom_call_target="tpu_custom_call" | custom-call | flops 939524096 | bytes 5111808 | tf_op jit(solution)/shard_map/down/pallas_call | solution.py:138
  193.2 11.1 %all-to-all-start.3 = ((bf16[64,4,1792]{2,1,0:T(4,128)(2,1)}), bf16[64,4,1792]{2,1,0:T(4,128)(2,1)S(1)}, u32[]{:S(2)}, u32[]{:S(2)}) async-start(bf16[64,4,1792]{2,1,0:T(4,128)(2,1)} %down.4), calls=%async_computation.3 | async-start | bytes 1835008 | tf_op jit(solution)/shard_map/all_to_all | solution.py:268
  204.3 6.2 %hidden_units.5.refs_0_ = bf16[256,256]{1,0:T(8,128)(2,1)} custom-call(s32[1]{0:T(128)} %bitcast.me_ref, bf16[4,256,1792]{2,1,0:T(8,128)(2,1)} %all-gather.5.cloned.1.call-done.refs_0_, bf16[4,1792,256]{2,1,0:T(8,128)(2,1)} %bitcast.41, bf16[4,1792,256]{2,1,0:T(8,128)(2,1)} %bitcast.44, bf16[256,256]{1,0:T(8,128)(2,1)} %hidden_units.4.refs_0_.refs_3_), custom_call_target="tpu_custom_call" | custom-call | flops 1879048192 | bytes 11141120 | tf_op jit(solution)/shard_map/hidden_units/pallas_call | solution.py:74
  217.2 3.7 %collective-permute-done.14.refs_3_ = bf16[256,256]{1,0:T(8,128)(2,1)S(1)} collective-permute-done((bf16[256,256]{1,0:T(8,128)(2,1)}, bf16[256,256]{1,0:T(8,128)(2,1)S(1)}, u32[]{:S(2)}, u32[]{:S(2)}) %collective-permute-start.14) | collective-permute-done | bytes 131104 | tf_op jit(solution)/shard_map/ppermute | solution.py:232
  221.6 4.8 %down.5 = bf16[64,4,1792]{2,1,0:T(4,128)(2,1)} custom-call(s32[1]{0:T(128)} %bitcast.me_ref, bf16[256,256]{1,0:T(8,128)(2,1)} %hidden_units.5.refs_0_, bf16[256,256]{1,0:T(8,128)(2,1)} %copy-done.10, bf16[256,256]{1,0:T(8,128)(2,1)} %copy-done.11, bf16[256,256]{1,0:T(8,128)(2,1)} %copy-done.13, bf16[256,7168]{1,0:T(8,128)(2,1)} %bitcast.38, ...), custom_call_target="tpu_custom_call" | custom-call | flops 939524096 | bytes 5111808 | tf_op jit(solution)/shard_map/down/pallas_call | solution.py:138
  226.4 3.1 %all-to-all-done.3 = bf16[64,4,1792]{2,1,0:T(4,128)(2,1)S(1)} async-done(((bf16[64,4,1792]{2,1,0:T(4,128)(2,1)}), bf16[64,4,1792]{2,1,0:T(4,128)(2,1)S(1)}, u32[]{:S(2)}, u32[]{:S(2)}) %all-to-all-start.3) | async-done | bytes 917536 | tf_op jit(solution)/shard_map/all_to_all | solution.py:268
  229.6 7.9 %all-to-all-start.5 = ((bf16[64,4,1792]{2,1,0:T(4,128)(2,1)}), bf16[64,4,1792]{2,1,0:T(4,128)(2,1)S(1)}, u32[]{:S(2)}, u32[]{:S(2)}) async-start(bf16[64,4,1792]{2,1,0:T(4,128)(2,1)} %down.5), calls=%async_computation.5 | async-start | bytes 1835008 | tf_op jit(solution)/shard_map/all_to_all | solution.py:268
  241.8 21.0 %all-to-all-done.5 = bf16[64,4,1792]{2,1,0:T(4,128)(2,1)S(1)} async-done(((bf16[64,4,1792]{2,1,0:T(4,128)(2,1)}), bf16[64,4,1792]{2,1,0:T(4,128)(2,1)S(1)}, u32[]{:S(2)}, u32[]{:S(2)}) %all-to-all-start.5) | async-done | bytes 917536 | tf_op jit(solution)/shard_map/all_to_all | solution.py:268
  (108 shorter events, 45.6 us)
Async XLA Ops:
  14.8 38.5 %all-to-all-start = ((bf16[64,4,1792]{2,1,0:T(4,128)(2,1)}), bf16[64,4,1792]{2,1,0:T(4,128)(2,1)S(1)}, u32[]{:S(2)}, u32[]{:S(2)}) async-start(bf16[64,4,1792]{2,1,0:T(4,128)(2,1)} %place_rows.3), calls=%async_computation | async-start | bytes 1835008 | tf_op jit(solution)/shard_map/all_to_all | solution.py:256
  28.0 80.7 %all-gather.3.cloned.1.call-start = ((), (), s32[]{:S(2)}) async-start(), calls=%async_computation.6 | async-start | bytes 4587520 | tf_op jit(solution)/shard_map/all_gather | solution.py:261
  28.0 35.4 %collective-permute-start.3 = (bf16[256,1792]{1,0:T(8,128)(2,1)}, bf16[256,1792]{1,0:T(8,128)(2,1)S(1)}, u32[]{:S(2)}, u32[]{:S(2)}) collective-permute-start(bf16[256,1792]{1,0:T(8,128)(2,1)} %get-tuple-element.7.rest_0_), channel_id=1, source_target_pairs={{0,1},{1,2},{2,3},{3,0},{4,5},{5,6},{6,7},{7,4},{8,9},{9,10},{10,1... | collective-permute-start | bytes 2752520 | tf_op jit(solution)/shard_map/ppermute | solution.py:232
  29.3 34.1 %collective-permute-start.4 = (bf16[256,1792]{1,0:T(8,128)(2,1)}, bf16[256,1792]{1,0:T(8,128)(2,1)S(1)}, u32[]{:S(2)}, u32[]{:S(2)}) collective-permute-start(bf16[256,1792]{1,0:T(8,128)(2,1)} %get-tuple-element.6.rest_1_), channel_id=1, source_target_pairs={{0,3},{1,0},{2,1},{3,2},{4,7},{5,4},{6,5},{7,6},{8,11},{9,8},{10,9... | collective-permute-start | bytes 2752520 | tf_op jit(solution)/shard_map/ppermute | solution.py:232
  30.8 43.6 %collective-permute-start.5 = (bf16[256,1792]{1,0:T(8,128)(2,1)}, bf16[256,1792]{1,0:T(8,128)(2,1)}, u32[]{:S(2)}, u32[]{:S(2)}) collective-permute-start(bf16[256,1792]{1,0:T(8,128)(2,1)} %get-tuple-element.5.rest_2_), channel_id=1, source_target_pairs={{0,2},{1,3},{2,0},{3,1},{4,6},{5,7},{6,4},{7,5},{8,10},{9,11},{10,... | collective-permute-start | bytes 2752520 | tf_op jit(solution)/shard_map/ppermute | solution.py:232
  56.8 31.9 %all-to-all-start.2 = ((bf16[64,4,1792]{2,1,0:T(4,128)(2,1)}), bf16[64,4,1792]{2,1,0:T(4,128)(2,1)}, u32[]{:S(2)}, u32[]{:S(2)}) async-start(bf16[64,4,1792]{2,1,0:T(4,128)(2,1)} %place_rows.4), calls=%async_computation.2 | async-start | bytes 1835008 | tf_op jit(solution)/shard_map/all_to_all | solution.py:256
  91.1 76.3 %collective-permute-start.6 = (bf16[256,1792]{1,0:T(8,128)(2,1)}, bf16[256,1792]{1,0:T(8,128)(2,1)}, u32[]{:S(2)}, u32[]{:S(2)}) collective-permute-start(bf16[256,1792]{1,0:T(8,128)(2,1)} %reshape.73.refs_0_), channel_id=1, source_target_pairs={{0,1},{1,2},{2,3},{3,0},{4,5},{5,6},{6,7},{7,4},{8,9},{9,10},{10,1... | collective-permute-start | bytes 2752520 | tf_op jit(solution)/shard_map/ppermute | solution.py:232
  92.3 75.1 %collective-permute-start.7 = (bf16[256,1792]{1,0:T(8,128)(2,1)}, bf16[256,1792]{1,0:T(8,128)(2,1)}, u32[]{:S(2)}, u32[]{:S(2)}) collective-permute-start(bf16[256,1792]{1,0:T(8,128)(2,1)} %reshape.73.refs_0_), channel_id=1, source_target_pairs={{0,3},{1,0},{2,1},{3,2},{4,7},{5,4},{6,5},{7,6},{8,11},{9,8},{10,9... | collective-permute-start | bytes 2752520 | tf_op jit(solution)/shard_map/ppermute | solution.py:232
  93.7 73.6 %collective-permute-start.8 = (bf16[256,1792]{1,0:T(8,128)(2,1)}, bf16[256,1792]{1,0:T(8,128)(2,1)}, u32[]{:S(2)}, u32[]{:S(2)}) collective-permute-start(bf16[256,1792]{1,0:T(8,128)(2,1)} %reshape.73.refs_0_), channel_id=1, source_target_pairs={{0,2},{1,3},{2,0},{3,1},{4,6},{5,7},{6,4},{7,5},{8,10},{9,11},{10,... | collective-permute-start | bytes 2752520 | tf_op jit(solution)/shard_map/ppermute | solution.py:232
  97.6 46.6 %all-to-all-start.4 = ((bf16[64,4,1792]{2,1,0:T(4,128)(2,1)}), bf16[64,4,1792]{2,1,0:T(4,128)(2,1)}, u32[]{:S(2)}, u32[]{:S(2)}) async-start(bf16[64,4,1792]{2,1,0:T(4,128)(2,1)} %place_rows.5), calls=%async_computation.4 | async-start | bytes 1835008 | tf_op jit(solution)/shard_map/all_to_all | solution.py:256
  105.0 99.2 %all-gather.5.cloned.1.call-start = ((), (), s32[]{:S(2)}) async-start(), calls=%async_computation.7 | async-start | bytes 4587520 | tf_op jit(solution)/shard_map/all_gather | solution.py:261
  114.2 29.4 %collective-permute-start = (bf16[256,256]{1,0:T(8,128)(2,1)}, bf16[256,256]{1,0:T(8,128)(2,1)S(1)}, u32[]{:S(2)}, u32[]{:S(2)}) collective-permute-start(bf16[256,256]{1,0:T(8,128)(2,1)} %hidden_units.3.refs_0_.refs_6_), channel_id=1, source_target_pairs={{0,1},{1,2},{2,3},{3,0},{4,5},{5,6},{6,7},{7,4},{8,9},{9,10},{10,1... | collective-permute-start | bytes 393224 | tf_op jit(solution)/shard_map/ppermute | solution.py:232
  114.9 31.7 %collective-permute-start.1 = (bf16[256,256]{1,0:T(8,128)(2,1)}, bf16[256,256]{1,0:T(8,128)(2,1)S(1)}, u32[]{:S(2)}, u32[]{:S(2)}) collective-permute-start(bf16[256,256]{1,0:T(8,128)(2,1)} %hidden_units.3.refs_0_.refs_6_), channel_id=1, source_target_pairs={{0,3},{1,0},{2,1},{3,2},{4,7},{5,4},{6,5},{7,6},{8,11},{9,8},{10,9... | collective-permute-start | bytes 393224 | tf_op jit(solution)/shard_map/ppermute | solution.py:232
  143.6 5.5 %collective-permute-start.2 = (bf16[256,256]{1,0:T(8,128)(2,1)}, bf16[256,256]{1,0:T(8,128)(2,1)S(1)}, u32[]{:S(2)}, u32[]{:S(2)}) collective-permute-start(bf16[256,256]{1,0:T(8,128)(2,1)} %hidden_units.3.refs_0_.refs_6_), channel_id=1, source_target_pairs={{0,2},{1,3},{2,0},{3,1},{4,6},{5,7},{6,4},{7,5},{8,10},{9,11},{10,... | collective-permute-start | bytes 393224 | tf_op jit(solution)/shard_map/ppermute | solution.py:232
  154.6 38.5 %all-to-all-start.1 = ((bf16[64,4,1792]{2,1,0:T(4,128)(2,1)}), bf16[64,4,1792]{2,1,0:T(4,128)(2,1)}, u32[]{:S(2)}, u32[]{:S(2)}) async-start(bf16[64,4,1792]{2,1,0:T(4,128)(2,1)} %down.3), calls=%async_computation.1 | async-start | bytes 1835008 | tf_op jit(solution)/shard_map/all_to_all | solution.py:268
  173.7 10.3 %collective-permute-start.9 = (bf16[256,256]{1,0:T(8,128)(2,1)}, bf16[256,256]{1,0:T(8,128)(2,1)S(1)}, u32[]{:S(2)}, u32[]{:S(2)}) collective-permute-start(bf16[256,256]{1,0:T(8,128)(2,1)} %hidden_units.4.refs_0_.refs_3_), channel_id=1, source_target_pairs={{0,1},{1,2},{2,3},{3,0},{4,5},{5,6},{6,7},{7,4},{8,9},{9,10},{10,1... | collective-permute-start | bytes 393224 | tf_op jit(solution)/shard_map/ppermute | solution.py:232
  173.8 10.2 %collective-permute-start.10 = (bf16[256,256]{1,0:T(8,128)(2,1)}, bf16[256,256]{1,0:T(8,128)(2,1)S(1)}, u32[]{:S(2)}, u32[]{:S(2)}) collective-permute-start(bf16[256,256]{1,0:T(8,128)(2,1)} %hidden_units.4.refs_0_.refs_3_), channel_id=1, source_target_pairs={{0,3},{1,0},{2,1},{3,2},{4,7},{5,4},{6,5},{7,6},{8,11},{9,8},{10,9... | collective-permute-start | bytes 393224 | tf_op jit(solution)/shard_map/ppermute | solution.py:232
  176.5 11.1 %collective-permute-start.11 = (bf16[256,256]{1,0:T(8,128)(2,1)}, bf16[256,256]{1,0:T(8,128)(2,1)S(1)}, u32[]{:S(2)}, u32[]{:S(2)}) collective-permute-start(bf16[256,256]{1,0:T(8,128)(2,1)} %hidden_units.4.refs_0_.refs_3_), channel_id=1, source_target_pairs={{0,2},{1,3},{2,0},{3,1},{4,6},{5,7},{6,4},{7,5},{8,10},{9,11},{10,... | collective-permute-start | bytes 393224 | tf_op jit(solution)/shard_map/ppermute | solution.py:232
  193.2 36.4 %all-to-all-start.3 = ((bf16[64,4,1792]{2,1,0:T(4,128)(2,1)}), bf16[64,4,1792]{2,1,0:T(4,128)(2,1)S(1)}, u32[]{:S(2)}, u32[]{:S(2)}) async-start(bf16[64,4,1792]{2,1,0:T(4,128)(2,1)} %down.4), calls=%async_computation.3 | async-start | bytes 1835008 | tf_op jit(solution)/shard_map/all_to_all | solution.py:268
  210.6 27.3 %copy-start.4 = (s32[64,64]{0,1:T(8,128)S(1)}, s32[64,64]{0,1:T(8,128)}, u32[]{:S(2)}) copy-start(s32[64,64]{0,1:T(8,128)} %copy-done.3) | copy-start | bytes 49156
  210.6 6.1 %collective-permute-start.12 = (bf16[256,256]{1,0:T(8,128)(2,1)}, bf16[256,256]{1,0:T(8,128)(2,1)S(1)}, u32[]{:S(2)}, u32[]{:S(2)}) collective-permute-start(bf16[256,256]{1,0:T(8,128)(2,1)} %hidden_units.5.refs_0_), channel_id=1, source_target_pairs={{0,1},{1,2},{2,3},{3,0},{4,5},{5,6},{6,7},{7,4},{8,9},{9,10},{10,1... | collective-permute-start | bytes 393224 | tf_op jit(solution)/shard_map/ppermute | solution.py:232
  212.7 4.5 %collective-permute-start.13 = (bf16[256,256]{1,0:T(8,128)(2,1)}, bf16[256,256]{1,0:T(8,128)(2,1)S(1)}, u32[]{:S(2)}, u32[]{:S(2)}) collective-permute-start(bf16[256,256]{1,0:T(8,128)(2,1)} %hidden_units.5.refs_0_), channel_id=1, source_target_pairs={{0,3},{1,0},{2,1},{3,2},{4,7},{5,4},{6,5},{7,6},{8,11},{9,8},{10,9... | collective-permute-start | bytes 393224 | tf_op jit(solution)/shard_map/ppermute | solution.py:232
  213.7 7.3 %collective-permute-start.14 = (bf16[256,256]{1,0:T(8,128)(2,1)}, bf16[256,256]{1,0:T(8,128)(2,1)S(1)}, u32[]{:S(2)}, u32[]{:S(2)}) collective-permute-start(bf16[256,256]{1,0:T(8,128)(2,1)} %hidden_units.5.refs_0_), channel_id=1, source_target_pairs={{0,2},{1,3},{2,0},{3,1},{4,6},{5,7},{6,4},{7,5},{8,10},{9,11},{10,... | collective-permute-start | bytes 393224 | tf_op jit(solution)/shard_map/ppermute | solution.py:232
  229.6 33.2 %all-to-all-start.5 = ((bf16[64,4,1792]{2,1,0:T(4,128)(2,1)}), bf16[64,4,1792]{2,1,0:T(4,128)(2,1)S(1)}, u32[]{:S(2)}, u32[]{:S(2)}) async-start(bf16[64,4,1792]{2,1,0:T(4,128)(2,1)} %down.5), calls=%async_computation.5 | async-start | bytes 1835008 | tf_op jit(solution)/shard_map/all_to_all | solution.py:268
  (20 other events, 180.6 us)
Sparse Core Ops, SparseCore 0:
  54.6 53.9 all-gather.2
  146.7 53.5 all-gather.4

commit v3 on v2

--- a/solution.py
+++ b/solution.py
@@ -34,18 +34,21 @@
 
 
 def hidden_kernel(gathered, parts, me_ref, *refs):
-    arrays = 1 if gathered else parts
+    arrays = 1 if gathered else parts + 1
     xs, (gate_ref, up_ref) = refs[:arrays], refs[arrays:arrays + 2]
     out_ref, x_buffer, gate_buffer, up_buffer, gate_sum, up_sum, arrivals = refs[-7:]
     copies = []
     for number, step in enumerate(range(parts) if gathered else STEPS):
         part = step if gathered else lax.rem(me_ref[0] + step, parts)
-        x_part = xs[0].at[step] if gathered else xs[number]
-        pairs = (
-            (x_part, x_buffer.at[number]),
-            (gate_ref.at[part], gate_buffer.at[number]),
-            (up_ref.at[part], up_buffer.at[number]),
-        )
+        pairs = [(gate_ref.at[part], gate_buffer.at[number]), (up_ref.at[part], up_buffer.at[number])]
+        if gathered:
+            pairs.append((xs[0].at[step], x_buffer.at[number]))
+        elif number < parts - 1:
+            pairs.append((xs[number], x_buffer.at[number]))
+        else:
+            half = x_buffer.shape[1] // 2
+            pairs.append((xs[number], x_buffer.at[number, pl.ds(0, half)]))
+            pairs.append((xs[number + 1], x_buffer.at[number, pl.ds(half, half)]))
         copies.append(
             [pltpu.make_async_copy(a, b, arrivals.at[number, i]) for i, (a, b) in enumerate(pairs)]
         )
@@ -84,7 +87,7 @@
                 pltpu.VMEM((parts, width, hidden), jnp.bfloat16),
                 pltpu.VMEM((rows, hidden), jnp.float32),
                 pltpu.VMEM((rows, hidden), jnp.float32),
-                pltpu.SemaphoreType.DMA((parts, 3)),
+                pltpu.SemaphoreType.DMA((parts, 4)),
             ],
         ),
         out_shape=jax.ShapeDtypeStruct((rows, hidden), jnp.bfloat16),
@@ -234,6 +237,11 @@
     def send_all(array):
         return [send(array, step) for step in SENDS]
 
+    def ring(rows):
+        half = rows.shape[0] // 2
+        left, right = send(rows, 1), send(rows, -1)
+        return [left, right, send(left[:half], 1), send(right[half:], -1)]
+
     slices = [
         lax.dynamic_slice_in_dim(w_down, (place + step) % parts * width, width, axis=1) for step in SENDS
     ]
@@ -247,23 +255,33 @@
     slot = jnp.dot(earlier, chosen.astype(jnp.bfloat16), preferred_element_type=jnp.float32).astype(jnp.int32)
     slot = jnp.where(chosen, slot, CAP)
 
-    places, gathered = [], []
-    for number, (first, count, by_permutes) in enumerate(CHUNKS):
+    places = []
+    for first, count, _ in CHUNKS:
         here = slot[:, :, None] == first + jnp.arange(count, dtype=jnp.int32)
         places.append(here.reshape(row_count, experts * count))
-        after = slices if number == 0 else [before] if number == 1 else [before, waited]
-        outgoing = place_rows(places[-1].astype(jnp.bfloat16), hidden_rows, experts, after, 1)
-        rows = lax.all_to_all(outgoing, "ep", split_axis=0, concat_axis=0, tiled=True)
-        if number == 0:
-            waited = wait_for([*pieces, rows], WAIT_TOLD)
-        before = rows
+
+    def outgoing(number, after):
+        return place_rows(places[number].astype(jnp.bfloat16), hidden_rows, experts, after, 1)
+
+    gathered = []
+    leaving = [outgoing(0, []), None, None]
+    leaving[2] = outgoing(2, leaving[:1])
+    for number, (first, count, by_permutes) in enumerate(CHUNKS):
+        if number == 1:
+            leaving[1] = outgoing(1, [rows, leaving[2], wait_for(pieces, WAIT_TOLD)])
+        rows = lax.all_to_all(leaving[number], "ep", split_axis=0, concat_axis=0, tiled=True)
         rows = rows.reshape(experts * count, width)
-        gathered.append([rows] + send_all(rows) if by_permutes else lax.all_gather(rows, "tp"))
+        if number == 1:
+            waited = wait_for([rows], WAIT_TOLD)
+        if by_permutes:
+            gathered.append([rows] + ring(rows))
+        else:
+            gathered.append([lax.all_gather(rows, "tp", tiled=True).reshape(parts, *rows.shape)])
 
     mixed = jnp.zeros((row_count, width), jnp.float32)
     for number, ((first, count, by_permutes), spot, x, told) in enumerate(zip(CHUNKS, places, gathered, TOLD)):
-        after = [activated] if number else []
-        activated = hidden_units(me, x if by_permutes else [x], w_gate, w_up, after, told)
+        after = [activated] if number else [waited]
+        activated = hidden_units(me, x, w_gate, w_up, after, told)
         outputs = down(me, [activated] + send_all(activated), w_down, pieces, experts)
         returned = lax.all_to_all(outputs, "ep", split_axis=0, concat_axis=0, tiled=True)
         returned = returned.reshape(experts * count, width)

time: 272 us -> 290 us (1.066)
  waiting for transfers between devices: 119 us -> 126 us
  starting transfers between devices: 77.9 us -> 82.1 us
  local copies, waits for them, and re-layouts: 13.1 us -> 17 us
    ppermute x15 -> x16, waiting for transfers between devices: 57 us -> 73.4 us  [send(): lax.ppermute(array, 'tp', [(i, (i + step) % parts) for i in range(parts)])]
    all_to_all x3, waiting for transfers between devices: 33.9 us -> 25.9 us  [on_device(): lax.all_to_all(leaving[number], 'ep', split_axis=0, concat_axis=0, tiled=...]
    all_to_all x3, starting transfers between devices: 27.3 us -> 31.8 us  [on_device(): lax.all_to_all(leaving[number], 'ep', split_axis=0, concat_axis=0, tiled=...]
    another operation x2 -> x0, local copies, waits for them, and re-layouts: 3.64 us -> none  [on_device(): lax.all_gather(rows, 'tp')]
    slice x0 -> x2, local copies, waits for them, and re-layouts: none -> 3.62 us  [ring(): return [left, right, send(left[:half], 1), send(right[half:], -1)]]
    all_gather x2, waiting for transfers between devices: 3.61 us -> 0.02 us  [on_device(): lax.all_gather(rows, 'tp', tiled=True).reshape(parts, *rows.shape)]
    reshape x1 -> x3, local copies, waits for them, and re-layouts: 2.41 us -> 5.98 us  [on_device(): rows = rows.reshape(experts * count, width)]
    ppermute x15 -> x16, starting transfers between devices: 18.9 us -> 19.9 us  [send(): lax.ppermute(array, 'tp', [(i, (i + step) % parts) for i in range(parts)])]
  transfers between devices with their start and end apart: 23 -> 24, of which waited for: 13 -> 12; matrix products, arithmetic and copies ran while one was open for 4% -> 5% of each run, Pallas kernels for 14% -> 14%
where the time goes in v3:
time: 290 us; the launch traced here: 288 us
  waiting for transfers between devices  126 us (43%)
  starting transfers between devices  82.1 us (28%)
  Pallas kernels  42.9 us (15%)
  local copies, waits for them, and re-layouts  17 us (6%)
  between operations  13.8 us (5%)
  matrix products  5.12 us (2%)
    ppermute x16, waiting for transfers between devices, send(): lax.ppermute(array, 'tp', [(i, (i + step) % parts) for i in range(parts)])  73.4 us
    all_to_all x3, starting transfers between devices, on_device(): lax.all_to_all(leaving[number], 'ep', split_axis=0, concat_axis=0, tiled=...  31.8 us
    all_to_all x3, starting transfers between devices, on_device(): lax.all_to_all(outputs, 'ep', split_axis=0, concat_axis=0, tiled=True)  30.4 us
    all_to_all x3, waiting for transfers between devices, on_device(): lax.all_to_all(leaving[number], 'ep', split_axis=0, concat_axis=0, tiled=...  25.9 us
    all_to_all x3, waiting for transfers between devices, on_device(): lax.all_to_all(outputs, 'ep', split_axis=0, concat_axis=0, tiled=True)  25.8 us
    ppermute x16, starting transfers between devices, send(): lax.ppermute(array, 'tp', [(i, (i + step) % parts) for i in range(parts)])  19.9 us
    pallas_call x3, Pallas kernels, hidden_units(): pl.pallas_call(functools.partial(hidden_kernel, gathered, parts), grid_sp...  18.9 us
    pallas_call x3, Pallas kernels, down(): pl.pallas_call(functools.partial(down_kernel, parts), grid_spec=pltpu.Pre...  14.6 us
  transfers between devices with their start and end apart: 24, of which 12 were waited for; matrix products, arithmetic and copies ran while one was open for 5% of the time, Pallas kernels for 14%

profile of v3, /device:TPU:1, one launch (start us, length us, event | category | flops | bytes accessed | tf_op | source)
XLA Modules:
  0.0 288.0 jit_solution(5940721042439238336)
XLA Ops:
  6.5 3.4 %dynamic-slice_bitcast_fusion = (bf16[256,1792]{1,0:T(8,128)(2,1)}, bf16[256,1792]{1,0:T(8,128)(2,1)}, bf16[256,1792]{1,0:T(8,128)(2,1)}) fusion(bf16[1,256,7168]{2,1,0:T(8,128)(2,1)} %param.11, s32[]{:T(128)S(6)} %select_n.61, s32[]{:T(128)S(6)} %select_n.59, s32[]{:T(128)S(6)} %select_n.57), kind=kLoop, calls=%fused_computation.14 | loop fusion | bytes 5505036 | tf_op jit(solution)/shard_map/dynamic_slice | solution.py:246
  19.1 13.3 %all-to-all-start = ((bf16[64,4,1792]{2,1,0:T(4,128)(2,1)}), bf16[64,4,1792]{2,1,0:T(4,128)(2,1)}, u32[]{:S(2)}, u32[]{:S(2)}) async-start(bf16[64,4,1792]{2,1,0:T(4,128)(2,1)} %place_rows.3.rest_0_), calls=%async_computation | async-start | bytes 1835008 | tf_op jit(solution)/shard_map/all_to_all | solution.py:272
  34.8 19.3 %collective-permute-done.2.refs_2_.refs_7_ = bf16[256,1792]{1,0:T(8,128)(2,1)S(1)} collective-permute-done((bf16[256,1792]{1,0:T(8,128)(2,1)}, bf16[256,1792]{1,0:T(8,128)(2,1)S(1)}, u32[]{:S(2)}, u32[]{:S(2)}) %collective-permute-start.2) | collective-permute-done | bytes 917536 | tf_op jit(solution)/shard_map/ppermute | solution.py:235
  62.4 11.8 %all-to-all-start.1 = ((bf16[64,4,1792]{2,1,0:T(4,128)(2,1)}), bf16[64,4,1792]{2,1,0:T(4,128)(2,1)S(1)}, u32[]{:S(2)}, u32[]{:S(2)}) async-start(bf16[64,4,1792]{2,1,0:T(4,128)(2,1)} %place_rows.5), calls=%async_computation.1 | async-start | bytes 1835008 | tf_op jit(solution)/shard_map/all_to_all | solution.py:272
  74.9 24.6 %all-to-all-done.1 = bf16[64,4,1792]{2,1,0:T(4,128)(2,1)S(1)} async-done(((bf16[64,4,1792]{2,1,0:T(4,128)(2,1)}), bf16[64,4,1792]{2,1,0:T(4,128)(2,1)S(1)}, u32[]{:S(2)}, u32[]{:S(2)}) %all-to-all-start.1) | async-done | bytes 917536 | tf_op jit(solution)/shard_map/all_to_all | solution.py:272
  99.5 6.6 %all-to-all-start.4 = ((bf16[64,4,1792]{2,1,0:T(4,128)(2,1)}), bf16[64,4,1792]{2,1,0:T(4,128)(2,1)}, u32[]{:S(2)}, u32[]{:S(2)}) async-start(bf16[64,4,1792]{2,1,0:T(4,128)(2,1)} %place_rows.4.rest_1_), calls=%async_computation.4 | async-start | bytes 1835008 | tf_op jit(solution)/shard_map/all_to_all | solution.py:272
  111.3 32.1 %collective-permute-done.6.refs_1_ = bf16[256,1792]{1,0:T(8,128)(2,1)} collective-permute-done((bf16[256,1792]{1,0:T(8,128)(2,1)}, bf16[256,1792]{1,0:T(8,128)(2,1)}, u32[]{:S(2)}, u32[]{:S(2)}) %collective-permute-start.6) | collective-permute-done | bytes 917536 | tf_op jit(solution)/shard_map/ppermute | solution.py:235
  147.1 2.7 collective-permute-start.9
  149.8 6.3 %hidden_units.3.refs_0_.refs_7_ = bf16[256,256]{1,0:T(8,128)(2,1)} custom-call(s32[1]{0:T(128)} %bitcast.me_ref, bf16[4,256,1792]{2,1,0:T(8,128)(2,1)} %bitcast.49, bf16[4,1792,256]{2,1,0:T(8,128)(2,1)} %bitcast.41, bf16[4,1792,256]{2,1,0:T(8,128)(2,1)} %bitcast.44, bf16[16,128]{1,0:T(8,128)(2,1)} %wait_for.3.refs_3_), custom_call_target="tpu_custom_call" | custom-call | flops 187904819200 | bytes 11141120 | tf_op jit(solution)/shard_map/hidden_units/pallas_call | solution.py:77
  161.4 3.7 %collective-permute-done.4.refs_2_ = bf16[256,256]{1,0:T(8,128)(2,1)S(1)} collective-permute-done((bf16[256,256]{1,0:T(8,128)(2,1)}, bf16[256,256]{1,0:T(8,128)(2,1)S(1)}, u32[]{:S(2)}, u32[]{:S(2)}) %collective-permute-start.4) | collective-permute-done | bytes 131104 | tf_op jit(solution)/shard_map/ppermute | solution.py:235
  165.8 4.9 %down.3 = bf16[64,4,1792]{2,1,0:T(4,128)(2,1)} custom-call(s32[1]{0:T(128)} %bitcast.me_ref, bf16[256,256]{1,0:T(8,128)(2,1)} %hidden_units.3.refs_0_.refs_7_, bf16[256,256]{1,0:T(8,128)(2,1)} %copy-done.7, bf16[256,256]{1,0:T(8,128)(2,1)} %copy-done.8, bf16[256,256]{1,0:T(8,128)(2,1)} %copy-done.9, bf16[256,7168]{1,0:T(8,128)(2,1)} %bitcast.38, ...), custom_call_target="tpu_custom_call" | custom-call | flops 939524096 | bytes 5111808 | tf_op jit(solution)/shard_map/down/pallas_call | solution.py:141
  170.7 12.4 %all-to-all-start.2 = ((bf16[64,4,1792]{2,1,0:T(4,128)(2,1)}), bf16[64,4,1792]{2,1,0:T(4,128)(2,1)}, u32[]{:S(2)}, u32[]{:S(2)}) async-start(bf16[64,4,1792]{2,1,0:T(4,128)(2,1)} %down.3), calls=%async_computation.2 | async-start | bytes 1835008 | tf_op jit(solution)/shard_map/all_to_all | solution.py:286
  183.1 6.4 %hidden_units.4.refs_0_.refs_3_ = bf16[256,256]{1,0:T(8,128)(2,1)} custom-call(s32[1]{0:T(128)} %bitcast.me_ref, bf16[256,1792]{1,0:T(8,128)(2,1)} %reshape.87.refs_0_, bf16[256,1792]{1,0:T(8,128)(2,1)} %collective-permute-done.6.refs_1_, bf16[256,1792]{1,0:T(8,128)(2,1)} %collective-permute-done.7.refs_2_, ...), custom_call_target="tpu_custom_call" | custom-call | flops 187904819200 | bytes 11141120 | tf_op jit(solution)/shard_map/hidden_units/pallas_call | solution.py:77
  193.2 5.8 %collective-permute-done.10.refs_1_ = bf16[256,256]{1,0:T(8,128)(2,1)S(1)} collective-permute-done((bf16[256,256]{1,0:T(8,128)(2,1)}, bf16[256,256]{1,0:T(8,128)(2,1)S(1)}, u32[]{:S(2)}, u32[]{:S(2)}) %collective-permute-start.10) | collective-permute-done | bytes 131104 | tf_op jit(solution)/shard_map/ppermute | solution.py:235
  199.1 6.6 %collective-permute-done.12.refs_3_ = bf16[256,256]{1,0:T(8,128)(2,1)S(1)} collective-permute-done((bf16[256,256]{1,0:T(8,128)(2,1)}, bf16[256,256]{1,0:T(8,128)(2,1)S(1)}, u32[]{:S(2)}, u32[]{:S(2)}) %collective-permute-start.12) | collective-permute-done | bytes 131104 | tf_op jit(solution)/shard_map/ppermute | solution.py:235
  206.3 4.9 %down.4 = bf16[64,4,1792]{2,1,0:T(4,128)(2,1)} custom-call(s32[1]{0:T(128)} %bitcast.me_ref, bf16[256,256]{1,0:T(8,128)(2,1)} %hidden_units.4.refs_0_.refs_3_, bf16[256,256]{1,0:T(8,128)(2,1)} %copy-done.12, bf16[256,256]{1,0:T(8,128)(2,1)} %copy-done.14, bf16[256,256]{1,0:T(8,128)(2,1)} %copy-done.15, bf16[256,7168]{1,0:T(8,128)(2,1)} %bitcast.39, ...), custom_call_target="tpu_custom_call" | custom-call | flops 939524096 | bytes 5111808 | tf_op jit(solution)/shard_map/down/pallas_call | solution.py:141
  211.2 11.1 %all-to-all-start.3 = ((bf16[64,4,1792]{2,1,0:T(4,128)(2,1)}), bf16[64,4,1792]{2,1,0:T(4,128)(2,1)S(1)}, u32[]{:S(2)}, u32[]{:S(2)}) async-start(bf16[64,4,1792]{2,1,0:T(4,128)(2,1)} %down.4), calls=%async_computation.3 | async-start | bytes 1835008 | tf_op jit(solution)/shard_map/all_to_all | solution.py:286
  222.4 6.3 %hidden_units.5.refs_0_ = bf16[256,256]{1,0:T(8,128)(2,1)} custom-call(s32[1]{0:T(128)} %bitcast.me_ref, bf16[4,256,1792]{2,1,0:T(8,128)(2,1)} %bitcast.47, bf16[4,1792,256]{2,1,0:T(8,128)(2,1)} %bitcast.43, bf16[4,1792,256]{2,1,0:T(8,128)(2,1)} %bitcast.46, bf16[256,256]{1,0:T(8,128)(2,1)} %hidden_units.4.refs_0_.refs_3_), custom_call_target="tpu_custom_call" | custom-call | flops 1879048192 | bytes 11141120 | tf_op jit(solution)/shard_map/hidden_units/pallas_call | solution.py:77
  231.7 2.9 collective-permute-done.13.refs_1_
  234.6 2.7 collective-permute-done.15.refs_3_
  238.0 4.8 %down.5 = bf16[64,4,1792]{2,1,0:T(4,128)(2,1)} custom-call(s32[1]{0:T(128)} %bitcast.me_ref, bf16[256,256]{1,0:T(8,128)(2,1)} %hidden_units.5.refs_0_, bf16[256,256]{1,0:T(8,128)(2,1)} %copy-done.10, bf16[256,256]{1,0:T(8,128)(2,1)} %copy-done.11, bf16[256,256]{1,0:T(8,128)(2,1)} %copy-done.13, bf16[256,7168]{1,0:T(8,128)(2,1)} %bitcast.40, ...), custom_call_target="tpu_custom_call" | custom-call | flops 939524096 | bytes 5111808 | tf_op jit(solution)/shard_map/down/pallas_call | solution.py:141
  242.8 4.8 %all-to-all-done.3 = bf16[64,4,1792]{2,1,0:T(4,128)(2,1)S(1)} async-done(((bf16[64,4,1792]{2,1,0:T(4,128)(2,1)}), bf16[64,4,1792]{2,1,0:T(4,128)(2,1)S(1)}, u32[]{:S(2)}, u32[]{:S(2)}) %all-to-all-start.3) | async-done | bytes 917536 | tf_op jit(solution)/shard_map/all_to_all | solution.py:286
  247.6 6.9 %all-to-all-start.5 = ((bf16[64,4,1792]{2,1,0:T(4,128)(2,1)}), bf16[64,4,1792]{2,1,0:T(4,128)(2,1)S(1)}, u32[]{:S(2)}, u32[]{:S(2)}) async-start(bf16[64,4,1792]{2,1,0:T(4,128)(2,1)} %down.5), calls=%async_computation.5 | async-start | bytes 1835008 | tf_op jit(solution)/shard_map/all_to_all | solution.py:286
  258.9 21.0 %all-to-all-done.5 = bf16[64,4,1792]{2,1,0:T(4,128)(2,1)S(1)} async-done(((bf16[64,4,1792]{2,1,0:T(4,128)(2,1)}), bf16[64,4,1792]{2,1,0:T(4,128)(2,1)S(1)}, u32[]{:S(2)}, u32[]{:S(2)}) %all-to-all-start.5) | async-done | bytes 917536 | tf_op jit(solution)/shard_map/all_to_all | solution.py:286
  (115 shorter events, 48.9 us)
Async XLA Ops:
  9.9 24.8 %collective-permute-start = (bf16[256,1792]{1,0:T(8,128)(2,1)}, bf16[256,1792]{1,0:T(8,128)(2,1)S(1)}, u32[]{:S(2)}, u32[]{:S(2)}) collective-permute-start(bf16[256,1792]{1,0:T(8,128)(2,1)} %get-tuple-element.7), channel_id=1, source_target_pairs={{0,1},{1,2},{2,3},{3,0},{4,5},{5,6},{6,7},{7,4},{8,9},{9,10},{10,1... | collective-permute-start | bytes 2752520 | tf_op jit(solution)/shard_map/ppermute | solution.py:235
  12.0 22.8 %collective-permute-start.1 = (bf16[256,1792]{1,0:T(8,128)(2,1)}, bf16[256,1792]{1,0:T(8,128)(2,1)S(1)}, u32[]{:S(2)}, u32[]{:S(2)}) collective-permute-start(bf16[256,1792]{1,0:T(8,128)(2,1)} %get-tuple-element.6), channel_id=1, source_target_pairs={{0,3},{1,0},{2,1},{3,2},{4,7},{5,4},{6,5},{7,6},{8,11},{9,8},{10,9... | collective-permute-start | bytes 2752520 | tf_op jit(solution)/shard_map/ppermute | solution.py:235
  13.2 40.9 %collective-permute-start.2 = (bf16[256,1792]{1,0:T(8,128)(2,1)}, bf16[256,1792]{1,0:T(8,128)(2,1)S(1)}, u32[]{:S(2)}, u32[]{:S(2)}) collective-permute-start(bf16[256,1792]{1,0:T(8,128)(2,1)} %get-tuple-element.5), channel_id=1, source_target_pairs={{0,2},{1,3},{2,0},{3,1},{4,6},{5,7},{6,4},{7,5},{8,10},{9,11},{10,... | collective-permute-start | bytes 2752520 | tf_op jit(solution)/shard_map/ppermute | solution.py:235
  19.1 38.6 %all-to-all-start = ((bf16[64,4,1792]{2,1,0:T(4,128)(2,1)}), bf16[64,4,1792]{2,1,0:T(4,128)(2,1)}, u32[]{:S(2)}, u32[]{:S(2)}) async-start(bf16[64,4,1792]{2,1,0:T(4,128)(2,1)} %place_rows.3.rest_0_), calls=%async_computation | async-start | bytes 1835008 | tf_op jit(solution)/shard_map/all_to_all | solution.py:272
  62.4 37.1 %all-to-all-start.1 = ((bf16[64,4,1792]{2,1,0:T(4,128)(2,1)}), bf16[64,4,1792]{2,1,0:T(4,128)(2,1)S(1)}, u32[]{:S(2)}, u32[]{:S(2)}) async-start(bf16[64,4,1792]{2,1,0:T(4,128)(2,1)} %place_rows.5), calls=%async_computation.1 | async-start | bytes 1835008 | tf_op jit(solution)/shard_map/all_to_all | solution.py:272
  74.2 75.6 %all-gather.3.cloned.1.call-start = ((), (), s32[]{:S(2)}) async-start(), calls=%async_computation.6 | async-start | bytes 4587520 | tf_op jit(solution)/shard_map/all_gather | solution.py:279
  99.5 59.4 %all-to-all-start.4 = ((bf16[64,4,1792]{2,1,0:T(4,128)(2,1)}), bf16[64,4,1792]{2,1,0:T(4,128)(2,1)}, u32[]{:S(2)}, u32[]{:S(2)}) async-start(bf16[64,4,1792]{2,1,0:T(4,128)(2,1)} %place_rows.4.rest_1_), calls=%async_computation.4 | async-start | bytes 1835008 | tf_op jit(solution)/shard_map/all_to_all | solution.py:272
  106.1 116.3 %all-gather.5.cloned.1.call-start = ((), (), s32[]{:S(2)}) async-start(), calls=%async_computation.7 | async-start | bytes 4587520 | tf_op jit(solution)/shard_map/all_gather | solution.py:279
  107.4 36.1 %collective-permute-start.6 = (bf16[256,1792]{1,0:T(8,128)(2,1)}, bf16[256,1792]{1,0:T(8,128)(2,1)}, u32[]{:S(2)}, u32[]{:S(2)}) collective-permute-start(bf16[256,1792]{1,0:T(8,128)(2,1)} %reshape.87.refs_0_), channel_id=1, source_target_pairs={{0,1},{1,2},{2,3},{3,0},{4,5},{5,6},{6,7},{7,4},{8,9},{9,10},{10,1... | collective-permute-start | bytes 2752520 | tf_op jit(solution)/shard_map/ppermute | solution.py:235
  108.2 37.1 %collective-permute-start.7 = (bf16[256,1792]{1,0:T(8,128)(2,1)}, bf16[256,1792]{1,0:T(8,128)(2,1)}, u32[]{:S(2)}, u32[]{:S(2)}) collective-permute-start(bf16[256,1792]{1,0:T(8,128)(2,1)} %reshape.87.refs_0_), channel_id=1, source_target_pairs={{0,3},{1,0},{2,1},{3,2},{4,7},{5,4},{6,5},{7,6},{8,11},{9,8},{10,9... | collective-permute-start | bytes 2752520 | tf_op jit(solution)/shard_map/ppermute | solution.py:235
  145.3 37.8 %collective-permute-start.8 = (bf16[128,1792]{1,0:T(8,128)(2,1)}, bf16[128,1792]{1,0:T(8,128)(2,1)}, u32[]{:S(2)}, u32[]{:S(2)}) collective-permute-start(bf16[128,1792]{1,0:T(8,128)(2,1)} %slice.8), channel_id=1, source_target_pairs={{0,1},{1,2},{2,3},{3,0},{4,5},{5,6},{6,7},{7,4},{8,9},{9,10},{10,1... | collective-permute-start | bytes 1376264 | tf_op jit(solution)/shard_map/ppermute | solution.py:235
  147.1 36.0 %collective-permute-start.9 = (bf16[128,1792]{1,0:T(8,128)(2,1)}, bf16[128,1792]{1,0:T(8,128)(2,1)}, u32[]{:S(2)}, u32[]{:S(2)}) collective-permute-start(bf16[128,1792]{1,0:T(8,128)(2,1)} %slice.9), channel_id=1, source_target_pairs={{0,3},{1,0},{2,1},{3,2},{4,7},{5,4},{6,5},{7,6},{8,11},{9,8},{10,9... | collective-permute-start | bytes 1376264 | tf_op jit(solution)/shard_map/ppermute | solution.py:235
  156.1 5.3 %collective-permute-start.3 = (bf16[256,256]{1,0:T(8,128)(2,1)}, bf16[256,256]{1,0:T(8,128)(2,1)S(1)}, u32[]{:S(2)}, u32[]{:S(2)}) collective-permute-start(bf16[256,256]{1,0:T(8,128)(2,1)} %hidden_units.3.refs_0_.refs_7_), channel_id=1, source_target_pairs={{0,1},{1,2},{2,3},{3,0},{4,5},{5,6},{6,7},{7,4},{8,9},{9,10},{10,1... | collective-permute-start | bytes 393224 | tf_op jit(solution)/shard_map/ppermute | solution.py:235
  156.2 9.0 %collective-permute-start.4 = (bf16[256,256]{1,0:T(8,128)(2,1)}, bf16[256,256]{1,0:T(8,128)(2,1)S(1)}, u32[]{:S(2)}, u32[]{:S(2)}) collective-permute-start(bf16[256,256]{1,0:T(8,128)(2,1)} %hidden_units.3.refs_0_.refs_7_), channel_id=1, source_target_pairs={{0,3},{1,0},{2,1},{3,2},{4,7},{5,4},{6,5},{7,6},{8,11},{9,8},{10,9... | collective-permute-start | bytes 393224 | tf_op jit(solution)/shard_map/ppermute | solution.py:235
  158.8 6.3 %collective-permute-start.5 = (bf16[256,256]{1,0:T(8,128)(2,1)}, bf16[256,256]{1,0:T(8,128)(2,1)S(1)}, u32[]{:S(2)}, u32[]{:S(2)}) collective-permute-start(bf16[256,256]{1,0:T(8,128)(2,1)} %hidden_units.3.refs_0_.refs_7_), channel_id=1, source_target_pairs={{0,2},{1,3},{2,0},{3,1},{4,6},{5,7},{6,4},{7,5},{8,10},{9,11},{10,... | collective-permute-start | bytes 393224 | tf_op jit(solution)/shard_map/ppermute | solution.py:235
  170.7 40.5 %all-to-all-start.2 = ((bf16[64,4,1792]{2,1,0:T(4,128)(2,1)}), bf16[64,4,1792]{2,1,0:T(4,128)(2,1)}, u32[]{:S(2)}, u32[]{:S(2)}) async-start(bf16[64,4,1792]{2,1,0:T(4,128)(2,1)} %down.3), calls=%async_computation.2 | async-start | bytes 1835008 | tf_op jit(solution)/shard_map/all_to_all | solution.py:286
  189.5 9.6 %collective-permute-start.10 = (bf16[256,256]{1,0:T(8,128)(2,1)}, bf16[256,256]{1,0:T(8,128)(2,1)S(1)}, u32[]{:S(2)}, u32[]{:S(2)}) collective-permute-start(bf16[256,256]{1,0:T(8,128)(2,1)} %hidden_units.4.refs_0_.refs_3_), channel_id=1, source_target_pairs={{0,1},{1,2},{2,3},{3,0},{4,5},{5,6},{6,7},{7,4},{8,9},{9,10},{10,1... | collective-permute-start | bytes 393224 | tf_op jit(solution)/shard_map/ppermute | solution.py:235
  189.9 9.2 %collective-permute-start.11 = (bf16[256,256]{1,0:T(8,128)(2,1)}, bf16[256,256]{1,0:T(8,128)(2,1)S(1)}, u32[]{:S(2)}, u32[]{:S(2)}) collective-permute-start(bf16[256,256]{1,0:T(8,128)(2,1)} %hidden_units.4.refs_0_.refs_3_), channel_id=1, source_target_pairs={{0,3},{1,0},{2,1},{3,2},{4,7},{5,4},{6,5},{7,6},{8,11},{9,8},{10,9... | collective-permute-start | bytes 393224 | tf_op jit(solution)/shard_map/ppermute | solution.py:235
  192.2 13.4 %collective-permute-start.12 = (bf16[256,256]{1,0:T(8,128)(2,1)}, bf16[256,256]{1,0:T(8,128)(2,1)S(1)}, u32[]{:S(2)}, u32[]{:S(2)}) collective-permute-start(bf16[256,256]{1,0:T(8,128)(2,1)} %hidden_units.4.refs_0_.refs_3_), channel_id=1, source_target_pairs={{0,2},{1,3},{2,0},{3,1},{4,6},{5,7},{6,4},{7,5},{8,10},{9,11},{10,... | collective-permute-start | bytes 393224 | tf_op jit(solution)/shard_map/ppermute | solution.py:235
  211.2 36.4 %all-to-all-start.3 = ((bf16[64,4,1792]{2,1,0:T(4,128)(2,1)}), bf16[64,4,1792]{2,1,0:T(4,128)(2,1)S(1)}, u32[]{:S(2)}, u32[]{:S(2)}) async-start(bf16[64,4,1792]{2,1,0:T(4,128)(2,1)} %down.4), calls=%async_computation.3 | async-start | bytes 1835008 | tf_op jit(solution)/shard_map/all_to_all | solution.py:286
  228.7 5.9 %collective-permute-start.13 = (bf16[256,256]{1,0:T(8,128)(2,1)}, bf16[256,256]{1,0:T(8,128)(2,1)S(1)}, u32[]{:S(2)}, u32[]{:S(2)}) collective-permute-start(bf16[256,256]{1,0:T(8,128)(2,1)} %hidden_units.5.refs_0_), channel_id=1, source_target_pairs={{0,1},{1,2},{2,3},{3,0},{4,5},{5,6},{6,7},{7,4},{8,9},{9,10},{10,1... | collective-permute-start | bytes 393224 | tf_op jit(solution)/shard_map/ppermute | solution.py:235
  229.8 4.8 %collective-permute-start.14 = (bf16[256,256]{1,0:T(8,128)(2,1)}, bf16[256,256]{1,0:T(8,128)(2,1)S(1)}, u32[]{:S(2)}, u32[]{:S(2)}) collective-permute-start(bf16[256,256]{1,0:T(8,128)(2,1)} %hidden_units.5.refs_0_), channel_id=1, source_target_pairs={{0,3},{1,0},{2,1},{3,2},{4,7},{5,4},{6,5},{7,6},{8,11},{9,8},{10,9... | collective-permute-start | bytes 393224 | tf_op jit(solution)/shard_map/ppermute | solution.py:235
  231.5 5.8 %collective-permute-start.15 = (bf16[256,256]{1,0:T(8,128)(2,1)}, bf16[256,256]{1,0:T(8,128)(2,1)S(1)}, u32[]{:S(2)}, u32[]{:S(2)}) collective-permute-start(bf16[256,256]{1,0:T(8,128)(2,1)} %hidden_units.5.refs_0_), channel_id=1, source_target_pairs={{0,2},{1,3},{2,0},{3,1},{4,6},{5,7},{6,4},{7,5},{8,10},{9,11},{10,... | collective-permute-start | bytes 393224 | tf_op jit(solution)/shard_map/ppermute | solution.py:235
  247.6 32.2 %all-to-all-start.5 = ((bf16[64,4,1792]{2,1,0:T(4,128)(2,1)}), bf16[64,4,1792]{2,1,0:T(4,128)(2,1)S(1)}, u32[]{:S(2)}, u32[]{:S(2)}) async-start(bf16[64,4,1792]{2,1,0:T(4,128)(2,1)} %down.5), calls=%async_computation.5 | async-start | bytes 1835008 | tf_op jit(solution)/shard_map/all_to_all | solution.py:286
  (22 other events, 326.4 us)
Sparse Core Ops, SparseCore 0:
  76.8 59.2 all-gather.2
  161.4 55.0 all-gather.4

commit v4 on v3

--- a/solution.py
+++ b/solution.py
@@ -8,7 +8,7 @@
 from jax.sharding import PartitionSpec as P
 
 CAP = 12
-CHUNKS = ((0, 4, False), (4, 4, True), (8, 4, False))
+CHUNKS = ((0, 4, True), (4, 4, False), (8, 4, False))
 SENDS = (1, 3, 2)
 STEPS = (0, 3, 1, 2)
 TILES = 2

time: 290 us -> 279 us (0.962)
  waiting for transfers between devices: 126 us -> 112 us
  starting transfers between devices: 82.1 us -> 87.5 us
    all_gather x2, waiting for transfers between devices: 0.02 us -> 25.1 us  [on_device(): lax.all_gather(rows, 'tp', tiled=True).reshape(parts, *rows.shape)]
    ppermute x16, waiting for transfers between devices: 73.4 us -> 50.7 us  [send(): lax.ppermute(array, 'tp', [(i, (i + step) % parts) for i in range(parts)])]
    all_to_all x3, waiting for transfers between devices: 25.9 us -> 14.8 us  [on_device(): lax.all_to_all(leaving[number], 'ep', split_axis=0, concat_axis=0, tiled=...]
    all_to_all x3, starting transfers between devices: 31.8 us -> 37.1 us  [on_device(): lax.all_to_all(leaving[number], 'ep', split_axis=0, concat_axis=0, tiled=...]
    all_to_all x3, waiting for transfers between devices: 25.8 us -> 21 us  [on_device(): lax.all_to_all(outputs, 'ep', split_axis=0, concat_axis=0, tiled=True)]
  transfers between devices with their start and end apart: 24 -> 24, of which waited for: 12 -> 12; matrix products, arithmetic and copies ran while one was open for 5% -> 4% of each run, Pallas kernels for 14% -> 15%
where the time goes in v4:
time: 279 us; the launch traced here: 278 us
  waiting for transfers between devices  112 us (40%)
  starting transfers between devices  87.5 us (31%)
  Pallas kernels  42.8 us (15%)
  local copies, waits for them, and re-layouts  15.3 us (5%)
  between operations  13.9 us (5%)
  matrix products  5.12 us (2%)
    ppermute x16, waiting for transfers between devices, send(): lax.ppermute(array, 'tp', [(i, (i + step) % parts) for i in range(parts)])  50.7 us
    all_to_all x3, starting transfers between devices, on_device(): lax.all_to_all(leaving[number], 'ep', split_axis=0, concat_axis=0, tiled=...  37.1 us
    all_to_all x3, starting transfers between devices, on_device(): lax.all_to_all(outputs, 'ep', split_axis=0, concat_axis=0, tiled=True)  30.1 us
    all_gather x2, waiting for transfers between devices, on_device(): lax.all_gather(rows, 'tp', tiled=True).reshape(parts, *rows.shape)  25.1 us
    all_to_all x3, waiting for transfers between devices, on_device(): lax.all_to_all(outputs, 'ep', split_axis=0, concat_axis=0, tiled=True)  21 us
    ppermute x16, starting transfers between devices, send(): lax.ppermute(array, 'tp', [(i, (i + step) % parts) for i in range(parts)])  20.1 us
    pallas_call x3, Pallas kernels, hidden_units(): pl.pallas_call(functools.partial(hidden_kernel, gathered, parts), grid_sp...  18.8 us
    all_to_all x3, waiting for transfers between devices, on_device(): lax.all_to_all(leaving[number], 'ep', split_axis=0, concat_axis=0, tiled=...  14.8 us
  transfers between devices with their start and end apart: 24, of which 12 were waited for; matrix products, arithmetic and copies ran while one was open for 4% of the time, Pallas kernels for 15%

profile of v4, /device:TPU:1, one launch (start us, length us, event | category | flops | bytes accessed | tf_op | source)
XLA Modules:
  0.0 277.6 jit_solution(14563469090567105130)
XLA Ops:
  6.5 3.3 %dynamic-slice_bitcast_fusion = (bf16[256,1792]{1,0:T(8,128)(2,1)}, bf16[256,1792]{1,0:T(8,128)(2,1)}, bf16[256,1792]{1,0:T(8,128)(2,1)}) fusion(bf16[1,256,7168]{2,1,0:T(8,128)(2,1)} %param.11, s32[]{:T(128)S(6)} %select_n.61, s32[]{:T(128)S(6)} %select_n.59, s32[]{:T(128)S(6)} %select_n.57), kind=kLoop, calls=%fused_computation.14 | loop fusion | bytes 5505036 | tf_op jit(solution)/shard_map/dynamic_slice | solution.py:246
  19.1 13.3 %all-to-all-start = ((bf16[64,4,1792]{2,1,0:T(4,128)(2,1)}), bf16[64,4,1792]{2,1,0:T(4,128)(2,1)}, u32[]{:S(2)}, u32[]{:S(2)}) async-start(bf16[64,4,1792]{2,1,0:T(4,128)(2,1)} %place_rows.3.rest_0_), calls=%async_computation | async-start | bytes 1835008 | tf_op jit(solution)/shard_map/all_to_all | solution.py:272
  34.7 19.4 %collective-permute-done.6.refs_2_.refs_7_ = bf16[256,1792]{1,0:T(8,128)(2,1)S(1)} collective-permute-done((bf16[256,1792]{1,0:T(8,128)(2,1)}, bf16[256,1792]{1,0:T(8,128)(2,1)S(1)}, u32[]{:S(2)}, u32[]{:S(2)}) %collective-permute-start.6) | collective-permute-done | bytes 917536 | tf_op jit(solution)/shard_map/ppermute | solution.py:235
  62.5 11.8 %all-to-all-start.1 = ((bf16[64,4,1792]{2,1,0:T(4,128)(2,1)}), bf16[64,4,1792]{2,1,0:T(4,128)(2,1)S(1)}, u32[]{:S(2)}, u32[]{:S(2)}) async-start(bf16[64,4,1792]{2,1,0:T(4,128)(2,1)} %place_rows.5), calls=%async_computation.1 | async-start | bytes 1835008 | tf_op jit(solution)/shard_map/all_to_all | solution.py:272
  77.0 20.0 %collective-permute-done.refs_1_ = bf16[256,1792]{1,0:T(8,128)(2,1)S(1)} collective-permute-done((bf16[256,1792]{1,0:T(8,128)(2,1)S(1)}, bf16[256,1792]{1,0:T(8,128)(2,1)S(1)}, u32[]{:S(2)}, u32[]{:S(2)}) %collective-permute-start) | collective-permute-done | bytes 917536 | tf_op jit(solution)/shard_map/ppermute | solution.py:235
  99.0 2.7 collective-permute-start.3
  101.6 12.0 %all-to-all-start.4 = ((bf16[64,4,1792]{2,1,0:T(4,128)(2,1)}), bf16[64,4,1792]{2,1,0:T(4,128)(2,1)}, u32[]{:S(2)}, u32[]{:S(2)}) async-start(bf16[64,4,1792]{2,1,0:T(4,128)(2,1)} %place_rows.4.rest_1_), calls=%async_computation.4 | async-start | bytes 1835008 | tf_op jit(solution)/shard_map/all_to_all | solution.py:272
  116.4 6.2 %hidden_units.3.refs_0_.refs_3_ = bf16[256,256]{1,0:T(8,128)(2,1)} custom-call(s32[1]{0:T(128)} %bitcast.me_ref, bf16[256,1792]{1,0:T(8,128)(2,1)} %reshape.85.rest_0_.refs_0_, bf16[256,1792]{1,0:T(8,128)(2,1)} %copy-done.8, bf16[256,1792]{1,0:T(8,128)(2,1)} %copy-done.9, bf16[128,1792]{1,0:T(8,128)(2,1)} %collective-permute-done.2.refs_3_, ...), custom_call_target="tpu_custom_call" | custom-call | flops 187904819200 | bytes 11141120 | tf_op jit(solution)/shard_map/hidden_units/pallas_call | solution.py:77
  122.8 2.7 collective-permute-start.8
  125.4 13.4 %all-to-all-done.4 = bf16[64,4,1792]{2,1,0:T(4,128)(2,1)} async-done(((bf16[64,4,1792]{2,1,0:T(4,128)(2,1)}), bf16[64,4,1792]{2,1,0:T(4,128)(2,1)}, u32[]{:S(2)}, u32[]{:S(2)}) %all-to-all-start.4) | async-done | bytes 917536 | tf_op jit(solution)/shard_map/all_to_all | solution.py:272
  142.0 4.9 %down.3 = bf16[64,4,1792]{2,1,0:T(4,128)(2,1)} custom-call(s32[1]{0:T(128)} %bitcast.me_ref, bf16[256,256]{1,0:T(8,128)(2,1)} %hidden_units.3.refs_0_.refs_3_, bf16[256,256]{1,0:T(8,128)(2,1)} %copy-done.10, bf16[256,256]{1,0:T(8,128)(2,1)} %copy-done.11, bf16[256,256]{1,0:T(8,128)(2,1)} %copy-done.12, bf16[256,7168]{1,0:T(8,128)(2,1)} %bitcast.38, ...), custom_call_target="tpu_custom_call" | custom-call | flops 939524096 | bytes 5111808 | tf_op jit(solution)/shard_map/down/pallas_call | solution.py:141
  146.9 6.6 %all-to-all-start.2 = ((bf16[64,4,1792]{2,1,0:T(4,128)(2,1)}), bf16[64,4,1792]{2,1,0:T(4,128)(2,1)}, u32[]{:S(2)}, u32[]{:S(2)}) async-start(bf16[64,4,1792]{2,1,0:T(4,128)(2,1)} %down.3), calls=%async_computation.2 | async-start | bytes 1835008 | tf_op jit(solution)/shard_map/all_to_all | solution.py:286
  153.6 9.0 %all-gather.3.cloned.1.call-done = bf16[1024,1792]{1,0:T(8,128)(2,1)} async-done(((bf16[256,1792]{1,0:T(8,128)(2,1)}), bf16[1024,1792]{1,0:T(8,128)(2,1)}) %all-gather.3.cloned.1.call-update) | async-done | bytes 3670032 | tf_op jit(solution)/shard_map/all_gather | solution.py:279
  162.6 6.3 %hidden_units.4.refs_0_.refs_3_ = bf16[256,256]{1,0:T(8,128)(2,1)} custom-call(s32[1]{0:T(128)} %bitcast.me_ref, bf16[4,256,1792]{2,1,0:T(8,128)(2,1)} %bitcast.49, bf16[4,1792,256]{2,1,0:T(8,128)(2,1)} %bitcast.42, bf16[4,1792,256]{2,1,0:T(8,128)(2,1)} %bitcast.45, bf16[256,256]{1,0:T(8,128)(2,1)} %hidden_units.3.refs_0_.refs_3_), custom_call_target="tpu_custom_call" | custom-call | flops 187904819200 | bytes 11141120 | tf_op jit(solution)/shard_map/hidden_units/pallas_call | solution.py:77
  172.6 2.6 collective-permute-done.10.refs_1_
  175.2 3.7 %collective-permute-done.12.refs_3_ = bf16[256,256]{1,0:T(8,128)(2,1)S(1)} collective-permute-done((bf16[256,256]{1,0:T(8,128)(2,1)}, bf16[256,256]{1,0:T(8,128)(2,1)S(1)}, u32[]{:S(2)}, u32[]{:S(2)}) %collective-permute-start.12) | collective-permute-done | bytes 131104 | tf_op jit(solution)/shard_map/ppermute | solution.py:235
  179.6 4.9 %down.4 = bf16[64,4,1792]{2,1,0:T(4,128)(2,1)} custom-call(s32[1]{0:T(128)} %bitcast.me_ref, bf16[256,256]{1,0:T(8,128)(2,1)} %hidden_units.4.refs_0_.refs_3_, bf16[256,256]{1,0:T(8,128)(2,1)} %copy-done.15, bf16[256,256]{1,0:T(8,128)(2,1)} %copy-done.17, bf16[256,256]{1,0:T(8,128)(2,1)} %copy-done.18, bf16[256,7168]{1,0:T(8,128)(2,1)} %bitcast.39, ...), custom_call_target="tpu_custom_call" | custom-call | flops 939524096 | bytes 5111808 | tf_op jit(solution)/shard_map/down/pallas_call | solution.py:141
  184.5 11.0 %all-to-all-start.3 = ((bf16[64,4,1792]{2,1,0:T(4,128)(2,1)}), bf16[64,4,1792]{2,1,0:T(4,128)(2,1)S(1)}, u32[]{:S(2)}, u32[]{:S(2)}) async-start(bf16[64,4,1792]{2,1,0:T(4,128)(2,1)} %down.4), calls=%async_computation.3 | async-start | bytes 1835008 | tf_op jit(solution)/shard_map/all_to_all | solution.py:286
  195.5 16.1 %all-gather.5.cloned.1.call-done = bf16[1024,1792]{1,0:T(8,128)(2,1)} async-done(((bf16[256,1792]{1,0:T(8,128)(2,1)}), bf16[1024,1792]{1,0:T(8,128)(2,1)}) %all-gather.5.cloned.1.call-update) | async-done | bytes 3670032 | tf_op jit(solution)/shard_map/all_gather | solution.py:279
  211.5 6.3 %hidden_units.5.refs_0_ = bf16[256,256]{1,0:T(8,128)(2,1)} custom-call(s32[1]{0:T(128)} %bitcast.me_ref, bf16[4,256,1792]{2,1,0:T(8,128)(2,1)} %bitcast.47, bf16[4,1792,256]{2,1,0:T(8,128)(2,1)} %bitcast.43, bf16[4,1792,256]{2,1,0:T(8,128)(2,1)} %bitcast.46, bf16[256,256]{1,0:T(8,128)(2,1)} %hidden_units.4.refs_0_.refs_3_), custom_call_target="tpu_custom_call" | custom-call | flops 1879048192 | bytes 11141120 | tf_op jit(solution)/shard_map/hidden_units/pallas_call | solution.py:77
  221.1 2.6 collective-permute-done.13.refs_1_
  226.8 4.8 %down.5 = bf16[64,4,1792]{2,1,0:T(4,128)(2,1)} custom-call(s32[1]{0:T(128)} %bitcast.me_ref, bf16[256,256]{1,0:T(8,128)(2,1)} %hidden_units.5.refs_0_, bf16[256,256]{1,0:T(8,128)(2,1)} %copy-done.13, bf16[256,256]{1,0:T(8,128)(2,1)} %copy-done.14, bf16[256,256]{1,0:T(8,128)(2,1)} %copy-done.16, bf16[256,7168]{1,0:T(8,128)(2,1)} %bitcast.40, ...), custom_call_target="tpu_custom_call" | custom-call | flops 939524096 | bytes 5111808 | tf_op jit(solution)/shard_map/down/pallas_call | solution.py:141
  231.7 12.4 %all-to-all-start.5 = ((bf16[64,4,1792]{2,1,0:T(4,128)(2,1)}), bf16[64,4,1792]{2,1,0:T(4,128)(2,1)S(1)}, u32[]{:S(2)}, u32[]{:S(2)}) async-start(bf16[64,4,1792]{2,1,0:T(4,128)(2,1)} %down.5), calls=%async_computation.5 | async-start | bytes 1835008 | tf_op jit(solution)/shard_map/all_to_all | solution.py:286
  248.5 21.0 %all-to-all-done.5 = bf16[64,4,1792]{2,1,0:T(4,128)(2,1)S(1)} async-done(((bf16[64,4,1792]{2,1,0:T(4,128)(2,1)}), bf16[64,4,1792]{2,1,0:T(4,128)(2,1)S(1)}, u32[]{:S(2)}, u32[]{:S(2)}) %all-to-all-start.5) | async-done | bytes 917536 | tf_op jit(solution)/shard_map/all_to_all | solution.py:286
  (121 shorter events, 46.7 us)
Async XLA Ops:
  9.9 24.8 %collective-permute-start.4 = (bf16[256,1792]{1,0:T(8,128)(2,1)}, bf16[256,1792]{1,0:T(8,128)(2,1)S(1)}, u32[]{:S(2)}, u32[]{:S(2)}) collective-permute-start(bf16[256,1792]{1,0:T(8,128)(2,1)} %get-tuple-element.7), channel_id=1, source_target_pairs={{0,1},{1,2},{2,3},{3,0},{4,5},{5,6},{6,7},{7,4},{8,9},{9,10},{10,1... | collective-permute-start | bytes 2752520 | tf_op jit(solution)/shard_map/ppermute | solution.py:235
  11.9 22.8 %collective-permute-start.5 = (bf16[256,1792]{1,0:T(8,128)(2,1)}, bf16[256,1792]{1,0:T(8,128)(2,1)S(1)}, u32[]{:S(2)}, u32[]{:S(2)}) collective-permute-start(bf16[256,1792]{1,0:T(8,128)(2,1)} %get-tuple-element.6), channel_id=1, source_target_pairs={{0,3},{1,0},{2,1},{3,2},{4,7},{5,4},{6,5},{7,6},{8,11},{9,8},{10,9... | collective-permute-start | bytes 2752520 | tf_op jit(solution)/shard_map/ppermute | solution.py:235
  13.2 40.9 %collective-permute-start.6 = (bf16[256,1792]{1,0:T(8,128)(2,1)}, bf16[256,1792]{1,0:T(8,128)(2,1)S(1)}, u32[]{:S(2)}, u32[]{:S(2)}) collective-permute-start(bf16[256,1792]{1,0:T(8,128)(2,1)} %get-tuple-element.5), channel_id=1, source_target_pairs={{0,2},{1,3},{2,0},{3,1},{4,6},{5,7},{6,4},{7,5},{8,10},{9,11},{10,... | collective-permute-start | bytes 2752520 | tf_op jit(solution)/shard_map/ppermute | solution.py:235
  19.1 38.6 %all-to-all-start = ((bf16[64,4,1792]{2,1,0:T(4,128)(2,1)}), bf16[64,4,1792]{2,1,0:T(4,128)(2,1)}, u32[]{:S(2)}, u32[]{:S(2)}) async-start(bf16[64,4,1792]{2,1,0:T(4,128)(2,1)} %place_rows.3.rest_0_), calls=%async_computation | async-start | bytes 1835008 | tf_op jit(solution)/shard_map/all_to_all | solution.py:272
  62.5 39.2 %all-to-all-start.1 = ((bf16[64,4,1792]{2,1,0:T(4,128)(2,1)}), bf16[64,4,1792]{2,1,0:T(4,128)(2,1)S(1)}, u32[]{:S(2)}, u32[]{:S(2)}) async-start(bf16[64,4,1792]{2,1,0:T(4,128)(2,1)} %place_rows.5), calls=%async_computation.1 | async-start | bytes 1835008 | tf_op jit(solution)/shard_map/all_to_all | solution.py:272
  74.2 22.8 %collective-permute-start = (bf16[256,1792]{1,0:T(8,128)(2,1)S(1)}, bf16[256,1792]{1,0:T(8,128)(2,1)S(1)}, u32[]{:S(2)}, u32[]{:S(2)}) collective-permute-start(bf16[256,1792]{1,0:T(8,128)(2,1)S(1)} %copy-done.3), channel_id=1, source_target_pairs={{0,1},{1,2},{2,3},{3,0},{4,5},{5,6},{6,7},{7,4},{8,9},{9,10},{10,1... | collective-permute-start | bytes 2752520 | tf_op jit(solution)/shard_map/ppermute | solution.py:235
  75.2 22.7 %collective-permute-start.1 = (bf16[256,1792]{1,0:T(8,128)(2,1)S(1)}, bf16[256,1792]{1,0:T(8,128)(2,1)S(1)}, u32[]{:S(2)}, u32[]{:S(2)}) collective-permute-start(bf16[256,1792]{1,0:T(8,128)(2,1)S(1)} %copy-done.3), channel_id=1, source_target_pairs={{0,3},{1,0},{2,1},{3,2},{4,7},{5,4},{6,5},{7,6},{8,11},{9,8},{10,9... | collective-permute-start | bytes 2752520 | tf_op jit(solution)/shard_map/ppermute | solution.py:235
  97.9 18.5 %collective-permute-start.2 = (bf16[128,1792]{1,0:T(8,128)(2,1)}, bf16[128,1792]{1,0:T(8,128)(2,1)}, u32[]{:S(2)}, u32[]{:S(2)}) collective-permute-start(bf16[128,1792]{1,0:T(8,128)(2,1)} %slice.8), channel_id=1, source_target_pairs={{0,1},{1,2},{2,3},{3,0},{4,5},{5,6},{6,7},{7,4},{8,9},{9,10},{10,1... | collective-permute-start | bytes 1376264 | tf_op jit(solution)/shard_map/ppermute | solution.py:235
  99.0 17.4 %collective-permute-start.3 = (bf16[128,1792]{1,0:T(8,128)(2,1)}, bf16[128,1792]{1,0:T(8,128)(2,1)}, u32[]{:S(2)}, u32[]{:S(2)}) collective-permute-start(bf16[128,1792]{1,0:T(8,128)(2,1)} %slice.9), channel_id=1, source_target_pairs={{0,3},{1,0},{2,1},{3,2},{4,7},{5,4},{6,5},{7,6},{8,11},{9,8},{10,9... | collective-permute-start | bytes 1376264 | tf_op jit(solution)/shard_map/ppermute | solution.py:235
  101.6 37.2 %all-to-all-start.4 = ((bf16[64,4,1792]{2,1,0:T(4,128)(2,1)}), bf16[64,4,1792]{2,1,0:T(4,128)(2,1)}, u32[]{:S(2)}, u32[]{:S(2)}) async-start(bf16[64,4,1792]{2,1,0:T(4,128)(2,1)} %place_rows.4.rest_1_), calls=%async_computation.4 | async-start | bytes 1835008 | tf_op jit(solution)/shard_map/all_to_all | solution.py:272
  113.6 49.0 %all-gather.3.cloned.1.call-start = ((), (), s32[]{:S(2)}) async-start(), calls=%async_computation.6 | async-start | bytes 4587520 | tf_op jit(solution)/shard_map/all_gather | solution.py:279
  116.2 95.4 %all-gather.5.cloned.1.call-start = ((), (), s32[]{:S(2)}) async-start(), calls=%async_computation.7 | async-start | bytes 4587520 | tf_op jit(solution)/shard_map/all_gather | solution.py:279
  122.7 18.6 %collective-permute-start.7 = (bf16[256,256]{1,0:T(8,128)(2,1)}, bf16[256,256]{1,0:T(8,128)(2,1)S(1)}, u32[]{:S(2)}, u32[]{:S(2)}) collective-permute-start(bf16[256,256]{1,0:T(8,128)(2,1)} %hidden_units.3.refs_0_.refs_3_), channel_id=1, source_target_pairs={{0,1},{1,2},{2,3},{3,0},{4,5},{5,6},{6,7},{7,4},{8,9},{9,10},{10,1... | collective-permute-start | bytes 393224 | tf_op jit(solution)/shard_map/ppermute | solution.py:235
  122.8 18.5 %collective-permute-start.8 = (bf16[256,256]{1,0:T(8,128)(2,1)}, bf16[256,256]{1,0:T(8,128)(2,1)S(1)}, u32[]{:S(2)}, u32[]{:S(2)}) collective-permute-start(bf16[256,256]{1,0:T(8,128)(2,1)} %hidden_units.3.refs_0_.refs_3_), channel_id=1, source_target_pairs={{0,3},{1,0},{2,1},{3,2},{4,7},{5,4},{6,5},{7,6},{8,11},{9,8},{10,9... | collective-permute-start | bytes 393224 | tf_op jit(solution)/shard_map/ppermute | solution.py:235
  125.4 15.9 %collective-permute-start.9 = (bf16[256,256]{1,0:T(8,128)(2,1)}, bf16[256,256]{1,0:T(8,128)(2,1)S(1)}, u32[]{:S(2)}, u32[]{:S(2)}) collective-permute-start(bf16[256,256]{1,0:T(8,128)(2,1)} %hidden_units.3.refs_0_.refs_3_), channel_id=1, source_target_pairs={{0,2},{1,3},{2,0},{3,1},{4,6},{5,7},{6,4},{7,5},{8,10},{9,11},{10,... | collective-permute-start | bytes 393224 | tf_op jit(solution)/shard_map/ppermute | solution.py:235
  146.9 37.5 %all-to-all-start.2 = ((bf16[64,4,1792]{2,1,0:T(4,128)(2,1)}), bf16[64,4,1792]{2,1,0:T(4,128)(2,1)}, u32[]{:S(2)}, u32[]{:S(2)}) async-start(bf16[64,4,1792]{2,1,0:T(4,128)(2,1)} %down.3), calls=%async_computation.2 | async-start | bytes 1835008 | tf_op jit(solution)/shard_map/all_to_all | solution.py:286
  168.9 6.2 %collective-permute-start.10 = (bf16[256,256]{1,0:T(8,128)(2,1)}, bf16[256,256]{1,0:T(8,128)(2,1)S(1)}, u32[]{:S(2)}, u32[]{:S(2)}) collective-permute-start(bf16[256,256]{1,0:T(8,128)(2,1)} %hidden_units.4.refs_0_.refs_3_), channel_id=1, source_target_pairs={{0,1},{1,2},{2,3},{3,0},{4,5},{5,6},{6,7},{7,4},{8,9},{9,10},{10,1... | collective-permute-start | bytes 393224 | tf_op jit(solution)/shard_map/ppermute | solution.py:235
  169.3 5.9 %collective-permute-start.11 = (bf16[256,256]{1,0:T(8,128)(2,1)}, bf16[256,256]{1,0:T(8,128)(2,1)S(1)}, u32[]{:S(2)}, u32[]{:S(2)}) collective-permute-start(bf16[256,256]{1,0:T(8,128)(2,1)} %hidden_units.4.refs_0_.refs_3_), channel_id=1, source_target_pairs={{0,3},{1,0},{2,1},{3,2},{4,7},{5,4},{6,5},{7,6},{8,11},{9,8},{10,9... | collective-permute-start | bytes 393224 | tf_op jit(solution)/shard_map/ppermute | solution.py:235
  171.7 7.2 %collective-permute-start.12 = (bf16[256,256]{1,0:T(8,128)(2,1)}, bf16[256,256]{1,0:T(8,128)(2,1)S(1)}, u32[]{:S(2)}, u32[]{:S(2)}) collective-permute-start(bf16[256,256]{1,0:T(8,128)(2,1)} %hidden_units.4.refs_0_.refs_3_), channel_id=1, source_target_pairs={{0,2},{1,3},{2,0},{3,1},{4,6},{5,7},{6,4},{7,5},{8,10},{9,11},{10,... | collective-permute-start | bytes 393224 | tf_op jit(solution)/shard_map/ppermute | solution.py:235
  184.5 47.2 %all-to-all-start.3 = ((bf16[64,4,1792]{2,1,0:T(4,128)(2,1)}), bf16[64,4,1792]{2,1,0:T(4,128)(2,1)S(1)}, u32[]{:S(2)}, u32[]{:S(2)}) async-start(bf16[64,4,1792]{2,1,0:T(4,128)(2,1)} %down.4), calls=%async_computation.3 | async-start | bytes 1835008 | tf_op jit(solution)/shard_map/all_to_all | solution.py:286
  217.9 5.9 %collective-permute-start.13 = (bf16[256,256]{1,0:T(8,128)(2,1)}, bf16[256,256]{1,0:T(8,128)(2,1)S(1)}, u32[]{:S(2)}, u32[]{:S(2)}) collective-permute-start(bf16[256,256]{1,0:T(8,128)(2,1)} %hidden_units.5.refs_0_), channel_id=1, source_target_pairs={{0,1},{1,2},{2,3},{3,0},{4,5},{5,6},{6,7},{7,4},{8,9},{9,10},{10,1... | collective-permute-start | bytes 393224 | tf_op jit(solution)/shard_map/ppermute | solution.py:235
  218.5 5.9 %collective-permute-start.14 = (bf16[256,256]{1,0:T(8,128)(2,1)}, bf16[256,256]{1,0:T(8,128)(2,1)S(1)}, u32[]{:S(2)}, u32[]{:S(2)}) collective-permute-start(bf16[256,256]{1,0:T(8,128)(2,1)} %hidden_units.5.refs_0_), channel_id=1, source_target_pairs={{0,3},{1,0},{2,1},{3,2},{4,7},{5,4},{6,5},{7,6},{8,11},{9,8},{10,9... | collective-permute-start | bytes 393224 | tf_op jit(solution)/shard_map/ppermute | solution.py:235
  220.6 5.5 %collective-permute-start.15 = (bf16[256,256]{1,0:T(8,128)(2,1)}, bf16[256,256]{1,0:T(8,128)(2,1)S(1)}, u32[]{:S(2)}, u32[]{:S(2)}) collective-permute-start(bf16[256,256]{1,0:T(8,128)(2,1)} %hidden_units.5.refs_0_), channel_id=1, source_target_pairs={{0,2},{1,3},{2,0},{3,1},{4,6},{5,7},{6,4},{7,5},{8,10},{9,11},{10,... | collective-permute-start | bytes 393224 | tf_op jit(solution)/shard_map/ppermute | solution.py:235
  231.7 37.7 %all-to-all-start.5 = ((bf16[64,4,1792]{2,1,0:T(4,128)(2,1)}), bf16[64,4,1792]{2,1,0:T(4,128)(2,1)S(1)}, u32[]{:S(2)}, u32[]{:S(2)}) async-start(bf16[64,4,1792]{2,1,0:T(4,128)(2,1)} %down.5), calls=%async_computation.5 | async-start | bytes 1835008 | tf_op jit(solution)/shard_map/all_to_all | solution.py:286
  (25 other events, 335.2 us)
Sparse Core Ops, SparseCore 0:
  116.3 46.2 all-gather.2
  164.4 47.0 all-gather.4

commit v5 on v4

--- a/solution.py
+++ b/solution.py
@@ -8,11 +8,13 @@
 from jax.sharding import PartitionSpec as P
 
 CAP = 12
-CHUNKS = ((0, 4, True), (4, 4, False), (8, 4, False))
+DISPATCHES = ((0, 8), (8, 4))
+CHUNKS = ((0, 4), (4, 4), (8, 4))
+BY_RING = (False, True, False)
 SENDS = (1, 3, 2)
 STEPS = (0, 3, 1, 2)
 TILES = 2
-TOLD = (100, 100, 1)
+TOLD = (100, 10, 1)
 WAIT_TOLD = 200_000_000_000
 MIB = 1024 * 1024
 CORNER = pl.BlockSpec((16, 128), lambda *index: (0, 0))
@@ -255,37 +257,34 @@
     slot = jnp.dot(earlier, chosen.astype(jnp.bfloat16), preferred_element_type=jnp.float32).astype(jnp.int32)
     slot = jnp.where(chosen, slot, CAP)
 
-    places = []
-    for first, count, _ in CHUNKS:
+    def spots(first, count):
         here = slot[:, :, None] == first + jnp.arange(count, dtype=jnp.int32)
-        places.append(here.reshape(row_count, experts * count))
-
-    def outgoing(number, after):
-        return place_rows(places[number].astype(jnp.bfloat16), hidden_rows, experts, after, 1)
+        return here.reshape(row_count, experts * count)
+
+    arrived = []
+    for number, (first, count) in enumerate(DISPATCHES):
+        after = [] if number == 0 else [arrived[0], wait_for(pieces, WAIT_TOLD)]
+        spot = spots(first, count).astype(jnp.bfloat16)
+        outgoing = place_rows(spot, hidden_rows, experts, after, 1)
+        rows = lax.all_to_all(outgoing, "ep", split_axis=0, concat_axis=0, tiled=True)
+        for start in range(0, count, 4):
+            arrived.append(rows[:, start:start + 4].reshape(experts * 4, width))
 
     gathered = []
-    leaving = [outgoing(0, []), None, None]
-    leaving[2] = outgoing(2, leaving[:1])
-    for number, (first, count, by_permutes) in enumerate(CHUNKS):
-        if number == 1:
-            leaving[1] = outgoing(1, [rows, leaving[2], wait_for(pieces, WAIT_TOLD)])
-        rows = lax.all_to_all(leaving[number], "ep", split_axis=0, concat_axis=0, tiled=True)
-        rows = rows.reshape(experts * count, width)
-        if number == 1:
-            waited = wait_for([rows], WAIT_TOLD)
-        if by_permutes:
+    for rows, by_ring in zip(arrived, BY_RING):
+        if by_ring:
             gathered.append([rows] + ring(rows))
         else:
             gathered.append([lax.all_gather(rows, "tp", tiled=True).reshape(parts, *rows.shape)])
 
     mixed = jnp.zeros((row_count, width), jnp.float32)
-    for number, ((first, count, by_permutes), spot, x, told) in enumerate(zip(CHUNKS, places, gathered, TOLD)):
-        after = [activated] if number else [waited]
+    for number, ((first, count), x, told) in enumerate(zip(CHUNKS, gathered, TOLD)):
+        after = [activated] if number else []
         activated = hidden_units(me, x, w_gate, w_up, after, told)
         outputs = down(me, [activated] + send_all(activated), w_down, pieces, experts)
         returned = lax.all_to_all(outputs, "ep", split_axis=0, concat_axis=0, tiled=True)
         returned = returned.reshape(experts * count, width)
-        mix = jnp.where(spot, jnp.repeat(weight, count, axis=1), 0.0)
+        mix = jnp.where(spots(first, count), jnp.repeat(weight, count, axis=1), 0.0)
         high = mix.astype(jnp.bfloat16)
         low = (mix - high.astype(jnp.float32)).astype(jnp.bfloat16)
         mixed = mixed + jnp.dot(high, returned, preferred_element_type=jnp.float32)

time: 279 us -> 278 us (level)
  starting transfers between devices: 87.5 us -> 69 us
  waiting for transfers between devices: 112 us -> 130 us
  local copies, waits for them, and re-layouts: 15.3 us -> 19.1 us
  Pallas kernels: 42.8 us -> 39.4 us
    all_gather x2, waiting for transfers between devices: 25.1 us -> 3.47 us  [on_device(): lax.all_gather(rows, 'tp', tiled=True).reshape(parts, *rows.shape)]
    all_to_all x3 -> x2, waiting for transfers between devices: 14.8 us -> 35.1 us  [on_device(): lax.all_to_all(outgoing, 'ep', split_axis=0, concat_axis=0, tiled=True)]
    all_to_all x3 -> x2, starting transfers between devices: 37.1 us -> 20.1 us  [on_device(): lax.all_to_all(outgoing, 'ep', split_axis=0, concat_axis=0, tiled=True)]
    ppermute x16, waiting for transfers between devices: 50.7 us -> 63.7 us  [send(): lax.ppermute(array, 'tp', [(i, (i + step) % parts) for i in range(parts)])]
    all_to_all x3, waiting for transfers between devices: 21 us -> 28.1 us  [on_device(): lax.all_to_all(outputs, 'ep', split_axis=0, concat_axis=0, tiled=True)]
    slice x0 -> x1, local copies, waits for them, and re-layouts: none -> 3.99 us  [on_device(): arrived.append(rows[:, start:start + 4].reshape(experts * 4, width))]
    pallas_call x3 -> x2, Pallas kernels: 6.82 us -> 5.05 us  [place_rows(): pl.pallas_call(place_kernel, grid=(1,), in_specs=[pl.BlockSpec((rows.shap...]
  transfers between devices with their start and end apart: 24 -> 23, of which waited for: 12 -> 12; matrix products, arithmetic and copies ran while one was open for 4% -> 6% of each run, Pallas kernels for 15% -> 13%
where the time goes in v5:
time: 278 us; the launch traced here: 277 us
  waiting for transfers between devices  130 us (47%)
  starting transfers between devices  69 us (25%)
  Pallas kernels  39.4 us (14%)
  local copies, waits for them, and re-layouts  19.1 us (7%)
  between operations  13.9 us (5%)
    ppermute x16, waiting for transfers between devices, send(): lax.ppermute(array, 'tp', [(i, (i + step) % parts) for i in range(parts)])  63.7 us
    all_to_all x2, waiting for transfers between devices, on_device(): lax.all_to_all(outgoing, 'ep', split_axis=0, concat_axis=0, tiled=True)  35.1 us
    all_to_all x3, starting transfers between devices, on_device(): lax.all_to_all(outputs, 'ep', split_axis=0, concat_axis=0, tiled=True)  30.4 us
    all_to_all x3, waiting for transfers between devices, on_device(): lax.all_to_all(outputs, 'ep', split_axis=0, concat_axis=0, tiled=True)  28.1 us
    all_to_all x2, starting transfers between devices, on_device(): lax.all_to_all(outgoing, 'ep', split_axis=0, concat_axis=0, tiled=True)  20.1 us
    ppermute x16, starting transfers between devices, send(): lax.ppermute(array, 'tp', [(i, (i + step) % parts) for i in range(parts)])  18.4 us
    pallas_call x3, Pallas kernels, hidden_units(): pl.pallas_call(functools.partial(hidden_kernel, gathered, parts), grid_sp...  18.2 us
    pallas_call x3, Pallas kernels, down(): pl.pallas_call(functools.partial(down_kernel, parts), grid_spec=pltpu.Pre...  14.8 us
  transfers between devices with their start and end apart: 23, of which 12 were waited for; matrix products, arithmetic and copies ran while one was open for 6% of the time, Pallas kernels for 13%

profile of v5, /device:TPU:1, one launch (start us, length us, event | category | flops | bytes accessed | tf_op | source)
XLA Modules:
  0.0 277.0 jit_solution(7204136900367137332)
XLA Ops:
  8.9 2.7 place_rows.2
  11.6 13.3 %all-to-all-start = ((bf16[64,8,1792]{2,1,0:T(8,128)(2,1)}), bf16[64,8,1792]{2,1,0:T(8,128)(2,1)}, u32[]{:S(2)}, u32[]{:S(2)}) async-start(bf16[64,8,1792]{2,1,0:T(8,128)(2,1)} %place_rows.2), calls=%async_computation | async-start | bytes 3670016 | tf_op jit(solution)/shard_map/all_to_all | solution.py:269
  25.1 3.4 %dynamic-slice_bitcast_fusion = (bf16[256,1792]{1,0:T(8,128)(2,1)}, bf16[256,1792]{1,0:T(8,128)(2,1)}, bf16[256,1792]{1,0:T(8,128)(2,1)}) fusion(bf16[1,256,7168]{2,1,0:T(8,128)(2,1)} %param.11, s32[]{:T(128)S(6)} %select_n.61, s32[]{:T(128)S(6)} %select_n.57, s32[]{:T(128)S(6)} %select_n.59), kind=kLoop, calls=%fused_computation.14 | loop fusion | bytes 5505036 | tf_op jit(solution)/shard_map/dynamic_slice | solution.py:248
  34.1 35.1 %all-to-all-done = bf16[64,8,1792]{2,1,0:T(8,128)(2,1)} async-done(((bf16[64,8,1792]{2,1,0:T(8,128)(2,1)}), bf16[64,8,1792]{2,1,0:T(8,128)(2,1)}, u32[]{:S(2)}, u32[]{:S(2)}) %all-to-all-start) | async-done | bytes 1835040 | tf_op jit(solution)/shard_map/all_to_all | solution.py:269
  69.2 4.0 %fusion.30 = (bf16[64,4,1792]{2,1,0:T(4,128)(2,1)}, bf16[64,4,1792]{2,1,0:T(4,128)(2,1)}) fusion(bf16[64,8,1792]{2,1,0:T(8,128)(2,1)} %all-to-all-done), kind=kLoop, calls=%fused_computation.56 | loop fusion | bytes 3670016 | tf_op jit(solution)/shard_map/slice | solution.py:271
  81.5 6.8 %all-to-all-start.3 = ((bf16[64,4,1792]{2,1,0:T(4,128)(2,1)}), bf16[64,4,1792]{2,1,0:T(4,128)(2,1)S(1)}, u32[]{:S(2)}, u32[]{:S(2)}) async-start(bf16[64,4,1792]{2,1,0:T(4,128)(2,1)} %place_rows.3), calls=%async_computation.3 | async-start | bytes 1835008 | tf_op jit(solution)/shard_map/all_to_all | solution.py:269
  91.4 40.3 %collective-permute-done.6.refs_1_ = bf16[256,1792]{1,0:T(8,128)(2,1)S(1)} collective-permute-done((bf16[256,1792]{1,0:T(8,128)(2,1)S(1)}, bf16[256,1792]{1,0:T(8,128)(2,1)S(1)}, u32[]{:S(2)}, u32[]{:S(2)}) %collective-permute-start.6) | collective-permute-done | bytes 917536 | tf_op jit(solution)/shard_map/ppermute | solution.py:237
  133.7 2.7 collective-permute-start.9
  137.5 3.4 %all-gather.3.cloned.1.call-done = bf16[1024,1792]{1,0:T(8,128)(2,1)} async-done(((bf16[256,1792]{1,0:T(8,128)(2,1)}), bf16[1024,1792]{1,0:T(8,128)(2,1)}) %all-gather.3.cloned.1.call-update) | async-done | bytes 3670032 | tf_op jit(solution)/shard_map/all_gather | solution.py:278
  141.0 5.6 %hidden_units.3.refs_0_.refs_7_ = bf16[256,256]{1,0:T(8,128)(2,1)} custom-call(s32[1]{0:T(128)} %bitcast.me_ref, bf16[4,256,1792]{2,1,0:T(8,128)(2,1)} %bitcast.51, bf16[4,1792,256]{2,1,0:T(8,128)(2,1)} %bitcast.43, bf16[4,1792,256]{2,1,0:T(8,128)(2,1)} %bitcast.46), custom_call_target="tpu_custom_call" | custom-call | flops 187904819200 | bytes 11141120 | tf_op jit(solution)/shard_map/hidden_units/pallas_call | solution.py:79
  155.5 5.1 %down.3 = bf16[64,4,1792]{2,1,0:T(4,128)(2,1)} custom-call(s32[1]{0:T(128)} %bitcast.me_ref, bf16[256,256]{1,0:T(8,128)(2,1)} %hidden_units.3.refs_0_.refs_7_, bf16[256,256]{1,0:T(8,128)(2,1)} %copy-done.13, bf16[256,256]{1,0:T(8,128)(2,1)} %copy-done.16, bf16[256,256]{1,0:T(8,128)(2,1)} %copy-done.18, bf16[256,7168]{1,0:T(8,128)(2,1)} %bitcast.40, ...), custom_call_target="tpu_custom_call" | custom-call | flops 939524096 | bytes 5111808 | tf_op jit(solution)/shard_map/down/pallas_call | solution.py:143
  160.6 12.7 %all-to-all-start.1 = ((bf16[64,4,1792]{2,1,0:T(4,128)(2,1)}), bf16[64,4,1792]{2,1,0:T(4,128)(2,1)S(1)}, u32[]{:S(2)}, u32[]{:S(2)}) async-start(bf16[64,4,1792]{2,1,0:T(4,128)(2,1)} %down.3), calls=%async_computation.1 | async-start | bytes 1835008 | tf_op jit(solution)/shard_map/all_to_all | solution.py:285
  173.3 6.3 %hidden_units.4.refs_0_.refs_3_ = bf16[256,256]{1,0:T(8,128)(2,1)} custom-call(s32[1]{0:T(128)} %bitcast.me_ref, bf16[256,1792]{1,0:T(8,128)(2,1)} %copy-done.4, bf16[256,1792]{1,0:T(8,128)(2,1)} %copy-done.9, bf16[256,1792]{1,0:T(8,128)(2,1)} %copy-done.10, bf16[128,1792]{1,0:T(8,128)(2,1)} %collective-permute-done.8.refs_3_, ...), custom_call_target="tpu_custom_call" | custom-call | flops 18790481920 | bytes 11141120 | tf_op jit(solution)/shard_map/hidden_units/pallas_call | solution.py:79
  182.9 6.4 %collective-permute-done.10.refs_1_ = bf16[256,256]{1,0:T(8,128)(2,1)S(1)} collective-permute-done((bf16[256,256]{1,0:T(8,128)(2,1)}, bf16[256,256]{1,0:T(8,128)(2,1)S(1)}, u32[]{:S(2)}, u32[]{:S(2)}) %collective-permute-start.10) | collective-permute-done | bytes 131104 | tf_op jit(solution)/shard_map/ppermute | solution.py:237
  189.3 5.7 %collective-permute-done.12.refs_3_ = bf16[256,256]{1,0:T(8,128)(2,1)S(1)} collective-permute-done((bf16[256,256]{1,0:T(8,128)(2,1)}, bf16[256,256]{1,0:T(8,128)(2,1)S(1)}, u32[]{:S(2)}, u32[]{:S(2)}) %collective-permute-start.12) | collective-permute-done | bytes 131104 | tf_op jit(solution)/shard_map/ppermute | solution.py:237
  195.6 4.9 %down.4 = bf16[64,4,1792]{2,1,0:T(4,128)(2,1)} custom-call(s32[1]{0:T(128)} %bitcast.me_ref, bf16[256,256]{1,0:T(8,128)(2,1)} %hidden_units.4.refs_0_.refs_3_, bf16[256,256]{1,0:T(8,128)(2,1)} %copy-done.14, bf16[256,256]{1,0:T(8,128)(2,1)} %copy-done.17, bf16[256,256]{1,0:T(8,128)(2,1)} %copy-done.19, bf16[256,7168]{1,0:T(8,128)(2,1)} %bitcast.41, ...), custom_call_target="tpu_custom_call" | custom-call | flops 939524096 | bytes 5111808 | tf_op jit(solution)/shard_map/down/pallas_call | solution.py:143
  200.5 10.7 %all-to-all-start.2 = ((bf16[64,4,1792]{2,1,0:T(4,128)(2,1)}), bf16[64,4,1792]{2,1,0:T(4,128)(2,1)S(1)}, u32[]{:S(2)}, u32[]{:S(2)}) async-start(bf16[64,4,1792]{2,1,0:T(4,128)(2,1)} %down.4), calls=%async_computation.2 | async-start | bytes 1835008 | tf_op jit(solution)/shard_map/all_to_all | solution.py:285
  211.3 6.3 %hidden_units.5.refs_0_ = bf16[256,256]{1,0:T(8,128)(2,1)} custom-call(s32[1]{0:T(128)} %bitcast.me_ref, bf16[4,256,1792]{2,1,0:T(8,128)(2,1)} %bitcast.49, bf16[4,1792,256]{2,1,0:T(8,128)(2,1)} %bitcast.45, bf16[4,1792,256]{2,1,0:T(8,128)(2,1)} %bitcast.48, bf16[256,256]{1,0:T(8,128)(2,1)} %hidden_units.4.refs_0_.refs_3_), custom_call_target="tpu_custom_call" | custom-call | flops 1879048192 | bytes 11141120 | tf_op jit(solution)/shard_map/hidden_units/pallas_call | solution.py:79
  220.4 3.1 %collective-permute-done.13.refs_1_ = bf16[256,256]{1,0:T(8,128)(2,1)S(1)} collective-permute-done((bf16[256,256]{1,0:T(8,128)(2,1)}, bf16[256,256]{1,0:T(8,128)(2,1)S(1)}, u32[]{:S(2)}, u32[]{:S(2)}) %collective-permute-start.13) | collective-permute-done | bytes 131104 | tf_op jit(solution)/shard_map/ppermute | solution.py:237
  223.5 2.7 collective-permute-done.15.refs_3_
  226.9 4.9 %down.5 = bf16[64,4,1792]{2,1,0:T(4,128)(2,1)} custom-call(s32[1]{0:T(128)} %bitcast.me_ref, bf16[256,256]{1,0:T(8,128)(2,1)} %hidden_units.5.refs_0_, bf16[256,256]{1,0:T(8,128)(2,1)} %copy-done.11, bf16[256,256]{1,0:T(8,128)(2,1)} %copy-done.12, bf16[256,256]{1,0:T(8,128)(2,1)} %copy-done.15, bf16[256,7168]{1,0:T(8,128)(2,1)} %bitcast.42, ...), custom_call_target="tpu_custom_call" | custom-call | flops 939524096 | bytes 5111808 | tf_op jit(solution)/shard_map/down/pallas_call | solution.py:143
  231.8 4.8 %all-to-all-done.2 = bf16[64,4,1792]{2,1,0:T(4,128)(2,1)S(1)} async-done(((bf16[64,4,1792]{2,1,0:T(4,128)(2,1)}), bf16[64,4,1792]{2,1,0:T(4,128)(2,1)S(1)}, u32[]{:S(2)}, u32[]{:S(2)}) %all-to-all-start.2) | async-done | bytes 917536 | tf_op jit(solution)/shard_map/all_to_all | solution.py:285
  236.5 7.0 %all-to-all-start.4 = ((bf16[64,4,1792]{2,1,0:T(4,128)(2,1)}), bf16[64,4,1792]{2,1,0:T(4,128)(2,1)S(1)}, u32[]{:S(2)}, u32[]{:S(2)}) async-start(bf16[64,4,1792]{2,1,0:T(4,128)(2,1)} %down.5), calls=%async_computation.4 | async-start | bytes 1835008 | tf_op jit(solution)/shard_map/all_to_all | solution.py:285
  245.5 23.3 %all-to-all-done.4 = bf16[64,4,1792]{2,1,0:T(4,128)(2,1)S(1)} async-done(((bf16[64,4,1792]{2,1,0:T(4,128)(2,1)}), bf16[64,4,1792]{2,1,0:T(4,128)(2,1)S(1)}, u32[]{:S(2)}, u32[]{:S(2)}) %all-to-all-start.4) | async-done | bytes 917536 | tf_op jit(solution)/shard_map/all_to_all | solution.py:285
  (117 shorter events, 41.9 us)
Async XLA Ops:
  11.6 57.6 %all-to-all-start = ((bf16[64,8,1792]{2,1,0:T(8,128)(2,1)}), bf16[64,8,1792]{2,1,0:T(8,128)(2,1)}, u32[]{:S(2)}, u32[]{:S(2)}) async-start(bf16[64,8,1792]{2,1,0:T(8,128)(2,1)} %place_rows.2), calls=%async_computation | async-start | bytes 3670016 | tf_op jit(solution)/shard_map/all_to_all | solution.py:269
  25.0 116.0 %all-gather.3.cloned.1.call-start = ((), (), s32[]{:S(2)}) async-start(), calls=%async_computation.5 | async-start | bytes 4587520 | tf_op jit(solution)/shard_map/all_gather | solution.py:278
  28.5 47.1 %collective-permute-start.3 = (bf16[256,1792]{1,0:T(8,128)(2,1)}, bf16[256,1792]{1,0:T(8,128)(2,1)S(1)}, u32[]{:S(2)}, u32[]{:S(2)}) collective-permute-start(bf16[256,1792]{1,0:T(8,128)(2,1)} %get-tuple-element.6), channel_id=1, source_target_pairs={{0,1},{1,2},{2,3},{3,0},{4,5},{5,6},{6,7},{7,4},{8,9},{9,10},{10,1... | collective-permute-start | bytes 2752520 | tf_op jit(solution)/shard_map/ppermute | solution.py:237
  29.7 45.9 %collective-permute-start.4 = (bf16[256,1792]{1,0:T(8,128)(2,1)}, bf16[256,1792]{1,0:T(8,128)(2,1)S(1)}, u32[]{:S(2)}, u32[]{:S(2)}) collective-permute-start(bf16[256,1792]{1,0:T(8,128)(2,1)} %get-tuple-element.7), channel_id=1, source_target_pairs={{0,3},{1,0},{2,1},{3,2},{4,7},{5,4},{6,5},{7,6},{8,11},{9,8},{10,9... | collective-permute-start | bytes 2752520 | tf_op jit(solution)/shard_map/ppermute | solution.py:237
  31.2 44.5 %collective-permute-start.5 = (bf16[256,1792]{1,0:T(8,128)(2,1)}, bf16[256,1792]{1,0:T(8,128)(2,1)S(1)}, u32[]{:S(2)}, u32[]{:S(2)}) collective-permute-start(bf16[256,1792]{1,0:T(8,128)(2,1)} %get-tuple-element.5), channel_id=1, source_target_pairs={{0,2},{1,3},{2,0},{3,1},{4,6},{5,7},{6,4},{7,5},{8,10},{9,11},{10,... | collective-permute-start | bytes 2752520 | tf_op jit(solution)/shard_map/ppermute | solution.py:237
  81.5 54.9 %all-to-all-start.3 = ((bf16[64,4,1792]{2,1,0:T(4,128)(2,1)}), bf16[64,4,1792]{2,1,0:T(4,128)(2,1)S(1)}, u32[]{:S(2)}, u32[]{:S(2)}) async-start(bf16[64,4,1792]{2,1,0:T(4,128)(2,1)} %place_rows.3), calls=%async_computation.3 | async-start | bytes 1835008 | tf_op jit(solution)/shard_map/all_to_all | solution.py:269
  88.3 123.0 %all-gather.5.cloned.1.call-start = ((), (), s32[]{:S(2)}) async-start(), calls=%async_computation.6 | async-start | bytes 4587520 | tf_op jit(solution)/shard_map/all_gather | solution.py:278
  88.6 58.0 %copy-start.4 = (bf16[256,1792]{1,0:T(8,128)(2,1)}, bf16[256,1792]{1,0:T(8,128)(2,1)S(1)}, u32[]{:S(2)}) copy-start(bf16[256,1792]{1,0:T(8,128)(2,1)S(1)} %reshape.91.refs_0_) | copy-start | bytes 2752516
  88.6 43.1 %collective-permute-start.6 = (bf16[256,1792]{1,0:T(8,128)(2,1)S(1)}, bf16[256,1792]{1,0:T(8,128)(2,1)S(1)}, u32[]{:S(2)}, u32[]{:S(2)}) collective-permute-start(bf16[256,1792]{1,0:T(8,128)(2,1)S(1)} %reshape.91.refs_0_), channel_id=1, source_target_pairs={{0,1},{1,2},{2,3},{3,0},{4,5},{5,6},{6,7},{7,4},{8,9},{9,10},{10,1... | collective-permute-start | bytes 2752520 | tf_op jit(solution)/shard_map/ppermute | solution.py:237
  89.9 42.7 %collective-permute-start.7 = (bf16[256,1792]{1,0:T(8,128)(2,1)S(1)}, bf16[256,1792]{1,0:T(8,128)(2,1)S(1)}, u32[]{:S(2)}, u32[]{:S(2)}) collective-permute-start(bf16[256,1792]{1,0:T(8,128)(2,1)S(1)} %reshape.91.refs_0_), channel_id=1, source_target_pairs={{0,3},{1,0},{2,1},{3,2},{4,7},{5,4},{6,5},{7,6},{8,11},{9,8},{10,9... | collective-permute-start | bytes 2752520 | tf_op jit(solution)/shard_map/ppermute | solution.py:237
  132.6 40.8 %collective-permute-start.8 = (bf16[128,1792]{1,0:T(8,128)(2,1)}, bf16[128,1792]{1,0:T(8,128)(2,1)}, u32[]{:S(2)}, u32[]{:S(2)}) collective-permute-start(bf16[128,1792]{1,0:T(8,128)(2,1)} %slice.18), channel_id=1, source_target_pairs={{0,1},{1,2},{2,3},{3,0},{4,5},{5,6},{6,7},{7,4},{8,9},{9,10},{10,1... | collective-permute-start | bytes 1376264 | tf_op jit(solution)/shard_map/ppermute | solution.py:237
  133.7 39.7 %collective-permute-start.9 = (bf16[128,1792]{1,0:T(8,128)(2,1)}, bf16[128,1792]{1,0:T(8,128)(2,1)}, u32[]{:S(2)}, u32[]{:S(2)}) collective-permute-start(bf16[128,1792]{1,0:T(8,128)(2,1)} %slice.19), channel_id=1, source_target_pairs={{0,3},{1,0},{2,1},{3,2},{4,7},{5,4},{6,5},{7,6},{8,11},{9,8},{10,9... | collective-permute-start | bytes 1376264 | tf_op jit(solution)/shard_map/ppermute | solution.py:237
  146.6 5.3 %collective-permute-start = (bf16[256,256]{1,0:T(8,128)(2,1)}, bf16[256,256]{1,0:T(8,128)(2,1)S(1)}, u32[]{:S(2)}, u32[]{:S(2)}) collective-permute-start(bf16[256,256]{1,0:T(8,128)(2,1)} %hidden_units.3.refs_0_.refs_7_), channel_id=1, source_target_pairs={{0,1},{1,2},{2,3},{3,0},{4,5},{5,6},{6,7},{7,4},{8,9},{9,10},{10,1... | collective-permute-start | bytes 393224 | tf_op jit(solution)/shard_map/ppermute | solution.py:237
  146.7 6.0 %collective-permute-start.1 = (bf16[256,256]{1,0:T(8,128)(2,1)}, bf16[256,256]{1,0:T(8,128)(2,1)S(1)}, u32[]{:S(2)}, u32[]{:S(2)}) collective-permute-start(bf16[256,256]{1,0:T(8,128)(2,1)} %hidden_units.3.refs_0_.refs_7_), channel_id=1, source_target_pairs={{0,3},{1,0},{2,1},{3,2},{4,7},{5,4},{6,5},{7,6},{8,11},{9,8},{10,9... | collective-permute-start | bytes 393224 | tf_op jit(solution)/shard_map/ppermute | solution.py:237
  149.3 5.5 %collective-permute-start.2 = (bf16[256,256]{1,0:T(8,128)(2,1)}, bf16[256,256]{1,0:T(8,128)(2,1)S(1)}, u32[]{:S(2)}, u32[]{:S(2)}) collective-permute-start(bf16[256,256]{1,0:T(8,128)(2,1)} %hidden_units.3.refs_0_.refs_7_), channel_id=1, source_target_pairs={{0,2},{1,3},{2,0},{3,1},{4,6},{5,7},{6,4},{7,5},{8,10},{9,11},{10,... | collective-permute-start | bytes 393224 | tf_op jit(solution)/shard_map/ppermute | solution.py:237
  160.6 39.9 %all-to-all-start.1 = ((bf16[64,4,1792]{2,1,0:T(4,128)(2,1)}), bf16[64,4,1792]{2,1,0:T(4,128)(2,1)S(1)}, u32[]{:S(2)}, u32[]{:S(2)}) async-start(bf16[64,4,1792]{2,1,0:T(4,128)(2,1)} %down.3), calls=%async_computation.1 | async-start | bytes 1835008 | tf_op jit(solution)/shard_map/all_to_all | solution.py:285
  179.7 9.6 %collective-permute-start.10 = (bf16[256,256]{1,0:T(8,128)(2,1)}, bf16[256,256]{1,0:T(8,128)(2,1)S(1)}, u32[]{:S(2)}, u32[]{:S(2)}) collective-permute-start(bf16[256,256]{1,0:T(8,128)(2,1)} %hidden_units.4.refs_0_.refs_3_), channel_id=1, source_target_pairs={{0,1},{1,2},{2,3},{3,0},{4,5},{5,6},{6,7},{7,4},{8,9},{9,10},{10,1... | collective-permute-start | bytes 393224 | tf_op jit(solution)/shard_map/ppermute | solution.py:237
  179.8 9.5 %collective-permute-start.11 = (bf16[256,256]{1,0:T(8,128)(2,1)}, bf16[256,256]{1,0:T(8,128)(2,1)S(1)}, u32[]{:S(2)}, u32[]{:S(2)}) collective-permute-start(bf16[256,256]{1,0:T(8,128)(2,1)} %hidden_units.4.refs_0_.refs_3_), channel_id=1, source_target_pairs={{0,3},{1,0},{2,1},{3,2},{4,7},{5,4},{6,5},{7,6},{8,11},{9,8},{10,9... | collective-permute-start | bytes 393224 | tf_op jit(solution)/shard_map/ppermute | solution.py:237
  182.4 12.5 %collective-permute-start.12 = (bf16[256,256]{1,0:T(8,128)(2,1)}, bf16[256,256]{1,0:T(8,128)(2,1)S(1)}, u32[]{:S(2)}, u32[]{:S(2)}) collective-permute-start(bf16[256,256]{1,0:T(8,128)(2,1)} %hidden_units.4.refs_0_.refs_3_), channel_id=1, source_target_pairs={{0,2},{1,3},{2,0},{3,1},{4,6},{5,7},{6,4},{7,5},{8,10},{9,11},{10,... | collective-permute-start | bytes 393224 | tf_op jit(solution)/shard_map/ppermute | solution.py:237
  200.5 36.0 %all-to-all-start.2 = ((bf16[64,4,1792]{2,1,0:T(4,128)(2,1)}), bf16[64,4,1792]{2,1,0:T(4,128)(2,1)S(1)}, u32[]{:S(2)}, u32[]{:S(2)}) async-start(bf16[64,4,1792]{2,1,0:T(4,128)(2,1)} %down.4), calls=%async_computation.2 | async-start | bytes 1835008 | tf_op jit(solution)/shard_map/all_to_all | solution.py:285
  217.6 5.9 %collective-permute-start.13 = (bf16[256,256]{1,0:T(8,128)(2,1)}, bf16[256,256]{1,0:T(8,128)(2,1)S(1)}, u32[]{:S(2)}, u32[]{:S(2)}) collective-permute-start(bf16[256,256]{1,0:T(8,128)(2,1)} %hidden_units.5.refs_0_), channel_id=1, source_target_pairs={{0,1},{1,2},{2,3},{3,0},{4,5},{5,6},{6,7},{7,4},{8,9},{9,10},{10,1... | collective-permute-start | bytes 393224 | tf_op jit(solution)/shard_map/ppermute | solution.py:237
  218.5 5.0 %collective-permute-start.14 = (bf16[256,256]{1,0:T(8,128)(2,1)}, bf16[256,256]{1,0:T(8,128)(2,1)S(1)}, u32[]{:S(2)}, u32[]{:S(2)}) collective-permute-start(bf16[256,256]{1,0:T(8,128)(2,1)} %hidden_units.5.refs_0_), channel_id=1, source_target_pairs={{0,3},{1,0},{2,1},{3,2},{4,7},{5,4},{6,5},{7,6},{8,11},{9,8},{10,9... | collective-permute-start | bytes 393224 | tf_op jit(solution)/shard_map/ppermute | solution.py:237
  220.4 5.8 %collective-permute-start.15 = (bf16[256,256]{1,0:T(8,128)(2,1)}, bf16[256,256]{1,0:T(8,128)(2,1)S(1)}, u32[]{:S(2)}, u32[]{:S(2)}) collective-permute-start(bf16[256,256]{1,0:T(8,128)(2,1)} %hidden_units.5.refs_0_), channel_id=1, source_target_pairs={{0,2},{1,3},{2,0},{3,1},{4,6},{5,7},{6,4},{7,5},{8,10},{9,11},{10,... | collective-permute-start | bytes 393224 | tf_op jit(solution)/shard_map/ppermute | solution.py:237
  236.5 32.3 %all-to-all-start.4 = ((bf16[64,4,1792]{2,1,0:T(4,128)(2,1)}), bf16[64,4,1792]{2,1,0:T(4,128)(2,1)S(1)}, u32[]{:S(2)}, u32[]{:S(2)}) async-start(bf16[64,4,1792]{2,1,0:T(4,128)(2,1)} %down.5), calls=%async_computation.4 | async-start | bytes 1835008 | tf_op jit(solution)/shard_map/all_to_all | solution.py:285
  (23 other events, 254.6 us)
Sparse Core Ops, SparseCore 0:
  75.7 65.2 all-gather.2
  142.8 51.3 all-gather.4

commit v6 on v4

--- a/solution.py
+++ b/solution.py
@@ -8,11 +8,11 @@
 from jax.sharding import PartitionSpec as P
 
 CAP = 12
-CHUNKS = ((0, 4, True), (4, 4, False), (8, 4, False))
+CHUNKS = ((0, 4, False), (4, 4, False), (8, 4, False))
 SENDS = (1, 3, 2)
 STEPS = (0, 3, 1, 2)
 TILES = 2
-TOLD = (100, 100, 1)
+TOLD = (1000, 100, 1)
 WAIT_TOLD = 200_000_000_000
 MIB = 1024 * 1024
 CORNER = pl.BlockSpec((16, 128), lambda *index: (0, 0))
@@ -268,11 +268,11 @@
     leaving[2] = outgoing(2, leaving[:1])
     for number, (first, count, by_permutes) in enumerate(CHUNKS):
         if number == 1:
-            leaving[1] = outgoing(1, [rows, leaving[2], wait_for(pieces, WAIT_TOLD)])
+            leaving[1] = outgoing(1, [rows, leaving[2]])
         rows = lax.all_to_all(leaving[number], "ep", split_axis=0, concat_axis=0, tiled=True)
         rows = rows.reshape(experts * count, width)
         if number == 1:
-            waited = wait_for([rows], WAIT_TOLD)
+            waited = wait_for([*pieces], WAIT_TOLD)
         if by_permutes:
             gathered.append([rows] + ring(rows))
         else:

time: 279 us -> 267 us (0.957)
  starting transfers between devices: 87.5 us -> 72.1 us
  waiting for transfers between devices: 112 us -> 117 us
    ppermute x16 -> x12, waiting for transfers between devices: 50.7 us -> 27.6 us  [send(): lax.ppermute(array, 'tp', [(i, (i + step) % parts) for i in range(parts)])]
    all_to_all x3, waiting for transfers between devices: 14.8 us -> 29.3 us  [on_device(): lax.all_to_all(leaving[number], 'ep', split_axis=0, concat_axis=0, tiled=...]
    all_gather x2 -> x3, waiting for transfers between devices: 25.1 us -> 38.7 us  [on_device(): lax.all_gather(rows, 'tp', tiled=True).reshape(parts, *rows.shape)]
    all_to_all x3, starting transfers between devices: 37.1 us -> 26.6 us  [on_device(): lax.all_to_all(leaving[number], 'ep', split_axis=0, concat_axis=0, tiled=...]
    ppermute x16 -> x12, starting transfers between devices: 20.1 us -> 13.2 us  [send(): lax.ppermute(array, 'tp', [(i, (i + step) % parts) for i in range(parts)])]
  transfers between devices with their start and end apart: 24 -> 21, of which waited for: 12 -> 14; matrix products, arithmetic and copies ran while one was open for 4% -> 6% of each run, Pallas kernels for 15% -> 15%
where the time goes in v6:
time: 267 us; the launch traced here: 266 us
  waiting for transfers between devices  117 us (44%)
  starting transfers between devices  72.1 us (27%)
  Pallas kernels  41.6 us (16%)
  local copies, waits for them, and re-layouts  15.3 us (6%)
  between operations  13.6 us (5%)
  matrix products  5.12 us (2%)
    all_gather x3, waiting for transfers between devices, on_device(): lax.all_gather(rows, 'tp', tiled=True).reshape(parts, *rows.shape)  38.7 us
    all_to_all x3, starting transfers between devices, on_device(): lax.all_to_all(outputs, 'ep', split_axis=0, concat_axis=0, tiled=True)  32.2 us
    all_to_all x3, waiting for transfers between devices, on_device(): lax.all_to_all(leaving[number], 'ep', split_axis=0, concat_axis=0, tiled=...  29.3 us
    ppermute x12, waiting for transfers between devices, send(): lax.ppermute(array, 'tp', [(i, (i + step) % parts) for i in range(parts)])  27.6 us
    all_to_all x3, starting transfers between devices, on_device(): lax.all_to_all(leaving[number], 'ep', split_axis=0, concat_axis=0, tiled=...  26.6 us
    all_to_all x3, waiting for transfers between devices, on_device(): lax.all_to_all(outputs, 'ep', split_axis=0, concat_axis=0, tiled=True)  21 us
    pallas_call x3, Pallas kernels, hidden_units(): pl.pallas_call(functools.partial(hidden_kernel, gathered, parts), grid_sp...  18.8 us
    pallas_call x3, Pallas kernels, down(): pl.pallas_call(functools.partial(down_kernel, parts), grid_spec=pltpu.Pre...  14.8 us
  transfers between devices with their start and end apart: 21, of which 14 were waited for; matrix products, arithmetic and copies ran while one was open for 6% of the time, Pallas kernels for 15%

profile of v6, /device:TPU:1, one launch (start us, length us, event | category | flops | bytes accessed | tf_op | source)
XLA Modules:
  0.0 265.7 jit_solution(18433507122962875656)
XLA Ops:
  11.4 13.3 %all-to-all-start = ((bf16[64,4,1792]{2,1,0:T(4,128)(2,1)}), bf16[64,4,1792]{2,1,0:T(4,128)(2,1)}, u32[]{:S(2)}, u32[]{:S(2)}) async-start(bf16[64,4,1792]{2,1,0:T(4,128)(2,1)} %place_rows.3.rest_0_), calls=%async_computation | async-start | bytes 1835008 | tf_op jit(solution)/shard_map/all_to_all | solution.py:272
  24.8 3.4 %dynamic-slice_bitcast_fusion = (bf16[256,1792]{1,0:T(8,128)(2,1)}, bf16[256,1792]{1,0:T(8,128)(2,1)}, bf16[256,1792]{1,0:T(8,128)(2,1)}) fusion(bf16[1,256,7168]{2,1,0:T(8,128)(2,1)} %param.11, s32[]{:T(128)S(6)} %select_n.61, s32[]{:T(128)S(6)} %select_n.59, s32[]{:T(128)S(6)} %select_n.57), kind=kLoop, calls=%fused_computation.14 | loop fusion | bytes 5505036 | tf_op jit(solution)/shard_map/dynamic_slice | solution.py:246
  34.7 15.2 %all-to-all-done = bf16[64,4,1792]{2,1,0:T(4,128)(2,1)} async-done(((bf16[64,4,1792]{2,1,0:T(4,128)(2,1)}), bf16[64,4,1792]{2,1,0:T(4,128)(2,1)}, u32[]{:S(2)}, u32[]{:S(2)}) %all-to-all-start) | async-done | bytes 917536 | tf_op jit(solution)/shard_map/all_to_all | solution.py:272
  54.6 6.6 %all-to-all-start.2 = ((bf16[64,4,1792]{2,1,0:T(4,128)(2,1)}), bf16[64,4,1792]{2,1,0:T(4,128)(2,1)}, u32[]{:S(2)}, u32[]{:S(2)}) async-start(bf16[64,4,1792]{2,1,0:T(4,128)(2,1)} %place_rows.5), calls=%async_computation.2 | async-start | bytes 1835008 | tf_op jit(solution)/shard_map/all_to_all | solution.py:272
  61.3 15.4 %collective-permute-done.2.refs_2_.refs_7_ = bf16[256,1792]{1,0:T(8,128)(2,1)S(1)} collective-permute-done((bf16[256,1792]{1,0:T(8,128)(2,1)}, bf16[256,1792]{1,0:T(8,128)(2,1)S(1)}, u32[]{:S(2)}, u32[]{:S(2)}) %collective-permute-start.2) | collective-permute-done | bytes 917536 | tf_op jit(solution)/shard_map/ppermute | solution.py:235
  79.0 7.5 %all-to-all-done.2 = bf16[64,4,1792]{2,1,0:T(4,128)(2,1)} async-done(((bf16[64,4,1792]{2,1,0:T(4,128)(2,1)}), bf16[64,4,1792]{2,1,0:T(4,128)(2,1)}, u32[]{:S(2)}, u32[]{:S(2)}) %all-to-all-start.2) | async-done | bytes 917536 | tf_op jit(solution)/shard_map/all_to_all | solution.py:272
  86.5 6.6 %all-to-all-start.4 = ((bf16[64,4,1792]{2,1,0:T(4,128)(2,1)}), bf16[64,4,1792]{2,1,0:T(4,128)(2,1)}, u32[]{:S(2)}, u32[]{:S(2)}) async-start(bf16[64,4,1792]{2,1,0:T(4,128)(2,1)} %place_rows.4.rest_1_), calls=%async_computation.4 | async-start | bytes 1835008 | tf_op jit(solution)/shard_map/all_to_all | solution.py:272
  95.7 6.9 %all-gather.4.cloned.1.call-done = bf16[1024,1792]{1,0:T(8,128)(2,1)} async-done(((bf16[256,1792]{1,0:T(8,128)(2,1)}), bf16[1024,1792]{1,0:T(8,128)(2,1)}) %all-gather.4.cloned.1.call-update) | async-done | bytes 3670032 | tf_op jit(solution)/shard_map/all_gather | solution.py:279
  102.6 6.3 %hidden_units.3.refs_0_.refs_3_ = bf16[256,256]{1,0:T(8,128)(2,1)} custom-call(s32[1]{0:T(128)} %bitcast.me_ref, bf16[4,256,1792]{2,1,0:T(8,128)(2,1)} %bitcast.51, bf16[4,1792,256]{2,1,0:T(8,128)(2,1)} %bitcast.42, bf16[4,1792,256]{2,1,0:T(8,128)(2,1)} %bitcast.45, bf16[16,128]{1,0:T(8,128)(2,1)} %wait_for.1.refs_3_), custom_call_target="tpu_custom_call" | custom-call | flops 1879048192000 | bytes 11141120 | tf_op jit(solution)/shard_map/hidden_units/pallas_call | solution.py:77
  111.8 6.5 %all-to-all-done.4 = bf16[64,4,1792]{2,1,0:T(4,128)(2,1)} async-done(((bf16[64,4,1792]{2,1,0:T(4,128)(2,1)}), bf16[64,4,1792]{2,1,0:T(4,128)(2,1)}, u32[]{:S(2)}, u32[]{:S(2)}) %all-to-all-start.4) | async-done | bytes 917536 | tf_op jit(solution)/shard_map/all_to_all | solution.py:272
  118.4 2.4 reshape.92
  121.6 4.9 %down.3 = bf16[64,4,1792]{2,1,0:T(4,128)(2,1)} custom-call(s32[1]{0:T(128)} %bitcast.me_ref, bf16[256,256]{1,0:T(8,128)(2,1)} %hidden_units.3.refs_0_.refs_3_, bf16[256,256]{1,0:T(8,128)(2,1)} %copy-done.7, bf16[256,256]{1,0:T(8,128)(2,1)} %copy-done.8, bf16[256,256]{1,0:T(8,128)(2,1)} %copy-done.9, bf16[256,7168]{1,0:T(8,128)(2,1)} %bitcast.39, ...), custom_call_target="tpu_custom_call" | custom-call | flops 939524096 | bytes 5111808 | tf_op jit(solution)/shard_map/down/pallas_call | solution.py:141
  126.5 8.5 %all-to-all-start.1 = ((bf16[64,4,1792]{2,1,0:T(4,128)(2,1)}), bf16[64,4,1792]{2,1,0:T(4,128)(2,1)}, u32[]{:S(2)}, u32[]{:S(2)}) async-start(bf16[64,4,1792]{2,1,0:T(4,128)(2,1)} %down.3), calls=%async_computation.1 | async-start | bytes 1835008 | tf_op jit(solution)/shard_map/all_to_all | solution.py:286
  134.9 15.9 %all-gather.6.cloned.1.call-done = bf16[1024,1792]{1,0:T(8,128)(2,1)} async-done(((bf16[256,1792]{1,0:T(8,128)(2,1)}), bf16[1024,1792]{1,0:T(8,128)(2,1)}) %all-gather.6.cloned.1.call-update) | async-done | bytes 3670032 | tf_op jit(solution)/shard_map/all_gather | solution.py:279
  150.8 6.3 %hidden_units.4.refs_0_.refs_3_ = bf16[256,256]{1,0:T(8,128)(2,1)} custom-call(s32[1]{0:T(128)} %bitcast.me_ref, bf16[4,256,1792]{2,1,0:T(8,128)(2,1)} %bitcast.50, bf16[4,1792,256]{2,1,0:T(8,128)(2,1)} %bitcast.43, bf16[4,1792,256]{2,1,0:T(8,128)(2,1)} %bitcast.46, bf16[256,256]{1,0:T(8,128)(2,1)} %hidden_units.3.refs_0_.refs_3_), custom_call_target="tpu_custom_call" | custom-call | flops 187904819200 | bytes 11141120 | tf_op jit(solution)/shard_map/hidden_units/pallas_call | solution.py:77
  160.3 2.6 collective-permute-done.6.refs_1_
  166.1 5.1 %down.4 = bf16[64,4,1792]{2,1,0:T(4,128)(2,1)} custom-call(s32[1]{0:T(128)} %bitcast.me_ref, bf16[256,256]{1,0:T(8,128)(2,1)} %hidden_units.4.refs_0_.refs_3_, bf16[256,256]{1,0:T(8,128)(2,1)} %copy-done.12, bf16[256,256]{1,0:T(8,128)(2,1)} %copy-done.14, bf16[256,256]{1,0:T(8,128)(2,1)} %copy-done.15, bf16[256,7168]{1,0:T(8,128)(2,1)} %bitcast.40, ...), custom_call_target="tpu_custom_call" | custom-call | flops 939524096 | bytes 5111808 | tf_op jit(solution)/shard_map/down/pallas_call | solution.py:141
  171.1 12.3 %all-to-all-start.3 = ((bf16[64,4,1792]{2,1,0:T(4,128)(2,1)}), bf16[64,4,1792]{2,1,0:T(4,128)(2,1)S(1)}, u32[]{:S(2)}, u32[]{:S(2)}) async-start(bf16[64,4,1792]{2,1,0:T(4,128)(2,1)} %down.4), calls=%async_computation.3 | async-start | bytes 1835008 | tf_op jit(solution)/shard_map/all_to_all | solution.py:286
  183.4 16.0 %all-gather.8.cloned.1.call-done = bf16[1024,1792]{1,0:T(8,128)(2,1)} async-done(((bf16[256,1792]{1,0:T(8,128)(2,1)}), bf16[1024,1792]{1,0:T(8,128)(2,1)}) %all-gather.8.cloned.1.call-update) | async-done | bytes 3670032 | tf_op jit(solution)/shard_map/all_gather | solution.py:279
  199.4 6.3 %hidden_units.5.refs_0_ = bf16[256,256]{1,0:T(8,128)(2,1)} custom-call(s32[1]{0:T(128)} %bitcast.me_ref, bf16[4,256,1792]{2,1,0:T(8,128)(2,1)} %bitcast.48, bf16[4,1792,256]{2,1,0:T(8,128)(2,1)} %bitcast.44, bf16[4,1792,256]{2,1,0:T(8,128)(2,1)} %bitcast.47, bf16[256,256]{1,0:T(8,128)(2,1)} %hidden_units.4.refs_0_.refs_3_), custom_call_target="tpu_custom_call" | custom-call | flops 1879048192 | bytes 11141120 | tf_op jit(solution)/shard_map/hidden_units/pallas_call | solution.py:77
  211.9 3.6 %collective-permute-done.9.refs_1_ = bf16[256,256]{1,0:T(8,128)(2,1)S(1)} collective-permute-done((bf16[256,256]{1,0:T(8,128)(2,1)}, bf16[256,256]{1,0:T(8,128)(2,1)S(1)}, u32[]{:S(2)}, u32[]{:S(2)}) %collective-permute-start.9) | collective-permute-done | bytes 131104 | tf_op jit(solution)/shard_map/ppermute | solution.py:235
  216.2 4.9 %down.5 = bf16[64,4,1792]{2,1,0:T(4,128)(2,1)} custom-call(s32[1]{0:T(128)} %bitcast.me_ref, bf16[256,256]{1,0:T(8,128)(2,1)} %hidden_units.5.refs_0_, bf16[256,256]{1,0:T(8,128)(2,1)} %copy-done.13, bf16[256,256]{1,0:T(8,128)(2,1)} %copy-done.10, bf16[256,256]{1,0:T(8,128)(2,1)} %copy-done.11, bf16[256,7168]{1,0:T(8,128)(2,1)} %bitcast.41, ...), custom_call_target="tpu_custom_call" | custom-call | flops 939524096 | bytes 5111808 | tf_op jit(solution)/shard_map/down/pallas_call | solution.py:141
  221.1 11.5 %all-to-all-start.5 = ((bf16[64,4,1792]{2,1,0:T(4,128)(2,1)}), bf16[64,4,1792]{2,1,0:T(4,128)(2,1)S(1)}, u32[]{:S(2)}, u32[]{:S(2)}) async-start(bf16[64,4,1792]{2,1,0:T(4,128)(2,1)} %down.5), calls=%async_computation.5 | async-start | bytes 1835008 | tf_op jit(solution)/shard_map/all_to_all | solution.py:286
  236.9 21.0 %all-to-all-done.5 = bf16[64,4,1792]{2,1,0:T(4,128)(2,1)S(1)} async-done(((bf16[64,4,1792]{2,1,0:T(4,128)(2,1)}), bf16[64,4,1792]{2,1,0:T(4,128)(2,1)S(1)}, u32[]{:S(2)}, u32[]{:S(2)}) %all-to-all-start.5) | async-done | bytes 917536 | tf_op jit(solution)/shard_map/all_to_all | solution.py:286
  (105 shorter events, 43.3 us)
Async XLA Ops:
  11.4 38.6 %all-to-all-start = ((bf16[64,4,1792]{2,1,0:T(4,128)(2,1)}), bf16[64,4,1792]{2,1,0:T(4,128)(2,1)}, u32[]{:S(2)}, u32[]{:S(2)}) async-start(bf16[64,4,1792]{2,1,0:T(4,128)(2,1)} %place_rows.3.rest_0_), calls=%async_computation | async-start | bytes 1835008 | tf_op jit(solution)/shard_map/all_to_all | solution.py:272
  24.7 77.8 %all-gather.4.cloned.1.call-start = ((), (), s32[]{:S(2)}) async-start(), calls=%async_computation.6 | async-start | bytes 4587520 | tf_op jit(solution)/shard_map/all_gather | solution.py:279
  28.2 33.0 %collective-permute-start = (bf16[256,1792]{1,0:T(8,128)(2,1)}, bf16[256,1792]{1,0:T(8,128)(2,1)S(1)}, u32[]{:S(2)}, u32[]{:S(2)}) collective-permute-start(bf16[256,1792]{1,0:T(8,128)(2,1)} %get-tuple-element.7), channel_id=1, source_target_pairs={{0,1},{1,2},{2,3},{3,0},{4,5},{5,6},{6,7},{7,4},{8,9},{9,10},{10,1... | collective-permute-start | bytes 2752520 | tf_op jit(solution)/shard_map/ppermute | solution.py:235
  29.5 31.8 %collective-permute-start.1 = (bf16[256,1792]{1,0:T(8,128)(2,1)}, bf16[256,1792]{1,0:T(8,128)(2,1)S(1)}, u32[]{:S(2)}, u32[]{:S(2)}) collective-permute-start(bf16[256,1792]{1,0:T(8,128)(2,1)} %get-tuple-element.6), channel_id=1, source_target_pairs={{0,3},{1,0},{2,1},{3,2},{4,7},{5,4},{6,5},{7,6},{8,11},{9,8},{10,9... | collective-permute-start | bytes 2752520 | tf_op jit(solution)/shard_map/ppermute | solution.py:235
  31.0 45.8 %collective-permute-start.2 = (bf16[256,1792]{1,0:T(8,128)(2,1)}, bf16[256,1792]{1,0:T(8,128)(2,1)S(1)}, u32[]{:S(2)}, u32[]{:S(2)}) collective-permute-start(bf16[256,1792]{1,0:T(8,128)(2,1)} %get-tuple-element.5), channel_id=1, source_target_pairs={{0,2},{1,3},{2,0},{3,1},{4,6},{5,7},{6,4},{7,5},{8,10},{9,11},{10,... | collective-permute-start | bytes 2752520 | tf_op jit(solution)/shard_map/ppermute | solution.py:235
  54.6 31.9 %all-to-all-start.2 = ((bf16[64,4,1792]{2,1,0:T(4,128)(2,1)}), bf16[64,4,1792]{2,1,0:T(4,128)(2,1)}, u32[]{:S(2)}, u32[]{:S(2)}) async-start(bf16[64,4,1792]{2,1,0:T(4,128)(2,1)} %place_rows.5), calls=%async_computation.2 | async-start | bytes 1835008 | tf_op jit(solution)/shard_map/all_to_all | solution.py:272
  86.5 31.9 %all-to-all-start.4 = ((bf16[64,4,1792]{2,1,0:T(4,128)(2,1)}), bf16[64,4,1792]{2,1,0:T(4,128)(2,1)}, u32[]{:S(2)}, u32[]{:S(2)}) async-start(bf16[64,4,1792]{2,1,0:T(4,128)(2,1)} %place_rows.4.rest_1_), calls=%async_computation.4 | async-start | bytes 1835008 | tf_op jit(solution)/shard_map/all_to_all | solution.py:272
  93.1 57.7 %all-gather.6.cloned.1.call-start = ((), (), s32[]{:S(2)}) async-start(), calls=%async_computation.7 | async-start | bytes 4587520 | tf_op jit(solution)/shard_map/all_gather | solution.py:279
  95.6 103.8 %all-gather.8.cloned.1.call-start = ((), (), s32[]{:S(2)}) async-start(), calls=%async_computation.8 | async-start | bytes 4587520 | tf_op jit(solution)/shard_map/all_gather | solution.py:279
  108.8 12.0 %collective-permute-start.3 = (bf16[256,256]{1,0:T(8,128)(2,1)}, bf16[256,256]{1,0:T(8,128)(2,1)S(1)}, u32[]{:S(2)}, u32[]{:S(2)}) collective-permute-start(bf16[256,256]{1,0:T(8,128)(2,1)} %hidden_units.3.refs_0_.refs_3_), channel_id=1, source_target_pairs={{0,1},{1,2},{2,3},{3,0},{4,5},{5,6},{6,7},{7,4},{8,9},{9,10},{10,1... | collective-permute-start | bytes 393224 | tf_op jit(solution)/shard_map/ppermute | solution.py:235
  109.8 11.1 %collective-permute-start.4 = (bf16[256,256]{1,0:T(8,128)(2,1)}, bf16[256,256]{1,0:T(8,128)(2,1)S(1)}, u32[]{:S(2)}, u32[]{:S(2)}) collective-permute-start(bf16[256,256]{1,0:T(8,128)(2,1)} %hidden_units.3.refs_0_.refs_3_), channel_id=1, source_target_pairs={{0,3},{1,0},{2,1},{3,2},{4,7},{5,4},{6,5},{7,6},{8,11},{9,8},{10,9... | collective-permute-start | bytes 393224 | tf_op jit(solution)/shard_map/ppermute | solution.py:235
  111.6 9.3 %collective-permute-start.5 = (bf16[256,256]{1,0:T(8,128)(2,1)}, bf16[256,256]{1,0:T(8,128)(2,1)S(1)}, u32[]{:S(2)}, u32[]{:S(2)}) collective-permute-start(bf16[256,256]{1,0:T(8,128)(2,1)} %hidden_units.3.refs_0_.refs_3_), channel_id=1, source_target_pairs={{0,2},{1,3},{2,0},{3,1},{4,6},{5,7},{6,4},{7,5},{8,10},{9,11},{10,... | collective-permute-start | bytes 393224 | tf_op jit(solution)/shard_map/ppermute | solution.py:235
  126.5 44.6 %all-to-all-start.1 = ((bf16[64,4,1792]{2,1,0:T(4,128)(2,1)}), bf16[64,4,1792]{2,1,0:T(4,128)(2,1)}, u32[]{:S(2)}, u32[]{:S(2)}) async-start(bf16[64,4,1792]{2,1,0:T(4,128)(2,1)} %down.3), calls=%async_computation.1 | async-start | bytes 1835008 | tf_op jit(solution)/shard_map/all_to_all | solution.py:286
  157.1 5.9 %collective-permute-start.6 = (bf16[256,256]{1,0:T(8,128)(2,1)}, bf16[256,256]{1,0:T(8,128)(2,1)S(1)}, u32[]{:S(2)}, u32[]{:S(2)}) collective-permute-start(bf16[256,256]{1,0:T(8,128)(2,1)} %hidden_units.4.refs_0_.refs_3_), channel_id=1, source_target_pairs={{0,1},{1,2},{2,3},{3,0},{4,5},{5,6},{6,7},{7,4},{8,9},{9,10},{10,1... | collective-permute-start | bytes 393224 | tf_op jit(solution)/shard_map/ppermute | solution.py:235
  157.7 5.9 %collective-permute-start.7 = (bf16[256,256]{1,0:T(8,128)(2,1)}, bf16[256,256]{1,0:T(8,128)(2,1)S(1)}, u32[]{:S(2)}, u32[]{:S(2)}) collective-permute-start(bf16[256,256]{1,0:T(8,128)(2,1)} %hidden_units.4.refs_0_.refs_3_), channel_id=1, source_target_pairs={{0,3},{1,0},{2,1},{3,2},{4,7},{5,4},{6,5},{7,6},{8,11},{9,8},{10,9... | collective-permute-start | bytes 393224 | tf_op jit(solution)/shard_map/ppermute | solution.py:235
  159.8 5.5 %collective-permute-start.8 = (bf16[256,256]{1,0:T(8,128)(2,1)}, bf16[256,256]{1,0:T(8,128)(2,1)S(1)}, u32[]{:S(2)}, u32[]{:S(2)}) collective-permute-start(bf16[256,256]{1,0:T(8,128)(2,1)} %hidden_units.4.refs_0_.refs_3_), channel_id=1, source_target_pairs={{0,2},{1,3},{2,0},{3,1},{4,6},{5,7},{6,4},{7,5},{8,10},{9,11},{10,... | collective-permute-start | bytes 393224 | tf_op jit(solution)/shard_map/ppermute | solution.py:235
  171.1 49.9 %all-to-all-start.3 = ((bf16[64,4,1792]{2,1,0:T(4,128)(2,1)}), bf16[64,4,1792]{2,1,0:T(4,128)(2,1)S(1)}, u32[]{:S(2)}, u32[]{:S(2)}) async-start(bf16[64,4,1792]{2,1,0:T(4,128)(2,1)} %down.4), calls=%async_computation.3 | async-start | bytes 1835008 | tf_op jit(solution)/shard_map/all_to_all | solution.py:286
  205.7 27.3 %copy-start.4 = (s32[64,64]{0,1:T(8,128)S(1)}, s32[64,64]{0,1:T(8,128)}, u32[]{:S(2)}) copy-start(s32[64,64]{0,1:T(8,128)} %copy-done.3) | copy-start | bytes 49156
  205.7 27.3 %copy-start.18 = (s32[4]{0:T(128)S(1)}, s32[4]{0:T(128)}, u32[]{:S(2)}) copy-start(s32[4]{0:T(128)} %copy-done.17) | copy-start | bytes 52
  205.7 27.3 %copy-start.20 = (s32[4]{0:T(128)S(1)}, s32[4]{0:T(128)}, u32[]{:S(2)}) copy-start(s32[4]{0:T(128)} %copy-done.19) | copy-start | bytes 52
  205.7 4.7 %collective-permute-start.10 = (bf16[256,256]{1,0:T(8,128)(2,1)}, bf16[256,256]{1,0:T(8,128)(2,1)S(1)}, u32[]{:S(2)}, u32[]{:S(2)}) collective-permute-start(bf16[256,256]{1,0:T(8,128)(2,1)} %hidden_units.5.refs_0_), channel_id=1, source_target_pairs={{0,3},{1,0},{2,1},{3,2},{4,7},{5,4},{6,5},{7,6},{8,11},{9,8},{10,9... | collective-permute-start | bytes 393224 | tf_op jit(solution)/shard_map/ppermute | solution.py:235
  206.4 5.5 %collective-permute-start.11 = (bf16[256,256]{1,0:T(8,128)(2,1)}, bf16[256,256]{1,0:T(8,128)(2,1)S(1)}, u32[]{:S(2)}, u32[]{:S(2)}) collective-permute-start(bf16[256,256]{1,0:T(8,128)(2,1)} %hidden_units.5.refs_0_), channel_id=1, source_target_pairs={{0,2},{1,3},{2,0},{3,1},{4,6},{5,7},{6,4},{7,5},{8,10},{9,11},{10,... | collective-permute-start | bytes 393224 | tf_op jit(solution)/shard_map/ppermute | solution.py:235
  208.1 7.5 %collective-permute-start.9 = (bf16[256,256]{1,0:T(8,128)(2,1)}, bf16[256,256]{1,0:T(8,128)(2,1)S(1)}, u32[]{:S(2)}, u32[]{:S(2)}) collective-permute-start(bf16[256,256]{1,0:T(8,128)(2,1)} %hidden_units.5.refs_0_), channel_id=1, source_target_pairs={{0,1},{1,2},{2,3},{3,0},{4,5},{5,6},{6,7},{7,4},{8,9},{9,10},{10,1... | collective-permute-start | bytes 393224 | tf_op jit(solution)/shard_map/ppermute | solution.py:235
  221.1 36.8 %all-to-all-start.5 = ((bf16[64,4,1792]{2,1,0:T(4,128)(2,1)}), bf16[64,4,1792]{2,1,0:T(4,128)(2,1)S(1)}, u32[]{:S(2)}, u32[]{:S(2)}) async-start(bf16[64,4,1792]{2,1,0:T(4,128)(2,1)} %down.5), calls=%async_computation.5 | async-start | bytes 1835008 | tf_op jit(solution)/shard_map/all_to_all | solution.py:286
  (18 other events, 166.4 us)
Sparse Core Ops, SparseCore 0:
  52.5 50.0 all-gather.3
  104.4 46.3 all-gather.5
  152.6 46.7 all-gather.7

commit v7 on v6

--- a/solution.py
+++ b/solution.py
@@ -8,7 +8,7 @@
 from jax.sharding import PartitionSpec as P
 
 CAP = 12
-CHUNKS = ((0, 4, False), (4, 4, False), (8, 4, False))
+CHUNKS = ((0, 4, 256), (4, 4, 256), (8, 4, 128))
 SENDS = (1, 3, 2)
 STEPS = (0, 3, 1, 2)
 TILES = 2
@@ -34,21 +34,21 @@
 
 
 def hidden_kernel(gathered, parts, me_ref, *refs):
-    arrays = 1 if gathered else parts + 1
-    xs, (gate_ref, up_ref) = refs[:arrays], refs[arrays:arrays + 2]
+    pieces = 1 if gathered == refs[-7].shape[0] else parts + 1
+    xs, (gate_ref, up_ref) = refs[:pieces], refs[pieces:pieces + 2]
     out_ref, x_buffer, gate_buffer, up_buffer, gate_sum, up_sum, arrivals = refs[-7:]
+    rest = x_buffer.shape[1] - gathered
     copies = []
-    for number, step in enumerate(range(parts) if gathered else STEPS):
-        part = step if gathered else lax.rem(me_ref[0] + step, parts)
-        pairs = [(gate_ref.at[part], gate_buffer.at[number]), (up_ref.at[part], up_buffer.at[number])]
-        if gathered:
-            pairs.append((xs[0].at[step], x_buffer.at[number]))
-        elif number < parts - 1:
-            pairs.append((xs[number], x_buffer.at[number]))
-        else:
-            half = x_buffer.shape[1] // 2
-            pairs.append((xs[number], x_buffer.at[number, pl.ds(0, half)]))
-            pairs.append((xs[number + 1], x_buffer.at[number, pl.ds(half, half)]))
+    for number, step in enumerate(STEPS):
+        part = lax.rem(me_ref[0] + step, parts)
+        pairs = [
+            (gate_ref.at[part], gate_buffer.at[number]),
+            (up_ref.at[part], up_buffer.at[number]),
+            (xs[0].at[part], x_buffer.at[number, pl.ds(0, gathered)]),
+        ]
+        if rest:
+            source = xs[1].at[pl.ds(gathered, rest)] if number == 0 else xs[1 + number]
+            pairs.append((source, x_buffer.at[number, pl.ds(gathered, rest)]))
         copies.append(
             [pltpu.make_async_copy(a, b, arrivals.at[number, i]) for i, (a, b) in enumerate(pairs)]
         )
@@ -71,15 +71,16 @@
 
 
 def hidden_units(me, xs, w_gate, w_up, after, told):
-    gathered = len(xs) == 1
     parts, width, hidden = w_gate.shape
-    rows = xs[0].shape[-2]
+    gathered = xs[0].shape[1]
+    rows = gathered if len(xs) == 1 else xs[1].shape[0]
     return pl.pallas_call(
         functools.partial(hidden_kernel, gathered, parts),
         grid_spec=pltpu.PrefetchScalarGridSpec(
             num_scalar_prefetch=1,
             grid=(1,),
-            in_specs=[IN_HBM] * (len(xs) + 2) + [CORNER] * len(after),
+            in_specs=[IN_HBM] * (len(xs) + 2)
+            + [CORNER if array.ndim == 2 else CORNER_SLOTS for array in after],
             out_specs=pl.BlockSpec((rows, hidden), lambda i, me: (0, 0)),
             scratch_shapes=[
                 pltpu.VMEM((parts, rows, width), jnp.bfloat16),
@@ -237,11 +238,6 @@
     def send_all(array):
         return [send(array, step) for step in SENDS]
 
-    def ring(rows):
-        half = rows.shape[0] // 2
-        left, right = send(rows, 1), send(rows, -1)
-        return [left, right, send(left[:half], 1), send(right[half:], -1)]
-
     slices = [
         lax.dynamic_slice_in_dim(w_down, (place + step) % parts * width, width, axis=1) for step in SENDS
     ]
@@ -260,27 +256,28 @@
         here = slot[:, :, None] == first + jnp.arange(count, dtype=jnp.int32)
         places.append(here.reshape(row_count, experts * count))
 
-    def outgoing(number, after):
-        return place_rows(places[number].astype(jnp.bfloat16), hidden_rows, experts, after, 1)
+    def outgoing(number, after, told=1):
+        return place_rows(places[number].astype(jnp.bfloat16), hidden_rows, experts, after, told)
 
     gathered = []
     leaving = [outgoing(0, []), None, None]
-    leaving[2] = outgoing(2, leaving[:1])
-    for number, (first, count, by_permutes) in enumerate(CHUNKS):
+    for number, (first, count, by_gather) in enumerate(CHUNKS):
         if number == 1:
-            leaving[1] = outgoing(1, [rows, leaving[2]])
+            leaving[1] = outgoing(1, [rows, *pieces[:2]], 3000)
+        if number == 2:
+            leaving[2] = outgoing(2, [rows])
         rows = lax.all_to_all(leaving[number], "ep", split_axis=0, concat_axis=0, tiled=True)
         rows = rows.reshape(experts * count, width)
         if number == 1:
-            waited = wait_for([*pieces], WAIT_TOLD)
-        if by_permutes:
-            gathered.append([rows] + ring(rows))
-        else:
-            gathered.append([lax.all_gather(rows, "tp", tiled=True).reshape(parts, *rows.shape)])
+            waited = wait_for([*pieces, rows], WAIT_TOLD)
+        head = lax.all_gather(rows[:by_gather], "tp", tiled=True).reshape(parts, by_gather, width)
+        gathered.append([head] + ([rows] + send_all(rows[by_gather:]) if by_gather < rows.shape[0] else []))
 
     mixed = jnp.zeros((row_count, width), jnp.float32)
-    for number, ((first, count, by_permutes), spot, x, told) in enumerate(zip(CHUNKS, places, gathered, TOLD)):
-        after = [activated] if number else [waited]
+    for number, ((first, count, _), spot, x, told) in enumerate(zip(CHUNKS, places, gathered, TOLD)):
+        after = [outputs] if number else [waited]
+        if number == 1:
+            after = after + gathered[number + 1][2:]
         activated = hidden_units(me, x, w_gate, w_up, after, told)
         outputs = down(me, [activated] + send_all(activated), w_down, pieces, experts)
         returned = lax.all_to_all(outputs, "ep", split_axis=0, concat_axis=0, tiled=True)

time: 267 us -> 308 us (1.15)
  waiting for transfers between devices: 117 us -> 144 us
  starting transfers between devices: 72.1 us -> 82.5 us
    all_gather x3, waiting for transfers between devices: 38.7 us -> 0.02 us  [on_device(): lax.all_gather(rows[:by_gather], 'tp', tiled=True)]
    ppermute x12 -> x15, waiting for transfers between devices: 27.6 us -> 64.9 us  [send(): lax.ppermute(array, 'tp', [(i, (i + step) % parts) for i in range(parts)])]
    all_to_all x3, waiting for transfers between devices: 29.3 us -> 57 us  [on_device(): lax.all_to_all(leaving[number], 'ep', split_axis=0, concat_axis=0, tiled=...]
    ppermute x12 -> x15, starting transfers between devices: 13.2 us -> 21.9 us  [send(): lax.ppermute(array, 'tp', [(i, (i + step) % parts) for i in range(parts)])]
    all_to_all x3, starting transfers between devices: 26.6 us -> 30.9 us  [on_device(): lax.all_to_all(leaving[number], 'ep', split_axis=0, concat_axis=0, tiled=...]
    slice x0 -> x3, local copies, waits for them, and re-layouts: none -> 4.03 us  [the longest x2 3.13 us: on_device(): rows[:by_gather]]
  transfers between devices with their start and end apart: 21 -> 24, of which waited for: 14 -> 13; matrix products, arithmetic and copies ran while one was open for 6% -> 5% of each run, Pallas kernels for 15% -> 13%
where the time goes in v7:
time: 308 us; the launch traced here: 307 us
  waiting for transfers between devices  144 us (47%)
  starting transfers between devices  82.5 us (27%)
  Pallas kernels  41.8 us (14%)
  local copies, waits for them, and re-layouts  18.1 us (6%)
  between operations  13.6 us (4%)
  matrix products  5.13 us (2%)
    ppermute x15, waiting for transfers between devices, send(): lax.ppermute(array, 'tp', [(i, (i + step) % parts) for i in range(parts)])  64.9 us
    all_to_all x3, waiting for transfers between devices, on_device(): lax.all_to_all(leaving[number], 'ep', split_axis=0, concat_axis=0, tiled=...  57 us
    all_to_all x3, starting transfers between devices, on_device(): lax.all_to_all(leaving[number], 'ep', split_axis=0, concat_axis=0, tiled=...  30.9 us
    all_to_all x3, starting transfers between devices, on_device(): lax.all_to_all(outputs, 'ep', split_axis=0, concat_axis=0, tiled=True)  29.6 us
    ppermute x15, starting transfers between devices, send(): lax.ppermute(array, 'tp', [(i, (i + step) % parts) for i in range(parts)])  21.9 us
    all_to_all x3, waiting for transfers between devices, on_device(): lax.all_to_all(outputs, 'ep', split_axis=0, concat_axis=0, tiled=True)  21.7 us
    pallas_call x3, Pallas kernels, hidden_units(): pl.pallas_call(functools.partial(hidden_kernel, gathered, parts), grid_sp...  19.1 us
    pallas_call x3, Pallas kernels, down(): pl.pallas_call(functools.partial(down_kernel, parts), grid_spec=pltpu.Pre...  14.6 us
  transfers between devices with their start and end apart: 24, of which 13 were waited for; matrix products, arithmetic and copies ran while one was open for 5% of the time, Pallas kernels for 13%

profile of v7, /device:TPU:1, one launch (start us, length us, event | category | flops | bytes accessed | tf_op | source)
XLA Modules:
  0.0 306.7 jit_solution(1298198116785753876)
XLA Ops:
  11.4 13.2 %all-to-all-start = ((bf16[64,4,1792]{2,1,0:T(4,128)(2,1)}), bf16[64,4,1792]{2,1,0:T(4,128)(2,1)S(1)}, u32[]{:S(2)}, u32[]{:S(2)}) async-start(bf16[64,4,1792]{2,1,0:T(4,128)(2,1)} %place_rows.3), calls=%async_computation | async-start | bytes 1835008 | tf_op jit(solution)/shard_map/all_to_all | solution.py:269
  24.7 3.4 %dynamic-slice_bitcast_fusion = (bf16[256,1792]{1,0:T(8,128)(2,1)}, bf16[256,1792]{1,0:T(8,128)(2,1)}, bf16[256,1792]{1,0:T(8,128)(2,1)}) fusion(bf16[1,256,7168]{2,1,0:T(8,128)(2,1)} %param.11, s32[]{:T(128)S(6)} %select_n.61, s32[]{:T(128)S(6)} %select_n.59, s32[]{:T(128)S(6)} %select_n.57), kind=kLoop, calls=%fused_computation.14 | loop fusion | bytes 5505036 | tf_op jit(solution)/shard_map/dynamic_slice | solution.py:242
  30.8 19.1 %all-to-all-done = bf16[64,4,1792]{2,1,0:T(4,128)(2,1)S(1)} async-done(((bf16[64,4,1792]{2,1,0:T(4,128)(2,1)}), bf16[64,4,1792]{2,1,0:T(4,128)(2,1)S(1)}, u32[]{:S(2)}, u32[]{:S(2)}) %all-to-all-start) | async-done | bytes 917536 | tf_op jit(solution)/shard_map/all_to_all | solution.py:269
  54.7 11.1 %all-to-all-start.1 = ((bf16[64,4,1792]{2,1,0:T(4,128)(2,1)}), bf16[64,4,1792]{2,1,0:T(4,128)(2,1)S(1)}, u32[]{:S(2)}, u32[]{:S(2)}) async-start(bf16[64,4,1792]{2,1,0:T(4,128)(2,1)} %place_rows.4), calls=%async_computation.1 | async-start | bytes 1835008 | tf_op jit(solution)/shard_map/all_to_all | solution.py:269
  67.9 23.1 %all-to-all-done.1 = bf16[64,4,1792]{2,1,0:T(4,128)(2,1)S(1)} async-done(((bf16[64,4,1792]{2,1,0:T(4,128)(2,1)}), bf16[64,4,1792]{2,1,0:T(4,128)(2,1)S(1)}, u32[]{:S(2)}, u32[]{:S(2)}) %all-to-all-start.1) | async-done | bytes 917536 | tf_op jit(solution)/shard_map/all_to_all | solution.py:269
  94.4 6.6 %all-to-all-start.3 = ((bf16[64,4,1792]{2,1,0:T(4,128)(2,1)}), bf16[64,4,1792]{2,1,0:T(4,128)(2,1)}, u32[]{:S(2)}, u32[]{:S(2)}) async-start(bf16[64,4,1792]{2,1,0:T(4,128)(2,1)} %place_rows.5), calls=%async_computation.3 | async-start | bytes 1835008 | tf_op jit(solution)/shard_map/all_to_all | solution.py:269
  101.9 7.5 %collective-permute-done.2.refs_2_.refs_7_ = bf16[256,1792]{1,0:T(8,128)(2,1)S(1)} collective-permute-done((bf16[256,1792]{1,0:T(8,128)(2,1)}, bf16[256,1792]{1,0:T(8,128)(2,1)S(1)}, u32[]{:S(2)}, u32[]{:S(2)}) %collective-permute-start.2) | collective-permute-done | bytes 917536 | tf_op jit(solution)/shard_map/ppermute | solution.py:236
  111.6 14.7 %all-to-all-done.3 = bf16[64,4,1792]{2,1,0:T(4,128)(2,1)} async-done(((bf16[64,4,1792]{2,1,0:T(4,128)(2,1)}), bf16[64,4,1792]{2,1,0:T(4,128)(2,1)}, u32[]{:S(2)}, u32[]{:S(2)}) %all-to-all-start.3) | async-done | bytes 917536 | tf_op jit(solution)/shard_map/all_to_all | solution.py:269
  133.0 6.3 %hidden_units.3.refs_0_ = bf16[256,256]{1,0:T(8,128)(2,1)} custom-call(s32[1]{0:T(128)} %bitcast.me_ref, bf16[4,256,1792]{2,1,0:T(8,128)(2,1)} %bitcast.51, bf16[4,1792,256]{2,1,0:T(8,128)(2,1)} %bitcast.42, bf16[4,1792,256]{2,1,0:T(8,128)(2,1)} %bitcast.45, bf16[16,128]{1,0:T(8,128)(2,1)} %wait_for.1.refs_3_), custom_call_target="tpu_custom_call" | custom-call | flops 1879048192000 | bytes 11141120 | tf_op jit(solution)/shard_map/hidden_units/pallas_call | solution.py:77
  142.3 33.0 %collective-permute-done.3.refs_1_ = bf16[256,256]{1,0:T(8,128)(2,1)S(1)} collective-permute-done((bf16[256,256]{1,0:T(8,128)(2,1)}, bf16[256,256]{1,0:T(8,128)(2,1)S(1)}, u32[]{:S(2)}, u32[]{:S(2)}) %collective-permute-start.3) | collective-permute-done | bytes 131104 | tf_op jit(solution)/shard_map/ppermute | solution.py:236
  178.5 6.2 %collective-permute-done.5.refs_3_ = bf16[256,256]{1,0:T(8,128)(2,1)S(1)} collective-permute-done((bf16[256,256]{1,0:T(8,128)(2,1)}, bf16[256,256]{1,0:T(8,128)(2,1)S(1)}, u32[]{:S(2)}, u32[]{:S(2)}) %collective-permute-start.5) | collective-permute-done | bytes 131104 | tf_op jit(solution)/shard_map/ppermute | solution.py:236
  185.3 4.9 %down.3.refs_3_ = bf16[64,4,1792]{2,1,0:T(4,128)(2,1)} custom-call(s32[1]{0:T(128)} %bitcast.me_ref, bf16[256,256]{1,0:T(8,128)(2,1)} %hidden_units.3.refs_0_, bf16[256,256]{1,0:T(8,128)(2,1)} %copy-done.8, bf16[256,256]{1,0:T(8,128)(2,1)} %copy-done.9, bf16[256,256]{1,0:T(8,128)(2,1)} %copy-done.11, bf16[256,7168]{1,0:T(8,128)(2,1)} %bitcast.39, ...), custom_call_target="tpu_custom_call" | custom-call | flops 939524096 | bytes 5111808 | tf_op jit(solution)/shard_map/down/pallas_call | solution.py:142
  190.3 8.0 %all-to-all-start.2 = ((bf16[64,4,1792]{2,1,0:T(4,128)(2,1)}), bf16[64,4,1792]{2,1,0:T(4,128)(2,1)}, u32[]{:S(2)}, u32[]{:S(2)}) async-start(bf16[64,4,1792]{2,1,0:T(4,128)(2,1)} %down.3.refs_3_), calls=%async_computation.2 | async-start | bytes 1835008 | tf_op jit(solution)/shard_map/all_to_all | solution.py:283
  198.3 6.5 %hidden_units.4.refs_0_ = bf16[256,256]{1,0:T(8,128)(2,1)} custom-call(s32[1]{0:T(128)} %bitcast.me_ref, bf16[4,256,1792]{2,1,0:T(8,128)(2,1)} %bitcast.50, bf16[4,1792,256]{2,1,0:T(8,128)(2,1)} %bitcast.43, bf16[4,1792,256]{2,1,0:T(8,128)(2,1)} %bitcast.46, bf16[64,4,1792]{2,1,0:T(4,128)(2,1)} %down.3.refs_3_, ...), custom_call_target="tpu_custom_call" | custom-call | flops 187904819200 | bytes 11141120 | tf_op jit(solution)/shard_map/hidden_units/pallas_call | solution.py:77
  204.9 3.5 %collective-permute-start.10 = (bf16[256,256]{1,0:T(8,128)(2,1)}, bf16[256,256]{1,0:T(8,128)(2,1)S(1)}, u32[]{:S(2)}, u32[]{:S(2)}) collective-permute-start(bf16[256,256]{1,0:T(8,128)(2,1)} %hidden_units.4.refs_0_), channel_id=1, source_target_pairs={{0,3},{1,0},{2,1},{3,2},{4,7},{5,4},{6,5},{7,6},{8,11},{9,8},{10,9... | collective-permute-start | bytes 393224 | tf_op jit(solution)/shard_map/ppermute | solution.py:236
  209.0 5.0 %collective-permute-done.10.refs_2_ = bf16[256,256]{1,0:T(8,128)(2,1)S(1)} collective-permute-done((bf16[256,256]{1,0:T(8,128)(2,1)}, bf16[256,256]{1,0:T(8,128)(2,1)S(1)}, u32[]{:S(2)}, u32[]{:S(2)}) %collective-permute-start.10) | collective-permute-done | bytes 131104 | tf_op jit(solution)/shard_map/ppermute | solution.py:236
  214.1 4.0 %collective-permute-done.11.refs_3_ = bf16[256,256]{1,0:T(8,128)(2,1)S(1)} collective-permute-done((bf16[256,256]{1,0:T(8,128)(2,1)}, bf16[256,256]{1,0:T(8,128)(2,1)S(1)}, u32[]{:S(2)}, u32[]{:S(2)}) %collective-permute-start.11) | collective-permute-done | bytes 131104 | tf_op jit(solution)/shard_map/ppermute | solution.py:236
  221.7 4.8 %down.4.refs_7_ = bf16[64,4,1792]{2,1,0:T(4,128)(2,1)} custom-call(s32[1]{0:T(128)} %bitcast.me_ref, bf16[256,256]{1,0:T(8,128)(2,1)} %hidden_units.4.refs_0_, bf16[256,256]{1,0:T(8,128)(2,1)} %copy-done.16, bf16[256,256]{1,0:T(8,128)(2,1)} %copy-done.13, bf16[256,256]{1,0:T(8,128)(2,1)} %copy-done.15, bf16[256,7168]{1,0:T(8,128)(2,1)} %bitcast.40, ...), custom_call_target="tpu_custom_call" | custom-call | flops 939524096 | bytes 5111808 | tf_op jit(solution)/shard_map/down/pallas_call | solution.py:142
  226.6 11.1 %all-to-all-start.4 = ((bf16[64,4,1792]{2,1,0:T(4,128)(2,1)}), bf16[64,4,1792]{2,1,0:T(4,128)(2,1)S(1)}, u32[]{:S(2)}, u32[]{:S(2)}) async-start(bf16[64,4,1792]{2,1,0:T(4,128)(2,1)} %down.4.refs_7_), calls=%async_computation.4 | async-start | bytes 1835008 | tf_op jit(solution)/shard_map/all_to_all | solution.py:283
  240.1 6.3 %hidden_units.5.refs_0_ = bf16[256,256]{1,0:T(8,128)(2,1)} custom-call(s32[1]{0:T(128)} %bitcast.me_ref, bf16[4,128,1792]{2,1,0:T(8,128)(2,1)} %bitcast.48, bf16[256,1792]{1,0:T(8,128)(2,1)} %reshape.95.refs_1_, bf16[128,1792]{1,0:T(8,128)(2,1)} %collective-permute-done.6.refs_4_.refs_2_, bf16[128,1792]{1,0:T(8,128)(2,1)} %collective-permute-done.7.refs_5_.refs_3_, ...), custom_call_target="tpu_custom_call" | custom-call | flops 1879048192 | bytes 11141120 | tf_op jit(solution)/shard_map/hidden_units/pallas_call | solution.py:77
  252.8 4.0 %collective-permute-done.14.refs_3_ = bf16[256,256]{1,0:T(8,128)(2,1)S(1)} collective-permute-done((bf16[256,256]{1,0:T(8,128)(2,1)}, bf16[256,256]{1,0:T(8,128)(2,1)S(1)}, u32[]{:S(2)}, u32[]{:S(2)}) %collective-permute-start.14) | collective-permute-done | bytes 131104 | tf_op jit(solution)/shard_map/ppermute | solution.py:236
  257.4 4.9 %down.5 = bf16[64,4,1792]{2,1,0:T(4,128)(2,1)} custom-call(s32[1]{0:T(128)} %bitcast.me_ref, bf16[256,256]{1,0:T(8,128)(2,1)} %hidden_units.5.refs_0_, bf16[256,256]{1,0:T(8,128)(2,1)} %copy-done.10, bf16[256,256]{1,0:T(8,128)(2,1)} %copy-done.12, bf16[256,256]{1,0:T(8,128)(2,1)} %copy-done.14, bf16[256,7168]{1,0:T(8,128)(2,1)} %bitcast.41, ...), custom_call_target="tpu_custom_call" | custom-call | flops 939524096 | bytes 5111808 | tf_op jit(solution)/shard_map/down/pallas_call | solution.py:142
  263.0 10.5 %all-to-all-start.5 = ((bf16[64,4,1792]{2,1,0:T(4,128)(2,1)}), bf16[64,4,1792]{2,1,0:T(4,128)(2,1)S(1)}, u32[]{:S(2)}, u32[]{:S(2)}) async-start(bf16[64,4,1792]{2,1,0:T(4,128)(2,1)} %down.5), calls=%async_computation.5 | async-start | bytes 1835008 | tf_op jit(solution)/shard_map/all_to_all | solution.py:283
  277.9 21.0 %all-to-all-done.5 = bf16[64,4,1792]{2,1,0:T(4,128)(2,1)S(1)} async-done(((bf16[64,4,1792]{2,1,0:T(4,128)(2,1)}), bf16[64,4,1792]{2,1,0:T(4,128)(2,1)S(1)}, u32[]{:S(2)}, u32[]{:S(2)}) %all-to-all-start.5) | async-done | bytes 917536 | tf_op jit(solution)/shard_map/all_to_all | solution.py:283
  (116 shorter events, 54.4 us)
Async XLA Ops:
  11.4 38.5 %all-to-all-start = ((bf16[64,4,1792]{2,1,0:T(4,128)(2,1)}), bf16[64,4,1792]{2,1,0:T(4,128)(2,1)S(1)}, u32[]{:S(2)}, u32[]{:S(2)}) async-start(bf16[64,4,1792]{2,1,0:T(4,128)(2,1)} %place_rows.3), calls=%async_computation | async-start | bytes 1835008 | tf_op jit(solution)/shard_map/all_to_all | solution.py:269
  24.6 108.4 %all-gather.4.cloned.1.call-start = ((), (), s32[]{:S(2)}) async-start(), calls=%async_computation.6 | async-start | bytes 4587520 | tf_op jit(solution)/shard_map/all_gather | solution.py:273
  28.1 23.0 %collective-permute-start = (bf16[256,1792]{1,0:T(8,128)(2,1)}, bf16[256,1792]{1,0:T(8,128)(2,1)S(1)}, u32[]{:S(2)}, u32[]{:S(2)}) collective-permute-start(bf16[256,1792]{1,0:T(8,128)(2,1)} %get-tuple-element.7), channel_id=1, source_target_pairs={{0,1},{1,2},{2,3},{3,0},{4,5},{5,6},{6,7},{7,4},{8,9},{9,10},{10,1... | collective-permute-start | bytes 2752520 | tf_op jit(solution)/shard_map/ppermute | solution.py:236
  29.3 21.8 %collective-permute-start.1 = (bf16[256,1792]{1,0:T(8,128)(2,1)}, bf16[256,1792]{1,0:T(8,128)(2,1)S(1)}, u32[]{:S(2)}, u32[]{:S(2)}) collective-permute-start(bf16[256,1792]{1,0:T(8,128)(2,1)} %get-tuple-element.6), channel_id=1, source_target_pairs={{0,3},{1,0},{2,1},{3,2},{4,7},{5,4},{6,5},{7,6},{8,11},{9,8},{10,9... | collective-permute-start | bytes 2752520 | tf_op jit(solution)/shard_map/ppermute | solution.py:236
  54.7 36.4 %all-to-all-start.1 = ((bf16[64,4,1792]{2,1,0:T(4,128)(2,1)}), bf16[64,4,1792]{2,1,0:T(4,128)(2,1)S(1)}, u32[]{:S(2)}, u32[]{:S(2)}) async-start(bf16[64,4,1792]{2,1,0:T(4,128)(2,1)} %place_rows.4), calls=%async_computation.1 | async-start | bytes 1835008 | tf_op jit(solution)/shard_map/all_to_all | solution.py:269
  65.8 43.6 %collective-permute-start.2 = (bf16[256,1792]{1,0:T(8,128)(2,1)}, bf16[256,1792]{1,0:T(8,128)(2,1)S(1)}, u32[]{:S(2)}, u32[]{:S(2)}) collective-permute-start(bf16[256,1792]{1,0:T(8,128)(2,1)} %get-tuple-element.5), channel_id=1, source_target_pairs={{0,2},{1,3},{2,0},{3,1},{4,6},{5,7},{6,4},{7,5},{8,10},{9,11},{10,... | collective-permute-start | bytes 2752520 | tf_op jit(solution)/shard_map/ppermute | solution.py:236
  94.4 31.9 %all-to-all-start.3 = ((bf16[64,4,1792]{2,1,0:T(4,128)(2,1)}), bf16[64,4,1792]{2,1,0:T(4,128)(2,1)}, u32[]{:S(2)}, u32[]{:S(2)}) async-start(bf16[64,4,1792]{2,1,0:T(4,128)(2,1)} %place_rows.5), calls=%async_computation.3 | async-start | bytes 1835008 | tf_op jit(solution)/shard_map/all_to_all | solution.py:269
  101.1 97.3 %all-gather.6.cloned.1.call-start = ((), (), s32[]{:S(2)}) async-start(), calls=%async_computation.7 | async-start | bytes 4587520 | tf_op jit(solution)/shard_map/all_gather | solution.py:273
  101.8 138.3 %all-gather.8.cloned.1.call-start = ((), (), s32[]{:S(2)}) async-start(), calls=%async_computation.8 | async-start | bytes 2293760 | tf_op jit(solution)/shard_map/all_gather | solution.py:273
  129.5 68.8 %collective-permute-start.6 = (bf16[128,1792]{1,0:T(8,128)(2,1)}, bf16[128,1792]{1,0:T(8,128)(2,1)}, u32[]{:S(2)}, u32[]{:S(2)}) collective-permute-start(bf16[128,1792]{1,0:T(8,128)(2,1)} %slice.13), channel_id=1, source_target_pairs={{0,1},{1,2},{2,3},{3,0},{4,5},{5,6},{6,7},{7,4},{8,9},{9,10},{10,1... | collective-permute-start | bytes 1376264 | tf_op jit(solution)/shard_map/ppermute | solution.py:236
  130.3 68.0 %collective-permute-start.7 = (bf16[128,1792]{1,0:T(8,128)(2,1)}, bf16[128,1792]{1,0:T(8,128)(2,1)}, u32[]{:S(2)}, u32[]{:S(2)}) collective-permute-start(bf16[128,1792]{1,0:T(8,128)(2,1)} %slice.13), channel_id=1, source_target_pairs={{0,3},{1,0},{2,1},{3,2},{4,7},{5,4},{6,5},{7,6},{8,11},{9,8},{10,9... | collective-permute-start | bytes 1376264 | tf_op jit(solution)/shard_map/ppermute | solution.py:236
  132.1 66.2 %collective-permute-start.8 = (bf16[128,1792]{1,0:T(8,128)(2,1)}, bf16[128,1792]{1,0:T(8,128)(2,1)}, u32[]{:S(2)}, u32[]{:S(2)}) collective-permute-start(bf16[128,1792]{1,0:T(8,128)(2,1)} %slice.13), channel_id=1, source_target_pairs={{0,2},{1,3},{2,0},{3,1},{4,6},{5,7},{6,4},{7,5},{8,10},{9,11},{10,... | collective-permute-start | bytes 1376264 | tf_op jit(solution)/shard_map/ppermute | solution.py:236
  139.3 35.9 %collective-permute-start.3 = (bf16[256,256]{1,0:T(8,128)(2,1)}, bf16[256,256]{1,0:T(8,128)(2,1)S(1)}, u32[]{:S(2)}, u32[]{:S(2)}) collective-permute-start(bf16[256,256]{1,0:T(8,128)(2,1)} %hidden_units.3.refs_0_), channel_id=1, source_target_pairs={{0,1},{1,2},{2,3},{3,0},{4,5},{5,6},{6,7},{7,4},{8,9},{9,10},{10,1... | collective-permute-start | bytes 393224 | tf_op jit(solution)/shard_map/ppermute | solution.py:236
  140.4 38.1 %collective-permute-start.4 = (bf16[256,256]{1,0:T(8,128)(2,1)}, bf16[256,256]{1,0:T(8,128)(2,1)S(1)}, u32[]{:S(2)}, u32[]{:S(2)}) collective-permute-start(bf16[256,256]{1,0:T(8,128)(2,1)} %hidden_units.3.refs_0_), channel_id=1, source_target_pairs={{0,3},{1,0},{2,1},{3,2},{4,7},{5,4},{6,5},{7,6},{8,11},{9,8},{10,9... | collective-permute-start | bytes 393224 | tf_op jit(solution)/shard_map/ppermute | solution.py:236
  175.3 9.4 %collective-permute-start.5 = (bf16[256,256]{1,0:T(8,128)(2,1)}, bf16[256,256]{1,0:T(8,128)(2,1)S(1)}, u32[]{:S(2)}, u32[]{:S(2)}) collective-permute-start(bf16[256,256]{1,0:T(8,128)(2,1)} %hidden_units.3.refs_0_), channel_id=1, source_target_pairs={{0,2},{1,3},{2,0},{3,1},{4,6},{5,7},{6,4},{7,5},{8,10},{9,11},{10,... | collective-permute-start | bytes 393224 | tf_op jit(solution)/shard_map/ppermute | solution.py:236
  190.3 36.3 %all-to-all-start.2 = ((bf16[64,4,1792]{2,1,0:T(4,128)(2,1)}), bf16[64,4,1792]{2,1,0:T(4,128)(2,1)}, u32[]{:S(2)}, u32[]{:S(2)}) async-start(bf16[64,4,1792]{2,1,0:T(4,128)(2,1)} %down.3.refs_3_), calls=%async_computation.2 | async-start | bytes 1835008 | tf_op jit(solution)/shard_map/all_to_all | solution.py:283
  204.9 9.2 %collective-permute-start.10 = (bf16[256,256]{1,0:T(8,128)(2,1)}, bf16[256,256]{1,0:T(8,128)(2,1)S(1)}, u32[]{:S(2)}, u32[]{:S(2)}) collective-permute-start(bf16[256,256]{1,0:T(8,128)(2,1)} %hidden_units.4.refs_0_), channel_id=1, source_target_pairs={{0,3},{1,0},{2,1},{3,2},{4,7},{5,4},{6,5},{7,6},{8,11},{9,8},{10,9... | collective-permute-start | bytes 393224 | tf_op jit(solution)/shard_map/ppermute | solution.py:236
  208.4 9.7 %collective-permute-start.11 = (bf16[256,256]{1,0:T(8,128)(2,1)}, bf16[256,256]{1,0:T(8,128)(2,1)S(1)}, u32[]{:S(2)}, u32[]{:S(2)}) collective-permute-start(bf16[256,256]{1,0:T(8,128)(2,1)} %hidden_units.4.refs_0_), channel_id=1, source_target_pairs={{0,2},{1,3},{2,0},{3,1},{4,6},{5,7},{6,4},{7,5},{8,10},{9,11},{10,... | collective-permute-start | bytes 393224 | tf_op jit(solution)/shard_map/ppermute | solution.py:236
  208.8 12.3 %collective-permute-start.9 = (bf16[256,256]{1,0:T(8,128)(2,1)}, bf16[256,256]{1,0:T(8,128)(2,1)S(1)}, u32[]{:S(2)}, u32[]{:S(2)}) collective-permute-start(bf16[256,256]{1,0:T(8,128)(2,1)} %hidden_units.4.refs_0_), channel_id=1, source_target_pairs={{0,1},{1,2},{2,3},{3,0},{4,5},{5,6},{6,7},{7,4},{8,9},{9,10},{10,1... | collective-permute-start | bytes 393224 | tf_op jit(solution)/shard_map/ppermute | solution.py:236
  226.6 36.4 %all-to-all-start.4 = ((bf16[64,4,1792]{2,1,0:T(4,128)(2,1)}), bf16[64,4,1792]{2,1,0:T(4,128)(2,1)S(1)}, u32[]{:S(2)}, u32[]{:S(2)}) async-start(bf16[64,4,1792]{2,1,0:T(4,128)(2,1)} %down.4.refs_7_), calls=%async_computation.4 | async-start | bytes 1835008 | tf_op jit(solution)/shard_map/all_to_all | solution.py:283
  246.4 6.3 %collective-permute-start.12 = (bf16[256,256]{1,0:T(8,128)(2,1)}, bf16[256,256]{1,0:T(8,128)(2,1)S(1)}, u32[]{:S(2)}, u32[]{:S(2)}) collective-permute-start(bf16[256,256]{1,0:T(8,128)(2,1)} %hidden_units.5.refs_0_), channel_id=1, source_target_pairs={{0,1},{1,2},{2,3},{3,0},{4,5},{5,6},{6,7},{7,4},{8,9},{9,10},{10,1... | collective-permute-start | bytes 393224 | tf_op jit(solution)/shard_map/ppermute | solution.py:236
  248.1 4.7 %collective-permute-start.13 = (bf16[256,256]{1,0:T(8,128)(2,1)}, bf16[256,256]{1,0:T(8,128)(2,1)S(1)}, u32[]{:S(2)}, u32[]{:S(2)}) collective-permute-start(bf16[256,256]{1,0:T(8,128)(2,1)} %hidden_units.5.refs_0_), channel_id=1, source_target_pairs={{0,3},{1,0},{2,1},{3,2},{4,7},{5,4},{6,5},{7,6},{8,11},{9,8},{10,9... | collective-permute-start | bytes 393224 | tf_op jit(solution)/shard_map/ppermute | solution.py:236
  249.5 7.3 %collective-permute-start.14 = (bf16[256,256]{1,0:T(8,128)(2,1)}, bf16[256,256]{1,0:T(8,128)(2,1)S(1)}, u32[]{:S(2)}, u32[]{:S(2)}) collective-permute-start(bf16[256,256]{1,0:T(8,128)(2,1)} %hidden_units.5.refs_0_), channel_id=1, source_target_pairs={{0,2},{1,3},{2,0},{3,1},{4,6},{5,7},{6,4},{7,5},{8,10},{9,11},{10,... | collective-permute-start | bytes 393224 | tf_op jit(solution)/shard_map/ppermute | solution.py:236
  263.0 35.9 %all-to-all-start.5 = ((bf16[64,4,1792]{2,1,0:T(4,128)(2,1)}), bf16[64,4,1792]{2,1,0:T(4,128)(2,1)S(1)}, u32[]{:S(2)}, u32[]{:S(2)}) async-start(bf16[64,4,1792]{2,1,0:T(4,128)(2,1)} %down.5), calls=%async_computation.5 | async-start | bytes 1835008 | tf_op jit(solution)/shard_map/all_to_all | solution.py:283
  (22 other events, 234.4 us)
Sparse Core Ops, SparseCore 0:
  51.2 63.1 all-gather.3
  116.2 72.2 all-gather.5
  190.3 33.5 all-gather.7

commit v8 on v2

--- a/solution.py
+++ b/solution.py
@@ -8,19 +8,24 @@
 from jax.sharding import PartitionSpec as P
 
 CAP = 12
-CHUNKS = ((0, 4, False), (4, 4, True), (8, 4, False))
+DISPATCHES = ((0, 4), (4, 4), (8, 4))
+CHUNKS = ((0, 4), (4, 4), (8, 2), (10, 2))
 SENDS = (1, 3, 2)
-STEPS = (0, 3, 1, 2)
 TILES = 2
-TOLD = (100, 100, 1)
+TOLD = (3000, 300, 30, 1)
 WAIT_TOLD = 200_000_000_000
 MIB = 1024 * 1024
 CORNER = pl.BlockSpec((16, 128), lambda *index: (0, 0))
 IN_HBM = pl.BlockSpec(memory_space=pltpu.HBM)
-CORNER_SLOTS = pl.BlockSpec((8, 4, 128), lambda *index: (0, 0, 0))
 
 
 route_scale = 2.5
+
+
+def corner(array):
+    if array.ndim == 2:
+        return CORNER
+    return pl.BlockSpec((8, array.shape[1], 128), lambda *index: (0, 0, 0))
 
 
 def store_slots(out_ref, total):
@@ -33,21 +38,18 @@
     return gate / (1.0 + jnp.exp(-gate)) * up
 
 
-def hidden_kernel(gathered, parts, me_ref, *refs):
-    arrays = 1 if gathered else parts
-    xs, (gate_ref, up_ref) = refs[:arrays], refs[arrays:arrays + 2]
+def hidden_kernel(parts, me_ref, *refs):
+    x_ref, gate_ref, up_ref = refs[:3]
     out_ref, x_buffer, gate_buffer, up_buffer, gate_sum, up_sum, arrivals = refs[-7:]
     copies = []
-    for number, step in enumerate(range(parts) if gathered else STEPS):
-        part = step if gathered else lax.rem(me_ref[0] + step, parts)
-        x_part = xs[0].at[step] if gathered else xs[number]
+    for part in range(parts):
         pairs = (
-            (x_part, x_buffer.at[number]),
-            (gate_ref.at[part], gate_buffer.at[number]),
-            (up_ref.at[part], up_buffer.at[number]),
+            (gate_ref.at[part], gate_buffer.at[part]),
+            (up_ref.at[part], up_buffer.at[part]),
+            (x_ref.at[part], x_buffer.at[part]),
         )
         copies.append(
-            [pltpu.make_async_copy(a, b, arrivals.at[number, i]) for i, (a, b) in enumerate(pairs)]
+            [pltpu.make_async_copy(a, b, arrivals.at[part, i]) for i, (a, b) in enumerate(pairs)]
         )
         for copy in copies[-1]:
             copy.start()
@@ -67,16 +69,15 @@
             out_ref[...] = silu_times(gate_sum[...] + gate_part, up_sum[...] + up_part).astype(out_ref.dtype)
 
 
-def hidden_units(me, xs, w_gate, w_up, after, told):
-    gathered = len(xs) == 1
-    parts, width, hidden = w_gate.shape
-    rows = xs[0].shape[-2]
+def hidden_units(me, x, w_gate, w_up, after, told):
+    parts, rows, width = x.shape
+    hidden = w_gate.shape[2]
     return pl.pallas_call(
-        functools.partial(hidden_kernel, gathered, parts),
+        functools.partial(hidden_kernel, parts),
         grid_spec=pltpu.PrefetchScalarGridSpec(
             num_scalar_prefetch=1,
             grid=(1,),
-            in_specs=[IN_HBM] * (len(xs) + 2) + [CORNER] * len(after),
+            in_specs=[IN_HBM] * 3 + [corner(array) for array in after],
             out_specs=pl.BlockSpec((rows, hidden), lambda i, me: (0, 0)),
             scratch_shapes=[
                 pltpu.VMEM((parts, rows, width), jnp.bfloat16),
@@ -95,7 +96,7 @@
             transcendentals=rows * hidden,
         ),
         name="hidden_units",
-    )(me, *xs, w_gate, w_up, *after)
+    )(me, x, w_gate, w_up, *after)
 
 
 def down_kernel(parts, me_ref, *refs):
@@ -186,7 +187,7 @@
     return pl.pallas_call(
         wait_kernel,
         grid=(1,),
-        in_specs=[CORNER if array.ndim == 2 else CORNER_SLOTS for array in arrays],
+        in_specs=[corner(array) for array in arrays],
         out_specs=CORNER,
         out_shape=jax.ShapeDtypeStruct((16, 128), jnp.bfloat16),
         cost_estimate=pl.CostEstimate(flops=told, bytes_accessed=0, transcendentals=0),
@@ -204,7 +205,7 @@
             pl.BlockSpec((rows.shape[0], slots), lambda i: (0, 0)),
             pl.BlockSpec((rows.shape[0], width), lambda i: (0, 0)),
         ]
-        + [CORNER if array.ndim == 2 else CORNER_SLOTS for array in after],
+        + [corner(array) for array in after],
         out_specs=IN_HBM,
         scratch_shapes=[pltpu.VMEM(shape, jnp.bfloat16), pltpu.SemaphoreType.DMA((TILES,))],
         out_shape=jax.ShapeDtypeStruct(shape, jnp.bfloat16),
@@ -247,27 +248,37 @@
     slot = jnp.dot(earlier, chosen.astype(jnp.bfloat16), preferred_element_type=jnp.float32).astype(jnp.int32)
     slot = jnp.where(chosen, slot, CAP)
 
-    places, gathered = [], []
-    for number, (first, count, by_permutes) in enumerate(CHUNKS):
+    def spots(first, count):
         here = slot[:, :, None] == first + jnp.arange(count, dtype=jnp.int32)
-        places.append(here.reshape(row_count, experts * count))
-        after = slices if number == 0 else [before] if number == 1 else [before, waited]
-        outgoing = place_rows(places[-1].astype(jnp.bfloat16), hidden_rows, experts, after, 1)
-        rows = lax.all_to_all(outgoing, "ep", split_axis=0, concat_axis=0, tiled=True)
-        if number == 0:
-            waited = wait_for([*pieces, rows], WAIT_TOLD)
-        before = rows
-        rows = rows.reshape(experts * count, width)
-        gathered.append([rows] + send_all(rows) if by_permutes else lax.all_gather(rows, "tp"))
-
+        return here.reshape(row_count, experts * count)
+
+    def outgoing(number, after):
+        return place_rows(spots(*DISPATCHES[number]).astype(jnp.bfloat16), hidden_rows, experts, after, 1)
+
+    gathered = []
+    leaving = [outgoing(0, []), None, None]
+    leaving[2] = outgoing(2, leaving[:1])
+    for number, (first, count) in enumerate(DISPATCHES):
+        if number == 1:
+            leaving[1] = outgoing(1, [rows, leaving[2]])
+        arrived = lax.all_to_all(leaving[number], "ep", split_axis=0, concat_axis=0, tiled=True)
+        if number == 1:
+            waited = wait_for([*pieces], WAIT_TOLD)
+        for start, slots in CHUNKS:
+            if first <= start < first + count:
+                rows = arrived[:, start - first:start - first + slots].reshape(experts * slots, width)
+                gathered.append(lax.all_gather(rows, "tp", tiled=True).reshape(parts, *rows.shape))
+
+    back = []
     mixed = jnp.zeros((row_count, width), jnp.float32)
-    for number, ((first, count, by_permutes), spot, x, told) in enumerate(zip(CHUNKS, places, gathered, TOLD)):
-        after = [activated] if number else []
-        activated = hidden_units(me, x if by_permutes else [x], w_gate, w_up, after, told)
+    for number, ((first, count), x, told) in enumerate(zip(CHUNKS, gathered, TOLD)):
+        after = [outputs] + (back[number - 2:number - 1] if number > 1 else []) if number else [waited]
+        activated = hidden_units(me, x, w_gate, w_up, after, told)
         outputs = down(me, [activated] + send_all(activated), w_down, pieces, experts)
         returned = lax.all_to_all(outputs, "ep", split_axis=0, concat_axis=0, tiled=True)
+        back.append(returned)
         returned = returned.reshape(experts * count, width)
-        mix = jnp.where(spot, jnp.repeat(weight, count, axis=1), 0.0)
+        mix = jnp.where(spots(first, count), jnp.repeat(weight, count, axis=1), 0.0)
         high = mix.astype(jnp.bfloat16)
         low = (mix - high.astype(jnp.float32)).astype(jnp.bfloat16)
         mixed = mixed + jnp.dot(high, returned, preferred_element_type=jnp.float32)

time: 272 us -> 274 us (level)
  waiting for transfers between devices: 119 us -> 102 us
  Pallas kernels: 40.9 us -> 49.7 us
  local copies, waits for them, and re-layouts: 13.1 us -> 19.2 us
  starting transfers between devices: 77.9 us -> 80.9 us
    ppermute x15, waiting for transfers between devices: 57 us -> 29.3 us  [send(): lax.ppermute(array, 'tp', [(i, (i + step) % parts) for i in range(parts)])]
    all_gather x2 -> x4, waiting for transfers between devices: 3.61 us -> 24.9 us  [on_device(): lax.all_gather(rows, 'tp', tiled=True).reshape(parts, *rows.shape)]
    all_to_all x3 -> x4, starting transfers between devices: 31.6 us -> 37.8 us  [on_device(): lax.all_to_all(outputs, 'ep', split_axis=0, concat_axis=0, tiled=True)]
    all_to_all x3 -> x4, waiting for transfers between devices: 24.1 us -> 18.7 us  [on_device(): lax.all_to_all(outputs, 'ep', split_axis=0, concat_axis=0, tiled=True)]
    pallas_call x4 -> x5, Pallas kernels: 19.5 us -> 24.8 us  [the longest x4 23.5 us: hidden_units(): pl.pallas_call(functools.partial(hidden_kernel, parts), grid_spec=pltpu.P...]
    all_to_all x3, waiting for transfers between devices: 33.9 us -> 29.1 us  [on_device(): lax.all_to_all(leaving[number], 'ep', split_axis=0, concat_axis=0, tiled=...]
    reshape x1 -> x4, local copies, waits for them, and re-layouts: 2.41 us -> 6.69 us  [on_device(): arrived[:, start - first:start - first + slots]]
    pallas_call x3 -> x4, Pallas kernels: 14.6 us -> 18.3 us  [down(): pl.pallas_call(functools.partial(down_kernel, parts), grid_spec=pltpu.Pre...]
  transfers between devices with their start and end apart: 23 -> 26, of which waited for: 13 -> 18; matrix products, arithmetic and copies ran while one was open for 4% -> 7% of each run, Pallas kernels for 14% -> 17%
where the time goes in v8:
time: 274 us; the launch traced here: 273 us
  waiting for transfers between devices  102 us (37%)
  starting transfers between devices  80.9 us (30%)
  Pallas kernels  49.7 us (18%)
  local copies, waits for them, and re-layouts  19.2 us (7%)
  between operations  13.6 us (5%)
  matrix products  5.8 us (2%)
    all_to_all x4, starting transfers between devices, on_device(): lax.all_to_all(outputs, 'ep', split_axis=0, concat_axis=0, tiled=True)  37.8 us
    ppermute x15, waiting for transfers between devices, send(): lax.ppermute(array, 'tp', [(i, (i + step) % parts) for i in range(parts)])  29.3 us
    all_to_all x3, waiting for transfers between devices, on_device(): lax.all_to_all(leaving[number], 'ep', split_axis=0, concat_axis=0, tiled=...  29.1 us
    all_to_all x3, starting transfers between devices, on_device(): lax.all_to_all(leaving[number], 'ep', split_axis=0, concat_axis=0, tiled=...  26.6 us
    all_gather x4, waiting for transfers between devices, on_device(): lax.all_gather(rows, 'tp', tiled=True).reshape(parts, *rows.shape)  24.9 us
    pallas_call x4, Pallas kernels, hidden_units(): pl.pallas_call(functools.partial(hidden_kernel, parts), grid_spec=pltpu.P...  23.5 us
    all_to_all x4, waiting for transfers between devices, on_device(): lax.all_to_all(outputs, 'ep', split_axis=0, concat_axis=0, tiled=True)  18.7 us
    pallas_call x4, Pallas kernels, down(): pl.pallas_call(functools.partial(down_kernel, parts), grid_spec=pltpu.Pre...  18.3 us
  transfers between devices with their start and end apart: 26, of which 18 were waited for; matrix products, arithmetic and copies ran while one was open for 7% of the time, Pallas kernels for 17%

profile of v8, /device:TPU:1, one launch (start us, length us, event | category | flops | bytes accessed | tf_op | source)
XLA Modules:
  0.0 272.6 jit_solution(10130749341366185818)
XLA Ops:
  11.8 13.3 %all-to-all-start = ((bf16[64,4,1792]{2,1,0:T(4,128)(2,1)}), bf16[64,4,1792]{2,1,0:T(4,128)(2,1)}, u32[]{:S(2)}, u32[]{:S(2)}) async-start(bf16[64,4,1792]{2,1,0:T(4,128)(2,1)} %place_rows.3.rest_0_), calls=%async_computation | async-start | bytes 1835008 | tf_op jit(solution)/shard_map/all_to_all | solution.py:264
  25.2 3.4 %dynamic-slice_bitcast_fusion = (bf16[256,1792]{1,0:T(8,128)(2,1)}, bf16[256,1792]{1,0:T(8,128)(2,1)}, bf16[256,1792]{1,0:T(8,128)(2,1)}) fusion(bf16[1,256,7168]{2,1,0:T(8,128)(2,1)} %param.11, s32[]{:T(128)S(6)} %select_n.67, s32[]{:T(128)S(6)} %select_n.65, s32[]{:T(128)S(6)} %select_n.63), kind=kLoop, calls=%fused_computation.18 | loop fusion | bytes 5505036 | tf_op jit(solution)/shard_map/dynamic_slice | solution.py:239
  35.2 15.2 %all-to-all-done = bf16[64,4,1792]{2,1,0:T(4,128)(2,1)} async-done(((bf16[64,4,1792]{2,1,0:T(4,128)(2,1)}), bf16[64,4,1792]{2,1,0:T(4,128)(2,1)}, u32[]{:S(2)}, u32[]{:S(2)}) %all-to-all-start) | async-done | bytes 917536 | tf_op jit(solution)/shard_map/all_to_all | solution.py:264
  55.0 6.6 %all-to-all-start.2 = ((bf16[64,4,1792]{2,1,0:T(4,128)(2,1)}), bf16[64,4,1792]{2,1,0:T(4,128)(2,1)}, u32[]{:S(2)}, u32[]{:S(2)}) async-start(bf16[64,4,1792]{2,1,0:T(4,128)(2,1)} %place_rows.5), calls=%async_computation.2 | async-start | bytes 1835008 | tf_op jit(solution)/shard_map/all_to_all | solution.py:264
  61.7 15.6 %collective-permute-done.2.refs_2_.refs_7_ = bf16[256,1792]{1,0:T(8,128)(2,1)S(1)} collective-permute-done((bf16[256,1792]{1,0:T(8,128)(2,1)}, bf16[256,1792]{1,0:T(8,128)(2,1)S(1)}, u32[]{:S(2)}, u32[]{:S(2)}) %collective-permute-start.2) | collective-permute-done | bytes 917536 | tf_op jit(solution)/shard_map/ppermute | solution.py:233
  79.5 7.4 %all-to-all-done.2 = bf16[64,4,1792]{2,1,0:T(4,128)(2,1)} async-done(((bf16[64,4,1792]{2,1,0:T(4,128)(2,1)}), bf16[64,4,1792]{2,1,0:T(4,128)(2,1)}, u32[]{:S(2)}, u32[]{:S(2)}) %all-to-all-start.2) | async-done | bytes 917536 | tf_op jit(solution)/shard_map/all_to_all | solution.py:264
  86.9 6.6 %all-to-all-start.4 = ((bf16[64,4,1792]{2,1,0:T(4,128)(2,1)}), bf16[64,4,1792]{2,1,0:T(4,128)(2,1)}, u32[]{:S(2)}, u32[]{:S(2)}) async-start(bf16[64,4,1792]{2,1,0:T(4,128)(2,1)} %place_rows.4.rest_1_), calls=%async_computation.4 | async-start | bytes 1835008 | tf_op jit(solution)/shard_map/all_to_all | solution.py:264
  96.1 6.9 %all-gather.5.cloned.1.call-done = bf16[1024,1792]{1,0:T(8,128)(2,1)} async-done(((bf16[256,1792]{1,0:T(8,128)(2,1)}), bf16[1024,1792]{1,0:T(8,128)(2,1)}) %all-gather.5.cloned.1.call-update) | async-done | bytes 3670032 | tf_op jit(solution)/shard_map/all_gather | solution.py:270
  103.0 6.2 %hidden_units.4.refs_0_ = bf16[256,256]{1,0:T(8,128)(2,1)} custom-call(s32[1]{0:T(128)} %bitcast.me_ref, bf16[4,256,1792]{2,1,0:T(8,128)(2,1)} %bitcast.63, bf16[4,1792,256]{2,1,0:T(8,128)(2,1)} %bitcast.52, bf16[4,1792,256]{2,1,0:T(8,128)(2,1)} %bitcast.56, bf16[16,128]{1,0:T(8,128)(2,1)} %wait_for.1.refs_3_), custom_call_target="tpu_custom_call" | custom-call | flops 5637144576000 | bytes 11141120 | tf_op jit(solution)/shard_map/hidden_units/pallas_call | solution.py:75
  112.2 6.5 %all-to-all-done.4 = bf16[64,4,1792]{2,1,0:T(4,128)(2,1)} async-done(((bf16[64,4,1792]{2,1,0:T(4,128)(2,1)}), bf16[64,4,1792]{2,1,0:T(4,128)(2,1)}, u32[]{:S(2)}, u32[]{:S(2)}) %all-to-all-start.4) | async-done | bytes 917536 | tf_op jit(solution)/shard_map/all_to_all | solution.py:264
  123.7 4.9 %down.4.refs_3_ = bf16[64,4,1792]{2,1,0:T(4,128)(2,1)} custom-call(s32[1]{0:T(128)} %bitcast.me_ref, bf16[256,256]{1,0:T(8,128)(2,1)} %hidden_units.4.refs_0_, bf16[256,256]{1,0:T(8,128)(2,1)} %copy-done.12, bf16[256,256]{1,0:T(8,128)(2,1)} %copy-done.13, bf16[256,256]{1,0:T(8,128)(2,1)} %copy-done.14, bf16[256,7168]{1,0:T(8,128)(2,1)} %bitcast.48, ...), custom_call_target="tpu_custom_call" | custom-call | flops 939524096 | bytes 5111808 | tf_op jit(solution)/shard_map/down/pallas_call | solution.py:139
  128.6 6.7 %all-to-all-start.1 = ((bf16[64,4,1792]{2,1,0:T(4,128)(2,1)}), bf16[64,4,1792]{2,1,0:T(4,128)(2,1)}, u32[]{:S(2)}, u32[]{:S(2)}) async-start(bf16[64,4,1792]{2,1,0:T(4,128)(2,1)} %down.4.refs_3_), calls=%async_computation.1 | async-start | bytes 1835008 | tf_op jit(solution)/shard_map/all_to_all | solution.py:278
  135.4 15.8 %all-gather.7.cloned.1.call-done = bf16[1024,1792]{1,0:T(8,128)(2,1)} async-done(((bf16[256,1792]{1,0:T(8,128)(2,1)}), bf16[1024,1792]{1,0:T(8,128)(2,1)}) %all-gather.7.cloned.1.call-update) | async-done | bytes 3670032 | tf_op jit(solution)/shard_map/all_gather | solution.py:270
  151.2 6.3 %hidden_units.5.refs_0_ = bf16[256,256]{1,0:T(8,128)(2,1)} custom-call(s32[1]{0:T(128)} %bitcast.me_ref, bf16[4,256,1792]{2,1,0:T(8,128)(2,1)} %bitcast.62, bf16[4,1792,256]{2,1,0:T(8,128)(2,1)} %bitcast.53, bf16[4,1792,256]{2,1,0:T(8,128)(2,1)} %bitcast.57, bf16[64,4,1792]{2,1,0:T(4,128)(2,1)} %down.4.refs_3_), custom_call_target="tpu_custom_call" | custom-call | flops 563714457600 | bytes 11141120 | tf_op jit(solution)/shard_map/hidden_units/pallas_call | solution.py:75
  166.5 4.9 %down.5.refs_3_ = bf16[64,4,1792]{2,1,0:T(4,128)(2,1)} custom-call(s32[1]{0:T(128)} %bitcast.me_ref, bf16[256,256]{1,0:T(8,128)(2,1)} %hidden_units.5.refs_0_, bf16[256,256]{1,0:T(8,128)(2,1)} %copy-done.15, bf16[256,256]{1,0:T(8,128)(2,1)} %copy-done.16, bf16[256,256]{1,0:T(8,128)(2,1)} %copy-done.17, bf16[256,7168]{1,0:T(8,128)(2,1)} %bitcast.49, ...), custom_call_target="tpu_custom_call" | custom-call | flops 939524096 | bytes 5111808 | tf_op jit(solution)/shard_map/down/pallas_call | solution.py:139
  171.4 12.4 %all-to-all-start.3 = ((bf16[64,4,1792]{2,1,0:T(4,128)(2,1)}), bf16[64,4,1792]{2,1,0:T(4,128)(2,1)S(1)}, u32[]{:S(2)}, u32[]{:S(2)}) async-start(bf16[64,4,1792]{2,1,0:T(4,128)(2,1)} %down.5.refs_3_), calls=%async_computation.3 | async-start | bytes 1835008 | tf_op jit(solution)/shard_map/all_to_all | solution.py:278
  184.6 5.5 %hidden_units.6.refs_0_ = bf16[128,256]{1,0:T(8,128)(2,1)} custom-call(s32[1]{0:T(128)} %bitcast.me_ref, bf16[4,128,1792]{2,1,0:T(8,128)(2,1)} %bitcast.64, bf16[4,1792,256]{2,1,0:T(8,128)(2,1)} %bitcast.54, bf16[4,1792,256]{2,1,0:T(8,128)(2,1)} %bitcast.58, bf16[64,4,1792]{2,1,0:T(4,128)(2,1)} %down.5.refs_3_, bf16[64,4,1792]{2,1,0:T(4,128)(2,1)} %all-to-all-done.1.refs_4_), custom_call_target="tpu_custom_call" | custom-call | flops 28185722880 | bytes 9240576 | tf_op jit(solution)/shard_map/hidden_units/pallas_call | solution.py:75
  198.6 4.2 %down.6.refs_3_ = bf16[64,2,1792]{2,1,0:T(2,128)(2,1)} custom-call(s32[1]{0:T(128)} %bitcast.me_ref, bf16[128,256]{1,0:T(8,128)(2,1)} %hidden_units.6.refs_0_, bf16[128,256]{1,0:T(8,128)(2,1)} %copy-done.23, bf16[128,256]{1,0:T(8,128)(2,1)} %copy-done.19, bf16[128,256]{1,0:T(8,128)(2,1)} %copy-done.21, bf16[256,7168]{1,0:T(8,128)(2,1)} %bitcast.50, ...), custom_call_target="tpu_custom_call" | custom-call | flops 469762048 | bytes 4390912 | tf_op jit(solution)/shard_map/down/pallas_call | solution.py:139
  202.9 6.2 %all-to-all-done.3.refs_4_ = bf16[64,4,1792]{2,1,0:T(4,128)(2,1)S(1)} async-done(((bf16[64,4,1792]{2,1,0:T(4,128)(2,1)}), bf16[64,4,1792]{2,1,0:T(4,128)(2,1)S(1)}, u32[]{:S(2)}, u32[]{:S(2)}) %all-to-all-start.3) | async-done | bytes 917536 | tf_op jit(solution)/shard_map/all_to_all | solution.py:278
  209.1 6.5 %all-to-all-start.5 = ((bf16[64,2,1792]{2,1,0:T(2,128)(2,1)}), bf16[64,2,1792]{2,1,0:T(2,128)(2,1)S(1)}, u32[]{:S(2)}, u32[]{:S(2)}) async-start(bf16[64,2,1792]{2,1,0:T(2,128)(2,1)} %down.6.refs_3_), calls=%async_computation.5 | async-start | bytes 917504 | tf_op jit(solution)/shard_map/all_to_all | solution.py:278
  217.5 5.5 %hidden_units.7.refs_0_ = bf16[128,256]{1,0:T(8,128)(2,1)} custom-call(s32[1]{0:T(128)} %bitcast.me_ref, bf16[4,128,1792]{2,1,0:T(8,128)(2,1)} %bitcast.60, bf16[4,1792,256]{2,1,0:T(8,128)(2,1)} %bitcast.55, bf16[4,1792,256]{2,1,0:T(8,128)(2,1)} %bitcast.59, bf16[64,2,1792]{2,1,0:T(2,128)(2,1)} %down.6.refs_3_, bf16[64,4,1792]{2,1,0:T(4,128)(2,1)} %copy-done.3), custom_call_target="tpu_custom_call" | custom-call | flops 939524096 | bytes 9240576 | tf_op jit(solution)/shard_map/hidden_units/pallas_call | solution.py:75
  231.5 4.2 %down.7 = bf16[64,2,1792]{2,1,0:T(2,128)(2,1)} custom-call(s32[1]{0:T(128)} %bitcast.me_ref, bf16[128,256]{1,0:T(8,128)(2,1)} %hidden_units.7.refs_0_, bf16[128,256]{1,0:T(8,128)(2,1)} %copy-done.18, bf16[128,256]{1,0:T(8,128)(2,1)} %copy-done.20, bf16[128,256]{1,0:T(8,128)(2,1)} %copy-done.22, bf16[256,7168]{1,0:T(8,128)(2,1)} %bitcast.51, ...), custom_call_target="tpu_custom_call" | custom-call | flops 469762048 | bytes 4390912 | tf_op jit(solution)/shard_map/down/pallas_call | solution.py:139
  235.7 12.3 %all-to-all-start.6 = ((bf16[64,2,1792]{2,1,0:T(2,128)(2,1)}), bf16[64,2,1792]{2,1,0:T(2,128)(2,1)S(1)}, u32[]{:S(2)}, u32[]{:S(2)}) async-start(bf16[64,2,1792]{2,1,0:T(2,128)(2,1)} %down.7), calls=%async_computation.6 | async-start | bytes 917504 | tf_op jit(solution)/shard_map/all_to_all | solution.py:278
  252.0 12.4 %all-to-all-done.6 = bf16[64,2,1792]{2,1,0:T(2,128)(2,1)S(1)} async-done(((bf16[64,2,1792]{2,1,0:T(2,128)(2,1)}), bf16[64,2,1792]{2,1,0:T(2,128)(2,1)S(1)}, u32[]{:S(2)}, u32[]{:S(2)}) %all-to-all-start.6) | async-done | bytes 458784 | tf_op jit(solution)/shard_map/all_to_all | solution.py:278
  (137 shorter events, 63.3 us)
Async XLA Ops:
  11.8 38.6 %all-to-all-start = ((bf16[64,4,1792]{2,1,0:T(4,128)(2,1)}), bf16[64,4,1792]{2,1,0:T(4,128)(2,1)}, u32[]{:S(2)}, u32[]{:S(2)}) async-start(bf16[64,4,1792]{2,1,0:T(4,128)(2,1)} %place_rows.3.rest_0_), calls=%async_computation | async-start | bytes 1835008 | tf_op jit(solution)/shard_map/all_to_all | solution.py:264
  25.1 77.9 %all-gather.5.cloned.1.call-start = ((), (), s32[]{:S(2)}) async-start(), calls=%async_computation.7 | async-start | bytes 4587520 | tf_op jit(solution)/shard_map/all_gather | solution.py:270
  28.6 33.0 %collective-permute-start = (bf16[256,1792]{1,0:T(8,128)(2,1)}, bf16[256,1792]{1,0:T(8,128)(2,1)S(1)}, u32[]{:S(2)}, u32[]{:S(2)}) collective-permute-start(bf16[256,1792]{1,0:T(8,128)(2,1)} %get-tuple-element.7), channel_id=1, source_target_pairs={{0,1},{1,2},{2,3},{3,0},{4,5},{5,6},{6,7},{7,4},{8,9},{9,10},{10,1... | collective-permute-start | bytes 2752520 | tf_op jit(solution)/shard_map/ppermute | solution.py:233
  29.9 31.7 %collective-permute-start.1 = (bf16[256,1792]{1,0:T(8,128)(2,1)}, bf16[256,1792]{1,0:T(8,128)(2,1)S(1)}, u32[]{:S(2)}, u32[]{:S(2)}) collective-permute-start(bf16[256,1792]{1,0:T(8,128)(2,1)} %get-tuple-element.6), channel_id=1, source_target_pairs={{0,3},{1,0},{2,1},{3,2},{4,7},{5,4},{6,5},{7,6},{8,11},{9,8},{10,9... | collective-permute-start | bytes 2752520 | tf_op jit(solution)/shard_map/ppermute | solution.py:233
  31.4 45.8 %collective-permute-start.2 = (bf16[256,1792]{1,0:T(8,128)(2,1)}, bf16[256,1792]{1,0:T(8,128)(2,1)S(1)}, u32[]{:S(2)}, u32[]{:S(2)}) collective-permute-start(bf16[256,1792]{1,0:T(8,128)(2,1)} %get-tuple-element.5), channel_id=1, source_target_pairs={{0,2},{1,3},{2,0},{3,1},{4,6},{5,7},{6,4},{7,5},{8,10},{9,11},{10,... | collective-permute-start | bytes 2752520 | tf_op jit(solution)/shard_map/ppermute | solution.py:233
  55.0 31.9 %all-to-all-start.2 = ((bf16[64,4,1792]{2,1,0:T(4,128)(2,1)}), bf16[64,4,1792]{2,1,0:T(4,128)(2,1)}, u32[]{:S(2)}, u32[]{:S(2)}) async-start(bf16[64,4,1792]{2,1,0:T(4,128)(2,1)} %place_rows.5), calls=%async_computation.2 | async-start | bytes 1835008 | tf_op jit(solution)/shard_map/all_to_all | solution.py:264
  86.9 31.9 %all-to-all-start.4 = ((bf16[64,4,1792]{2,1,0:T(4,128)(2,1)}), bf16[64,4,1792]{2,1,0:T(4,128)(2,1)}, u32[]{:S(2)}, u32[]{:S(2)}) async-start(bf16[64,4,1792]{2,1,0:T(4,128)(2,1)} %place_rows.4.rest_1_), calls=%async_computation.4 | async-start | bytes 1835008 | tf_op jit(solution)/shard_map/all_to_all | solution.py:264
  93.5 57.7 %all-gather.7.cloned.1.call-start = ((), (), s32[]{:S(2)}) async-start(), calls=%async_computation.8 | async-start | bytes 4587520 | tf_op jit(solution)/shard_map/all_gather | solution.py:270
  96.0 88.6 %all-gather.9.cloned.1.call-start = ((), (), s32[]{:S(2)}) async-start(), calls=%async_computation.9 | async-start | bytes 2293760 | tf_op jit(solution)/shard_map/all_gather | solution.py:270
  109.2 13.7 %collective-permute-start.3 = (bf16[256,256]{1,0:T(8,128)(2,1)}, bf16[256,256]{1,0:T(8,128)(2,1)S(1)}, u32[]{:S(2)}, u32[]{:S(2)}) collective-permute-start(bf16[256,256]{1,0:T(8,128)(2,1)} %hidden_units.4.refs_0_), channel_id=1, source_target_pairs={{0,1},{1,2},{2,3},{3,0},{4,5},{5,6},{6,7},{7,4},{8,9},{9,10},{10,1... | collective-permute-start | bytes 393224 | tf_op jit(solution)/shard_map/ppermute | solution.py:233
  110.2 12.8 %collective-permute-start.4 = (bf16[256,256]{1,0:T(8,128)(2,1)}, bf16[256,256]{1,0:T(8,128)(2,1)S(1)}, u32[]{:S(2)}, u32[]{:S(2)}) collective-permute-start(bf16[256,256]{1,0:T(8,128)(2,1)} %hidden_units.4.refs_0_), channel_id=1, source_target_pairs={{0,3},{1,0},{2,1},{3,2},{4,7},{5,4},{6,5},{7,6},{8,11},{9,8},{10,9... | collective-permute-start | bytes 393224 | tf_op jit(solution)/shard_map/ppermute | solution.py:233
  112.0 11.0 %collective-permute-start.5 = (bf16[256,256]{1,0:T(8,128)(2,1)}, bf16[256,256]{1,0:T(8,128)(2,1)S(1)}, u32[]{:S(2)}, u32[]{:S(2)}) collective-permute-start(bf16[256,256]{1,0:T(8,128)(2,1)} %hidden_units.4.refs_0_), channel_id=1, source_target_pairs={{0,2},{1,3},{2,0},{3,1},{4,6},{5,7},{6,4},{7,5},{8,10},{9,11},{10,... | collective-permute-start | bytes 393224 | tf_op jit(solution)/shard_map/ppermute | solution.py:233
  128.6 42.8 %all-to-all-start.1 = ((bf16[64,4,1792]{2,1,0:T(4,128)(2,1)}), bf16[64,4,1792]{2,1,0:T(4,128)(2,1)}, u32[]{:S(2)}, u32[]{:S(2)}) async-start(bf16[64,4,1792]{2,1,0:T(4,128)(2,1)} %down.4.refs_3_), calls=%async_computation.1 | async-start | bytes 1835008 | tf_op jit(solution)/shard_map/all_to_all | solution.py:278
  135.4 82.1 %all-gather.11.cloned.1.call-start = ((), (), s32[]{:S(2)}) async-start(), calls=%async_computation.10 | async-start | bytes 2293760 | tf_op jit(solution)/shard_map/all_gather | solution.py:270
  157.6 5.9 %collective-permute-start.6 = (bf16[256,256]{1,0:T(8,128)(2,1)}, bf16[256,256]{1,0:T(8,128)(2,1)S(1)}, u32[]{:S(2)}, u32[]{:S(2)}) collective-permute-start(bf16[256,256]{1,0:T(8,128)(2,1)} %hidden_units.5.refs_0_), channel_id=1, source_target_pairs={{0,1},{1,2},{2,3},{3,0},{4,5},{5,6},{6,7},{7,4},{8,9},{9,10},{10,1... | collective-permute-start | bytes 393224 | tf_op jit(solution)/shard_map/ppermute | solution.py:233
  158.1 5.9 %collective-permute-start.7 = (bf16[256,256]{1,0:T(8,128)(2,1)}, bf16[256,256]{1,0:T(8,128)(2,1)S(1)}, u32[]{:S(2)}, u32[]{:S(2)}) collective-permute-start(bf16[256,256]{1,0:T(8,128)(2,1)} %hidden_units.5.refs_0_), channel_id=1, source_target_pairs={{0,3},{1,0},{2,1},{3,2},{4,7},{5,4},{6,5},{7,6},{8,11},{9,8},{10,9... | collective-permute-start | bytes 393224 | tf_op jit(solution)/shard_map/ppermute | solution.py:233
  160.3 5.5 %collective-permute-start.8 = (bf16[256,256]{1,0:T(8,128)(2,1)}, bf16[256,256]{1,0:T(8,128)(2,1)S(1)}, u32[]{:S(2)}, u32[]{:S(2)}) collective-permute-start(bf16[256,256]{1,0:T(8,128)(2,1)} %hidden_units.5.refs_0_), channel_id=1, source_target_pairs={{0,2},{1,3},{2,0},{3,1},{4,6},{5,7},{6,4},{7,5},{8,10},{9,11},{10,... | collective-permute-start | bytes 393224 | tf_op jit(solution)/shard_map/ppermute | solution.py:233
  171.4 37.7 %all-to-all-start.3 = ((bf16[64,4,1792]{2,1,0:T(4,128)(2,1)}), bf16[64,4,1792]{2,1,0:T(4,128)(2,1)S(1)}, u32[]{:S(2)}, u32[]{:S(2)}) async-start(bf16[64,4,1792]{2,1,0:T(4,128)(2,1)} %down.5.refs_3_), calls=%async_computation.3 | async-start | bytes 1835008 | tf_op jit(solution)/shard_map/all_to_all | solution.py:278
  192.3 5.1 %collective-permute-start.11 = (bf16[128,256]{1,0:T(8,128)(2,1)}, bf16[128,256]{1,0:T(8,128)(2,1)S(1)}, u32[]{:S(2)}, u32[]{:S(2)}) collective-permute-start(bf16[128,256]{1,0:T(8,128)(2,1)} %hidden_units.6.refs_0_), channel_id=1, source_target_pairs={{0,2},{1,3},{2,0},{3,1},{4,6},{5,7},{6,4},{7,5},{8,10},{9,11},{10,... | collective-permute-start | bytes 196616 | tf_op jit(solution)/shard_map/ppermute | solution.py:233
  192.3 5.5 %collective-permute-start.9 = (bf16[128,256]{1,0:T(8,128)(2,1)}, bf16[128,256]{1,0:T(8,128)(2,1)S(1)}, u32[]{:S(2)}, u32[]{:S(2)}) collective-permute-start(bf16[128,256]{1,0:T(8,128)(2,1)} %hidden_units.6.refs_0_), channel_id=1, source_target_pairs={{0,1},{1,2},{2,3},{3,0},{4,5},{5,6},{6,7},{7,4},{8,9},{9,10},{10,1... | collective-permute-start | bytes 196616 | tf_op jit(solution)/shard_map/ppermute | solution.py:233
  209.1 26.6 %all-to-all-start.5 = ((bf16[64,2,1792]{2,1,0:T(2,128)(2,1)}), bf16[64,2,1792]{2,1,0:T(2,128)(2,1)S(1)}, u32[]{:S(2)}, u32[]{:S(2)}) async-start(bf16[64,2,1792]{2,1,0:T(2,128)(2,1)} %down.6.refs_3_), calls=%async_computation.5 | async-start | bytes 917504 | tf_op jit(solution)/shard_map/all_to_all | solution.py:278
  223.0 4.9 %collective-permute-start.12 = (bf16[128,256]{1,0:T(8,128)(2,1)}, bf16[128,256]{1,0:T(8,128)(2,1)S(1)}, u32[]{:S(2)}, u32[]{:S(2)}) collective-permute-start(bf16[128,256]{1,0:T(8,128)(2,1)} %hidden_units.7.refs_0_), channel_id=1, source_target_pairs={{0,1},{1,2},{2,3},{3,0},{4,5},{5,6},{6,7},{7,4},{8,9},{9,10},{10,1... | collective-permute-start | bytes 196616 | tf_op jit(solution)/shard_map/ppermute | solution.py:233
  225.7 5.1 %collective-permute-start.14 = (bf16[128,256]{1,0:T(8,128)(2,1)}, bf16[128,256]{1,0:T(8,128)(2,1)S(1)}, u32[]{:S(2)}, u32[]{:S(2)}) collective-permute-start(bf16[128,256]{1,0:T(8,128)(2,1)} %hidden_units.7.refs_0_), channel_id=1, source_target_pairs={{0,2},{1,3},{2,0},{3,1},{4,6},{5,7},{6,4},{7,5},{8,10},{9,11},{10,... | collective-permute-start | bytes 196616 | tf_op jit(solution)/shard_map/ppermute | solution.py:233
  235.7 28.6 %all-to-all-start.6 = ((bf16[64,2,1792]{2,1,0:T(2,128)(2,1)}), bf16[64,2,1792]{2,1,0:T(2,128)(2,1)S(1)}, u32[]{:S(2)}, u32[]{:S(2)}) async-start(bf16[64,2,1792]{2,1,0:T(2,128)(2,1)} %down.7), calls=%async_computation.6 | async-start | bytes 917504 | tf_op jit(solution)/shard_map/all_to_all | solution.py:278
  (29 other events, 249.6 us)
Sparse Core Ops, SparseCore 0:
  52.9 50.0 all-gather.4
  104.8 46.3 all-gather.6
  153.0 31.4 all-gather.8
  186.3 31.1 all-gather.10

commit v9 on v6

--- a/solution.py
+++ b/solution.py
@@ -11,7 +11,7 @@
 CHUNKS = ((0, 4, False), (4, 4, False), (8, 4, False))
 SENDS = (1, 3, 2)
 STEPS = (0, 3, 1, 2)
-TILES = 2
+TILES = 7
 TOLD = (1000, 100, 1)
 WAIT_TOLD = 200_000_000_000
 MIB = 1024 * 1024

time: 267 us -> 268 us (level)
  Pallas kernels: 41.6 us -> 45 us
  waiting for transfers between devices: 117 us -> 114 us
    pallas_call x3, Pallas kernels: 14.8 us -> 18.2 us  [down(): pl.pallas_call(functools.partial(down_kernel, parts), grid_spec=pltpu.Pre...]
  transfers between devices with their start and end apart: 21 -> 21, of which waited for: 14 -> 14; matrix products, arithmetic and copies ran while one was open for 6% -> 6% of each run, Pallas kernels for 15% -> 16%
where the time goes in v9:
time: 268 us; the launch traced here: 267 us
  waiting for transfers between devices  114 us (43%)
  starting transfers between devices  72.2 us (27%)
  Pallas kernels  45 us (17%)
  local copies, waits for them, and re-layouts  15.3 us (6%)
  between operations  13.6 us (5%)
  matrix products  5.12 us (2%)
    all_gather x3, waiting for transfers between devices, on_device(): lax.all_gather(rows, 'tp', tiled=True).reshape(parts, *rows.shape)  36.4 us
    all_to_all x3, starting transfers between devices, on_device(): lax.all_to_all(outputs, 'ep', split_axis=0, concat_axis=0, tiled=True)  32.3 us
    all_to_all x3, waiting for transfers between devices, on_device(): lax.all_to_all(leaving[number], 'ep', split_axis=0, concat_axis=0, tiled=...  29.2 us
    ppermute x12, waiting for transfers between devices, send(): lax.ppermute(array, 'tp', [(i, (i + step) % parts) for i in range(parts)])  27.7 us
    all_to_all x3, starting transfers between devices, on_device(): lax.all_to_all(leaving[number], 'ep', split_axis=0, concat_axis=0, tiled=...  26.6 us
    all_to_all x3, waiting for transfers between devices, on_device(): lax.all_to_all(outputs, 'ep', split_axis=0, concat_axis=0, tiled=True)  21 us
    pallas_call x3, Pallas kernels, hidden_units(): pl.pallas_call(functools.partial(hidden_kernel, gathered, parts), grid_sp...  18.8 us
    pallas_call x3, Pallas kernels, down(): pl.pallas_call(functools.partial(down_kernel, parts), grid_spec=pltpu.Pre...  18.2 us
  transfers between devices with their start and end apart: 21, of which 14 were waited for; matrix products, arithmetic and copies ran while one was open for 6% of the time, Pallas kernels for 16%

profile of v9, /device:TPU:1, one launch (start us, length us, event | category | flops | bytes accessed | tf_op | source)
XLA Modules:
  0.0 266.9 jit_solution(12628028902235779401)
XLA Ops:
  11.4 13.3 %all-to-all-start = ((bf16[64,4,1792]{2,1,0:T(4,128)(2,1)}), bf16[64,4,1792]{2,1,0:T(4,128)(2,1)}, u32[]{:S(2)}, u32[]{:S(2)}) async-start(bf16[64,4,1792]{2,1,0:T(4,128)(2,1)} %place_rows.3.rest_0_), calls=%async_computation | async-start | bytes 1835008 | tf_op jit(solution)/shard_map/all_to_all | solution.py:272
  24.8 3.4 %dynamic-slice_bitcast_fusion = (bf16[256,1792]{1,0:T(8,128)(2,1)}, bf16[256,1792]{1,0:T(8,128)(2,1)}, bf16[256,1792]{1,0:T(8,128)(2,1)}) fusion(bf16[1,256,7168]{2,1,0:T(8,128)(2,1)} %param.11, s32[]{:T(128)S(6)} %select_n.61, s32[]{:T(128)S(6)} %select_n.59, s32[]{:T(128)S(6)} %select_n.57), kind=kLoop, calls=%fused_computation.14 | loop fusion | bytes 5505036 | tf_op jit(solution)/shard_map/dynamic_slice | solution.py:246
  34.7 15.2 %all-to-all-done = bf16[64,4,1792]{2,1,0:T(4,128)(2,1)} async-done(((bf16[64,4,1792]{2,1,0:T(4,128)(2,1)}), bf16[64,4,1792]{2,1,0:T(4,128)(2,1)}, u32[]{:S(2)}, u32[]{:S(2)}) %all-to-all-start) | async-done | bytes 917536 | tf_op jit(solution)/shard_map/all_to_all | solution.py:272
  54.6 6.6 %all-to-all-start.2 = ((bf16[64,4,1792]{2,1,0:T(4,128)(2,1)}), bf16[64,4,1792]{2,1,0:T(4,128)(2,1)}, u32[]{:S(2)}, u32[]{:S(2)}) async-start(bf16[64,4,1792]{2,1,0:T(4,128)(2,1)} %place_rows.5), calls=%async_computation.2 | async-start | bytes 1835008 | tf_op jit(solution)/shard_map/all_to_all | solution.py:272
  61.3 15.4 %collective-permute-done.2.refs_2_.refs_7_ = bf16[256,1792]{1,0:T(8,128)(2,1)S(1)} collective-permute-done((bf16[256,1792]{1,0:T(8,128)(2,1)}, bf16[256,1792]{1,0:T(8,128)(2,1)S(1)}, u32[]{:S(2)}, u32[]{:S(2)}) %collective-permute-start.2) | collective-permute-done | bytes 917536 | tf_op jit(solution)/shard_map/ppermute | solution.py:235
  79.0 7.5 %all-to-all-done.2 = bf16[64,4,1792]{2,1,0:T(4,128)(2,1)} async-done(((bf16[64,4,1792]{2,1,0:T(4,128)(2,1)}), bf16[64,4,1792]{2,1,0:T(4,128)(2,1)}, u32[]{:S(2)}, u32[]{:S(2)}) %all-to-all-start.2) | async-done | bytes 917536 | tf_op jit(solution)/shard_map/all_to_all | solution.py:272
  86.5 6.6 %all-to-all-start.4 = ((bf16[64,4,1792]{2,1,0:T(4,128)(2,1)}), bf16[64,4,1792]{2,1,0:T(4,128)(2,1)}, u32[]{:S(2)}, u32[]{:S(2)}) async-start(bf16[64,4,1792]{2,1,0:T(4,128)(2,1)} %place_rows.4.rest_1_), calls=%async_computation.4 | async-start | bytes 1835008 | tf_op jit(solution)/shard_map/all_to_all | solution.py:272
  95.6 6.9 %all-gather.4.cloned.1.call-done = bf16[1024,1792]{1,0:T(8,128)(2,1)} async-done(((bf16[256,1792]{1,0:T(8,128)(2,1)}), bf16[1024,1792]{1,0:T(8,128)(2,1)}) %all-gather.4.cloned.1.call-update) | async-done | bytes 3670032 | tf_op jit(solution)/shard_map/all_gather | solution.py:279
  102.5 6.3 %hidden_units.3.refs_0_.refs_3_ = bf16[256,256]{1,0:T(8,128)(2,1)} custom-call(s32[1]{0:T(128)} %bitcast.me_ref, bf16[4,256,1792]{2,1,0:T(8,128)(2,1)} %bitcast.51, bf16[4,1792,256]{2,1,0:T(8,128)(2,1)} %bitcast.42, bf16[4,1792,256]{2,1,0:T(8,128)(2,1)} %bitcast.45, bf16[16,128]{1,0:T(8,128)(2,1)} %wait_for.1.refs_3_), custom_call_target="tpu_custom_call" | custom-call | flops 1879048192000 | bytes 11141120 | tf_op jit(solution)/shard_map/hidden_units/pallas_call | solution.py:77
  111.8 6.5 %all-to-all-done.4 = bf16[64,4,1792]{2,1,0:T(4,128)(2,1)} async-done(((bf16[64,4,1792]{2,1,0:T(4,128)(2,1)}), bf16[64,4,1792]{2,1,0:T(4,128)(2,1)}, u32[]{:S(2)}, u32[]{:S(2)}) %all-to-all-start.4) | async-done | bytes 917536 | tf_op jit(solution)/shard_map/all_to_all | solution.py:272
  118.3 2.4 reshape.92
  121.6 6.0 %down.3 = bf16[64,4,1792]{2,1,0:T(4,128)(2,1)} custom-call(s32[1]{0:T(128)} %bitcast.me_ref, bf16[256,256]{1,0:T(8,128)(2,1)} %hidden_units.3.refs_0_.refs_3_, bf16[256,256]{1,0:T(8,128)(2,1)} %copy-done.7, bf16[256,256]{1,0:T(8,128)(2,1)} %copy-done.8, bf16[256,256]{1,0:T(8,128)(2,1)} %copy-done.9, bf16[256,7168]{1,0:T(8,128)(2,1)} %bitcast.39, ...), custom_call_target="tpu_custom_call" | custom-call | flops 939524096 | bytes 5111808 | tf_op jit(solution)/shard_map/down/pallas_call | solution.py:141
  127.6 8.5 %all-to-all-start.1 = ((bf16[64,4,1792]{2,1,0:T(4,128)(2,1)}), bf16[64,4,1792]{2,1,0:T(4,128)(2,1)}, u32[]{:S(2)}, u32[]{:S(2)}) async-start(bf16[64,4,1792]{2,1,0:T(4,128)(2,1)} %down.3), calls=%async_computation.1 | async-start | bytes 1835008 | tf_op jit(solution)/shard_map/all_to_all | solution.py:286
  136.1 14.7 %all-gather.6.cloned.1.call-done = bf16[1024,1792]{1,0:T(8,128)(2,1)} async-done(((bf16[256,1792]{1,0:T(8,128)(2,1)}), bf16[1024,1792]{1,0:T(8,128)(2,1)}) %all-gather.6.cloned.1.call-update) | async-done | bytes 3670032 | tf_op jit(solution)/shard_map/all_gather | solution.py:279
  150.8 6.3 %hidden_units.4.refs_0_.refs_3_ = bf16[256,256]{1,0:T(8,128)(2,1)} custom-call(s32[1]{0:T(128)} %bitcast.me_ref, bf16[4,256,1792]{2,1,0:T(8,128)(2,1)} %bitcast.50, bf16[4,1792,256]{2,1,0:T(8,128)(2,1)} %bitcast.43, bf16[4,1792,256]{2,1,0:T(8,128)(2,1)} %bitcast.46, bf16[256,256]{1,0:T(8,128)(2,1)} %hidden_units.3.refs_0_.refs_3_), custom_call_target="tpu_custom_call" | custom-call | flops 187904819200 | bytes 11141120 | tf_op jit(solution)/shard_map/hidden_units/pallas_call | solution.py:77
  160.3 2.6 collective-permute-done.6.refs_1_
  166.0 6.1 %down.4 = bf16[64,4,1792]{2,1,0:T(4,128)(2,1)} custom-call(s32[1]{0:T(128)} %bitcast.me_ref, bf16[256,256]{1,0:T(8,128)(2,1)} %hidden_units.4.refs_0_.refs_3_, bf16[256,256]{1,0:T(8,128)(2,1)} %copy-done.12, bf16[256,256]{1,0:T(8,128)(2,1)} %copy-done.14, bf16[256,256]{1,0:T(8,128)(2,1)} %copy-done.15, bf16[256,7168]{1,0:T(8,128)(2,1)} %bitcast.40, ...), custom_call_target="tpu_custom_call" | custom-call | flops 939524096 | bytes 5111808 | tf_op jit(solution)/shard_map/down/pallas_call | solution.py:141
  172.2 12.3 %all-to-all-start.3 = ((bf16[64,4,1792]{2,1,0:T(4,128)(2,1)}), bf16[64,4,1792]{2,1,0:T(4,128)(2,1)S(1)}, u32[]{:S(2)}, u32[]{:S(2)}) async-start(bf16[64,4,1792]{2,1,0:T(4,128)(2,1)} %down.4), calls=%async_computation.3 | async-start | bytes 1835008 | tf_op jit(solution)/shard_map/all_to_all | solution.py:286
  184.5 14.9 %all-gather.8.cloned.1.call-done = bf16[1024,1792]{1,0:T(8,128)(2,1)} async-done(((bf16[256,1792]{1,0:T(8,128)(2,1)}), bf16[1024,1792]{1,0:T(8,128)(2,1)}) %all-gather.8.cloned.1.call-update) | async-done | bytes 3670032 | tf_op jit(solution)/shard_map/all_gather | solution.py:279
  199.4 6.3 %hidden_units.5.refs_0_ = bf16[256,256]{1,0:T(8,128)(2,1)} custom-call(s32[1]{0:T(128)} %bitcast.me_ref, bf16[4,256,1792]{2,1,0:T(8,128)(2,1)} %bitcast.48, bf16[4,1792,256]{2,1,0:T(8,128)(2,1)} %bitcast.44, bf16[4,1792,256]{2,1,0:T(8,128)(2,1)} %bitcast.47, bf16[256,256]{1,0:T(8,128)(2,1)} %hidden_units.4.refs_0_.refs_3_), custom_call_target="tpu_custom_call" | custom-call | flops 1879048192 | bytes 11141120 | tf_op jit(solution)/shard_map/hidden_units/pallas_call | solution.py:77
  211.9 3.6 %collective-permute-done.9.refs_1_ = bf16[256,256]{1,0:T(8,128)(2,1)S(1)} collective-permute-done((bf16[256,256]{1,0:T(8,128)(2,1)}, bf16[256,256]{1,0:T(8,128)(2,1)S(1)}, u32[]{:S(2)}, u32[]{:S(2)}) %collective-permute-start.9) | collective-permute-done | bytes 131104 | tf_op jit(solution)/shard_map/ppermute | solution.py:235
  216.2 6.0 %down.5 = bf16[64,4,1792]{2,1,0:T(4,128)(2,1)} custom-call(s32[1]{0:T(128)} %bitcast.me_ref, bf16[256,256]{1,0:T(8,128)(2,1)} %hidden_units.5.refs_0_, bf16[256,256]{1,0:T(8,128)(2,1)} %copy-done.13, bf16[256,256]{1,0:T(8,128)(2,1)} %copy-done.10, bf16[256,256]{1,0:T(8,128)(2,1)} %copy-done.11, bf16[256,7168]{1,0:T(8,128)(2,1)} %bitcast.41, ...), custom_call_target="tpu_custom_call" | custom-call | flops 939524096 | bytes 5111808 | tf_op jit(solution)/shard_map/down/pallas_call | solution.py:141
  222.3 11.5 %all-to-all-start.5 = ((bf16[64,4,1792]{2,1,0:T(4,128)(2,1)}), bf16[64,4,1792]{2,1,0:T(4,128)(2,1)S(1)}, u32[]{:S(2)}, u32[]{:S(2)}) async-start(bf16[64,4,1792]{2,1,0:T(4,128)(2,1)} %down.5), calls=%async_computation.5 | async-start | bytes 1835008 | tf_op jit(solution)/shard_map/all_to_all | solution.py:286
  238.1 21.0 %all-to-all-done.5 = bf16[64,4,1792]{2,1,0:T(4,128)(2,1)S(1)} async-done(((bf16[64,4,1792]{2,1,0:T(4,128)(2,1)}), bf16[64,4,1792]{2,1,0:T(4,128)(2,1)S(1)}, u32[]{:S(2)}, u32[]{:S(2)}) %all-to-all-start.5) | async-done | bytes 917536 | tf_op jit(solution)/shard_map/all_to_all | solution.py:286
  (105 shorter events, 43.2 us)
Async XLA Ops:
  11.4 38.6 %all-to-all-start = ((bf16[64,4,1792]{2,1,0:T(4,128)(2,1)}), bf16[64,4,1792]{2,1,0:T(4,128)(2,1)}, u32[]{:S(2)}, u32[]{:S(2)}) async-start(bf16[64,4,1792]{2,1,0:T(4,128)(2,1)} %place_rows.3.rest_0_), calls=%async_computation | async-start | bytes 1835008 | tf_op jit(solution)/shard_map/all_to_all | solution.py:272
  24.7 77.8 %all-gather.4.cloned.1.call-start = ((), (), s32[]{:S(2)}) async-start(), calls=%async_computation.6 | async-start | bytes 4587520 | tf_op jit(solution)/shard_map/all_gather | solution.py:279
  28.2 33.0 %collective-permute-start = (bf16[256,1792]{1,0:T(8,128)(2,1)}, bf16[256,1792]{1,0:T(8,128)(2,1)S(1)}, u32[]{:S(2)}, u32[]{:S(2)}) collective-permute-start(bf16[256,1792]{1,0:T(8,128)(2,1)} %get-tuple-element.7), channel_id=1, source_target_pairs={{0,1},{1,2},{2,3},{3,0},{4,5},{5,6},{6,7},{7,4},{8,9},{9,10},{10,1... | collective-permute-start | bytes 2752520 | tf_op jit(solution)/shard_map/ppermute | solution.py:235
  29.5 31.8 %collective-permute-start.1 = (bf16[256,1792]{1,0:T(8,128)(2,1)}, bf16[256,1792]{1,0:T(8,128)(2,1)S(1)}, u32[]{:S(2)}, u32[]{:S(2)}) collective-permute-start(bf16[256,1792]{1,0:T(8,128)(2,1)} %get-tuple-element.6), channel_id=1, source_target_pairs={{0,3},{1,0},{2,1},{3,2},{4,7},{5,4},{6,5},{7,6},{8,11},{9,8},{10,9... | collective-permute-start | bytes 2752520 | tf_op jit(solution)/shard_map/ppermute | solution.py:235
  31.0 45.8 %collective-permute-start.2 = (bf16[256,1792]{1,0:T(8,128)(2,1)}, bf16[256,1792]{1,0:T(8,128)(2,1)S(1)}, u32[]{:S(2)}, u32[]{:S(2)}) collective-permute-start(bf16[256,1792]{1,0:T(8,128)(2,1)} %get-tuple-element.5), channel_id=1, source_target_pairs={{0,2},{1,3},{2,0},{3,1},{4,6},{5,7},{6,4},{7,5},{8,10},{9,11},{10,... | collective-permute-start | bytes 2752520 | tf_op jit(solution)/shard_map/ppermute | solution.py:235
  54.6 31.9 %all-to-all-start.2 = ((bf16[64,4,1792]{2,1,0:T(4,128)(2,1)}), bf16[64,4,1792]{2,1,0:T(4,128)(2,1)}, u32[]{:S(2)}, u32[]{:S(2)}) async-start(bf16[64,4,1792]{2,1,0:T(4,128)(2,1)} %place_rows.5), calls=%async_computation.2 | async-start | bytes 1835008 | tf_op jit(solution)/shard_map/all_to_all | solution.py:272
  86.5 31.9 %all-to-all-start.4 = ((bf16[64,4,1792]{2,1,0:T(4,128)(2,1)}), bf16[64,4,1792]{2,1,0:T(4,128)(2,1)}, u32[]{:S(2)}, u32[]{:S(2)}) async-start(bf16[64,4,1792]{2,1,0:T(4,128)(2,1)} %place_rows.4.rest_1_), calls=%async_computation.4 | async-start | bytes 1835008 | tf_op jit(solution)/shard_map/all_to_all | solution.py:272
  93.1 57.7 %all-gather.6.cloned.1.call-start = ((), (), s32[]{:S(2)}) async-start(), calls=%async_computation.7 | async-start | bytes 4587520 | tf_op jit(solution)/shard_map/all_gather | solution.py:279
  95.6 103.8 %all-gather.8.cloned.1.call-start = ((), (), s32[]{:S(2)}) async-start(), calls=%async_computation.8 | async-start | bytes 4587520 | tf_op jit(solution)/shard_map/all_gather | solution.py:279
  108.8 12.0 %collective-permute-start.3 = (bf16[256,256]{1,0:T(8,128)(2,1)}, bf16[256,256]{1,0:T(8,128)(2,1)S(1)}, u32[]{:S(2)}, u32[]{:S(2)}) collective-permute-start(bf16[256,256]{1,0:T(8,128)(2,1)} %hidden_units.3.refs_0_.refs_3_), channel_id=1, source_target_pairs={{0,1},{1,2},{2,3},{3,0},{4,5},{5,6},{6,7},{7,4},{8,9},{9,10},{10,1... | collective-permute-start | bytes 393224 | tf_op jit(solution)/shard_map/ppermute | solution.py:235
  109.8 11.1 %collective-permute-start.4 = (bf16[256,256]{1,0:T(8,128)(2,1)}, bf16[256,256]{1,0:T(8,128)(2,1)S(1)}, u32[]{:S(2)}, u32[]{:S(2)}) collective-permute-start(bf16[256,256]{1,0:T(8,128)(2,1)} %hidden_units.3.refs_0_.refs_3_), channel_id=1, source_target_pairs={{0,3},{1,0},{2,1},{3,2},{4,7},{5,4},{6,5},{7,6},{8,11},{9,8},{10,9... | collective-permute-start | bytes 393224 | tf_op jit(solution)/shard_map/ppermute | solution.py:235
  111.6 9.3 %collective-permute-start.5 = (bf16[256,256]{1,0:T(8,128)(2,1)}, bf16[256,256]{1,0:T(8,128)(2,1)S(1)}, u32[]{:S(2)}, u32[]{:S(2)}) collective-permute-start(bf16[256,256]{1,0:T(8,128)(2,1)} %hidden_units.3.refs_0_.refs_3_), channel_id=1, source_target_pairs={{0,2},{1,3},{2,0},{3,1},{4,6},{5,7},{6,4},{7,5},{8,10},{9,11},{10,... | collective-permute-start | bytes 393224 | tf_op jit(solution)/shard_map/ppermute | solution.py:235
  127.6 44.6 %all-to-all-start.1 = ((bf16[64,4,1792]{2,1,0:T(4,128)(2,1)}), bf16[64,4,1792]{2,1,0:T(4,128)(2,1)}, u32[]{:S(2)}, u32[]{:S(2)}) async-start(bf16[64,4,1792]{2,1,0:T(4,128)(2,1)} %down.3), calls=%async_computation.1 | async-start | bytes 1835008 | tf_op jit(solution)/shard_map/all_to_all | solution.py:286
  157.1 5.9 %collective-permute-start.6 = (bf16[256,256]{1,0:T(8,128)(2,1)}, bf16[256,256]{1,0:T(8,128)(2,1)S(1)}, u32[]{:S(2)}, u32[]{:S(2)}) collective-permute-start(bf16[256,256]{1,0:T(8,128)(2,1)} %hidden_units.4.refs_0_.refs_3_), channel_id=1, source_target_pairs={{0,1},{1,2},{2,3},{3,0},{4,5},{5,6},{6,7},{7,4},{8,9},{9,10},{10,1... | collective-permute-start | bytes 393224 | tf_op jit(solution)/shard_map/ppermute | solution.py:235
  157.6 5.9 %collective-permute-start.7 = (bf16[256,256]{1,0:T(8,128)(2,1)}, bf16[256,256]{1,0:T(8,128)(2,1)S(1)}, u32[]{:S(2)}, u32[]{:S(2)}) collective-permute-start(bf16[256,256]{1,0:T(8,128)(2,1)} %hidden_units.4.refs_0_.refs_3_), channel_id=1, source_target_pairs={{0,3},{1,0},{2,1},{3,2},{4,7},{5,4},{6,5},{7,6},{8,11},{9,8},{10,9... | collective-permute-start | bytes 393224 | tf_op jit(solution)/shard_map/ppermute | solution.py:235
  159.8 5.5 %collective-permute-start.8 = (bf16[256,256]{1,0:T(8,128)(2,1)}, bf16[256,256]{1,0:T(8,128)(2,1)S(1)}, u32[]{:S(2)}, u32[]{:S(2)}) collective-permute-start(bf16[256,256]{1,0:T(8,128)(2,1)} %hidden_units.4.refs_0_.refs_3_), channel_id=1, source_target_pairs={{0,2},{1,3},{2,0},{3,1},{4,6},{5,7},{6,4},{7,5},{8,10},{9,11},{10,... | collective-permute-start | bytes 393224 | tf_op jit(solution)/shard_map/ppermute | solution.py:235
  172.2 50.0 %all-to-all-start.3 = ((bf16[64,4,1792]{2,1,0:T(4,128)(2,1)}), bf16[64,4,1792]{2,1,0:T(4,128)(2,1)S(1)}, u32[]{:S(2)}, u32[]{:S(2)}) async-start(bf16[64,4,1792]{2,1,0:T(4,128)(2,1)} %down.4), calls=%async_computation.3 | async-start | bytes 1835008 | tf_op jit(solution)/shard_map/all_to_all | solution.py:286
  205.7 28.5 %copy-start.4 = (s32[64,64]{0,1:T(8,128)S(1)}, s32[64,64]{0,1:T(8,128)}, u32[]{:S(2)}) copy-start(s32[64,64]{0,1:T(8,128)} %copy-done.3) | copy-start | bytes 49156
  205.7 28.5 %copy-start.18 = (s32[4]{0:T(128)S(1)}, s32[4]{0:T(128)}, u32[]{:S(2)}) copy-start(s32[4]{0:T(128)} %copy-done.17) | copy-start | bytes 52
  205.7 28.5 %copy-start.20 = (s32[4]{0:T(128)S(1)}, s32[4]{0:T(128)}, u32[]{:S(2)}) copy-start(s32[4]{0:T(128)} %copy-done.19) | copy-start | bytes 52
  205.7 4.7 %collective-permute-start.10 = (bf16[256,256]{1,0:T(8,128)(2,1)}, bf16[256,256]{1,0:T(8,128)(2,1)S(1)}, u32[]{:S(2)}, u32[]{:S(2)}) collective-permute-start(bf16[256,256]{1,0:T(8,128)(2,1)} %hidden_units.5.refs_0_), channel_id=1, source_target_pairs={{0,3},{1,0},{2,1},{3,2},{4,7},{5,4},{6,5},{7,6},{8,11},{9,8},{10,9... | collective-permute-start | bytes 393224 | tf_op jit(solution)/shard_map/ppermute | solution.py:235
  206.3 5.5 %collective-permute-start.11 = (bf16[256,256]{1,0:T(8,128)(2,1)}, bf16[256,256]{1,0:T(8,128)(2,1)S(1)}, u32[]{:S(2)}, u32[]{:S(2)}) collective-permute-start(bf16[256,256]{1,0:T(8,128)(2,1)} %hidden_units.5.refs_0_), channel_id=1, source_target_pairs={{0,2},{1,3},{2,0},{3,1},{4,6},{5,7},{6,4},{7,5},{8,10},{9,11},{10,... | collective-permute-start | bytes 393224 | tf_op jit(solution)/shard_map/ppermute | solution.py:235
  208.1 7.5 %collective-permute-start.9 = (bf16[256,256]{1,0:T(8,128)(2,1)}, bf16[256,256]{1,0:T(8,128)(2,1)S(1)}, u32[]{:S(2)}, u32[]{:S(2)}) collective-permute-start(bf16[256,256]{1,0:T(8,128)(2,1)} %hidden_units.5.refs_0_), channel_id=1, source_target_pairs={{0,1},{1,2},{2,3},{3,0},{4,5},{5,6},{6,7},{7,4},{8,9},{9,10},{10,1... | collective-permute-start | bytes 393224 | tf_op jit(solution)/shard_map/ppermute | solution.py:235
  222.3 36.8 %all-to-all-start.5 = ((bf16[64,4,1792]{2,1,0:T(4,128)(2,1)}), bf16[64,4,1792]{2,1,0:T(4,128)(2,1)S(1)}, u32[]{:S(2)}, u32[]{:S(2)}) async-start(bf16[64,4,1792]{2,1,0:T(4,128)(2,1)} %down.5), calls=%async_computation.5 | async-start | bytes 1835008 | tf_op jit(solution)/shard_map/all_to_all | solution.py:286
  (18 other events, 168.8 us)
Sparse Core Ops, SparseCore 0:
  52.5 50.0 all-gather.3
  104.4 46.3 all-gather.5
  152.6 46.7 all-gather.7
